TPU v7x, 128 devices: a whole 4x4x4 slice. The times are simulated.
128 devices in a mesh: row: 4 (over x), col: 32 (over y, z, core).
Axes of the slice: x: 4, y: 4, z: 4, core: 2. Of those that a mesh axis runs over, the one named last changes fastest.
Arguments:
- features: bfloat16 [32768, 128], P(('row', 'col')), may hold values from -6 to 6
- weight: bfloat16 [128, 256], replicated, may hold values from -0.5 to 0.5
- bias_vector: float32 [256], replicated, may hold values from -3 to 3
- adjacency: bfloat16 [4, 32, 128, 128, 128], P('row', 'col'), may hold values from -0.078125 to 0.078125
- tile_rows: int32 [4, 32, 128], P('row', 'col'), may hold values from 0 to 63, as said below
- tile_cols: int32 [4, 32, 128], P('row', 'col'), may hold values from 0 to 7
- tile_count: int32 [4, 32], P('row', 'col'), may hold values from 32 to 128, as said below
- cotangent: bfloat16 [32768, 256], P(('row', 'col')), may hold values from -6 to 6
Outputs:
- activations: bfloat16 [32768, 256], P(('row', 'col'))
- grad_features: bfloat16 [32768, 128], P(('row', 'col'))
- grad_weight: float32 [128, 256], replicated
- grad_bias: float32 [256], replicated
Inputs may be any that keep to these rules, and one draw needn't show every extreme that they name: Within one grid cell no two slots name the same pair of tile_rows and tile_cols. On each grid cell the live tiles are the first tile_count slots; at least one cell has all 128 slots live.
All inputs are finite; a program needn't handle non-finite values.
Results may differ from a plain program's by a relative error of at most 0.0075.
Values may be sent and summed in bfloat16 or wider, within the bound.
No kernel may reach another device: no remote copies, remote signals or barrier semaphores. Data moves between devices by JAX's collectives and lax.ppermute only.
A program may use at most 128 MiB of HBM per device.

v0:
```python
import jax
import jax.numpy as jnp
from jax import lax
from jax.sharding import PartitionSpec as P


def build_dense(adjacency, index_out, index_in, live_count, out_count, in_count):
    slot_total = adjacency.shape[0]
    block_size = adjacency.shape[1]
    live_mask = jnp.arange(slot_total, dtype=jnp.int32) < live_count
    tiles = jnp.where(live_mask[:, None, None], adjacency, jnp.zeros_like(adjacency))
    dense = jnp.zeros((out_count, in_count, block_size, block_size), jnp.bfloat16)
    return dense.at[index_out, index_in].add(tiles)


def on_device(
    features, weight, bias_vector, adjacency, tile_rows, tile_cols, tile_count, cotangent
):
    block_size = adjacency.shape[-1]
    hidden = weight.shape[1]
    own_nodes = features.shape[0]
    blocks_own = own_nodes // block_size
    row_blocks = lax.axis_size("col") * blocks_own
    col_blocks = lax.axis_size("row") * blocks_own
    dense = build_dense(
        adjacency[0, 0], tile_rows[0, 0], tile_cols[0, 0], tile_count[0, 0], row_blocks, col_blocks
    )
    projected = jnp.dot(features, weight, preferred_element_type=jnp.float32).astype(jnp.bfloat16)
    column_feats = lax.all_gather(projected, "row", axis=0, tiled=True)
    column_feats = column_feats.reshape(col_blocks, block_size, hidden)
    partial_value = jnp.einsum(
        "ijab,jbh->iah", dense, column_feats, preferred_element_type=jnp.float32
    )
    partial_value = partial_value.reshape(row_blocks * block_size, hidden)
    summed_own = lax.psum_scatter(partial_value, "col", scatter_dimension=0, tiled=True)
    pre = summed_own + bias_vector
    sigmoid_value = jax.nn.sigmoid(pre)
    activations = (pre * sigmoid_value).astype(jnp.bfloat16)
    slope = sigmoid_value * (1.0 + pre * (1.0 - sigmoid_value))
    grad_own = (cotangent.astype(jnp.float32) * slope).astype(jnp.bfloat16)
    row_grad = lax.all_gather(grad_own, "col", axis=0, tiled=True)
    row_grad = row_grad.reshape(row_blocks, block_size, hidden)
    column_part = jnp.einsum("ijab,iah->jbh", dense, row_grad, preferred_element_type=jnp.float32)
    column_part = column_part.reshape(col_blocks * block_size, hidden)
    proj_grad = lax.psum_scatter(column_part, "row", scatter_dimension=0, tiled=True).astype(
        jnp.bfloat16
    )
    weight_term = lax.dot_general(
        features, proj_grad, (((0,), (0,)), ((), ())), preferred_element_type=jnp.float32
    )
    bias_term = jnp.sum(grad_own.astype(jnp.float32), axis=0)
    grad_weight, grad_bias = lax.psum((weight_term, bias_term), ("row", "col"))
    grad_features = lax.dot_general(
        proj_grad, weight, (((1,), (1,)), ((), ())), preferred_element_type=jnp.float32
    ).astype(jnp.bfloat16)
    return (activations, grad_features, grad_weight, grad_bias)


def solution(mesh):
    placed = (
        P(("row", "col"), None),
        P(),
        P(),
        P("row", "col", None, None, None),
        P("row", "col", None),
        P("row", "col", None),
        P("row", "col"),
        P(("row", "col"), None),
    )
    return jax.shard_map(
        on_device,
        mesh=mesh,
        in_specs=placed,
        out_specs=(P(("row", "col"), None), P(("row", "col"), None), P(), P()),
        check_vma=False,
    )
```

profile of v0, /device:TPU:1, one launch (start us, length us, event | category | flops | bytes accessed | tf_op | source)
XLA Modules:
  0.0 451.8 jit_solution(2769405229844759662)
XLA Ops:
  7.2 0.0 reduce-scatter.3.cloned.1.call-start
  7.9 0.1 copy-done
  8.0 1.0 convolution_convert_fusion
  9.0 12.3 %all_gather.6 = bf16[1024,256]{1,0:T(8,128)(2,1)S(1)} all-gather(bf16[256,256]{1,0:T(8,128)(2,1)S(1)} %convolution_convert_fusion), channel_id=1, replica_groups=mesh['row'=4,'col'=32] {'row'}, dimensions={0}, use_global_device_ids=true | all-gather | bytes 655360 | tf_op jit(solution)/shard_map/all_gather | solution.py:29
  21.4 0.7 fusion.8
  22.0 4.5 bitcast_select_fusion
  26.5 6.3 %broadcast_in_dim.18 = bf16[64,8,128,128]{3,2,1,0:T(8,128)(2,1)} broadcast(bf16[]{:T(256)} %constant.6.clone.1), dimensions={} | broadcast | bytes 16777218 | tf_op jit(solution)/shard_map/broadcast_in_dim | solution.py:12
  32.8 26.8 %scatter_fusion = bf16[64,8,128,128]{3,2,1,0:T(8,128)(2,1)} fusion(bf16[64,8,128,128]{3,2,1,0:T(8,128)(2,1)} %broadcast_in_dim.18, s32[128]{0:T(128)S(1)} %fusion.8, bf16[128,128,128]{2,1,0:T(8,128)(2,1)} %bitcast_select_fusion), kind=kCustom, calls=%fused_computation | custom fusion | flops 2097152 | bytes 12583936 | tf_op jit(solution)/shard_map/scatter-add | solution.py:13
  59.6 16.8 %copy.15 = bf16[64,128,128,8]{2,3,1,0:T(8,128)(2,1)S(1)} copy(bf16[64,128,128,8]{2,1,3,0:T(8,128)(2,1)} %bitcast.34) | data formatting | bytes 33554432 | tf_op jit(solution)/shard_map/ijab,jbh->iah/dot_general | solution.py:31
  76.4 7.2 %fusion.2 = f32[8192,256]{1,0:T(8,128)} fusion(bf16[8,128,256]{2,1,0:T(8,128)(2,1)S(1)} %bitcast.38, bf16[8192,128,8]{1,2,0:T(8,128)(2,1)S(1)} %bitcast.37), kind=kOutput, calls=%fused_computation.3 | convolution fusion | flops 4294967296 | bytes 25690112 | tf_op jit(solution)/shard_map/ijab,jbh->iah/dot_general | solution.py:31
  83.6 0.0 all-gather.2.cloned.1.call-start
  83.7 95.3 %reduce-scatter.3.cloned.1.call-done = f32[256,256]{1,0:T(8,128)} async-done(((f32[8192,256]{1,0:T(8,128)}), f32[256,256]{1,0:T(8,128)}) %reduce-scatter.3.cloned.1.call-update) | async-done | bytes 262160 | tf_op jit(solution)/shard_map/reduce_scatter | solution.py:35
  178.9 1.8 convert_reduce_fusion
  180.7 0.0 all-gather.2.cloned.1.call-update
  180.8 0.0 reduce-scatter.5.cloned.1.call-start
  180.8 22.4 %copy.20 = bf16[8,128,128,64]{2,1,0,3:T(8,128)(2,1)} copy(bf16[8,128,128,64]{1,2,0,3:T(8,128)(2,1)} %bitcast.35) | data formatting | bytes 33554432 | tf_op jit(solution)/shard_map/ijab,iah->jbh/dot_general | solution.py:43
  203.2 26.6 %all-gather.2.cloned.1.call-done = bf16[8192,256]{1,0:T(8,128)(2,1)} async-done(((bf16[256,256]{1,0:T(8,128)(2,1)}), bf16[8192,256]{1,0:T(8,128)(2,1)}) %all-gather.2.cloned.1.call-update) | async-done | bytes 4194320 | tf_op jit(solution)/shard_map/all_gather | solution.py:41
  229.8 10.1 %convolution_bitcast_fusion = f32[1024,256]{1,0:T(8,128)} fusion(bf16[1024,128,64]{1,0,2:T(8,128)(2,1)} %bitcast.36, bf16[64,128,256]{2,1,0:T(8,128)(2,1)} %bitcast.39), kind=kOutput, calls=%fused_computation.5 | convolution fusion | flops 4294967296 | bytes 22020096 | tf_op jit(solution)/shard_map/ijab,iah->jbh/dot_general | solution.py:43
  240.0 0.0 all-reduce.2.cloned.1.call-start
  240.0 64.4 %psum.15 = f32[256]{0:T(256)} all-reduce(f32[256]{0:T(256)S(1)} %get-tuple-element.16), channel_id=1, replica_groups=mesh['row'=4,'col'=32] {'row','col'}, use_global_device_ids=true, to_apply=%region_5.6 | all-reduce | flops 256 | bytes 2048 | tf_op jit(solution)/shard_map/psum | solution.py:52
  304.4 1.8 convolution_bitcast_fusion.1
  306.3 1.8 convolution_convert_fusion.1
  308.0 135.5 %all-reduce.2.cloned.1.call-done = f32[128,256]{0,1:T(8,128)} async-done(((f32[128,256]{0,1:T(8,128)}), f32[128,256]{0,1:T(8,128)}) %all-reduce.2.cloned.1.call-update) | async-done | bytes 131088 | tf_op jit(solution)/shard_map/psum | solution.py:52
  443.6 1.7 copy.19
  (12 shorter events, 0.1 us)
Async XLA Ops:
  7.2 0.8 copy-start
  7.2 171.8 %reduce-scatter.3.cloned.1.call-start = ((), (), s32[]{:S(2)}) async-start(), calls=%async_computation.2 | async-start | bytes 8650752 | tf_op jit(solution)/shard_map/reduce_scatter | solution.py:35
  83.6 95.3 %copy-start.2 = (bf16[256,256]{1,0:T(8,128)(2,1)S(1)}, bf16[256,256]{1,0:T(8,128)(2,1)}, u32[]{:S(2)}) copy-start(bf16[256,256]{1,0:T(8,128)(2,1)} %param.15) | copy-start | bytes 393220
  83.6 95.3 %copy-start.3 = (f32[256]{0:T(256)S(1)}, f32[256]{0:T(256)}, u32[]{:S(2)}) copy-start(f32[256]{0:T(256)} %param.10) | copy-start | bytes 3076
  83.6 146.2 %all-gather.2.cloned.1.call-start = ((), (), s32[]{:S(2)}) async-start(), calls=%async_computation.3 | async-start | bytes 4325376 | tf_op jit(solution)/shard_map/all_gather | solution.py:41
  180.8 123.6 %reduce-scatter.5.cloned.1.call-start = ((), (), s32[]{:S(2)}) async-start(), calls=%async_computation.4 | async-start | bytes 1310720 | tf_op jit(solution)/shard_map/reduce_scatter | solution.py:45
  229.8 76.5 %copy-start.1 = (bf16[128,256]{1,0:T(8,128)(2,1)S(1)}, bf16[128,256]{1,0:T(8,128)(2,1)}, u32[]{:S(2)}) copy-start(bf16[128,256]{1,0:T(8,128)(2,1)} %param.9) | copy-start | bytes 196612
  240.0 203.6 %all-reduce.2.cloned.1.call-start = ((), (), s32[]{:S(2)}) async-start(), calls=%async_computation.5 | async-start | bytes 262144 | tf_op jit(solution)/shard_map/psum | solution.py:52
Sparse Core Ops, SparseCore 0:
  83.7 95.1 reduce-scatter.2
  182.0 47.7 all-gather.1
  240.1 21.0 reduce-scatter.4
  306.4 137.1 all-reduce.1
where the time goes:
time: 453 us; the launch traced here: 452 us
  waiting for transfers between devices  257 us (57%)
  blocking collectives  76.7 us (17%)
  local copies, waits for them, and re-layouts  47.3 us (10%)
  other arithmetic  33.7 us (7%)
  matrix products  21.9 us (5%)
  between operations  14.5 us (3%)
    psum x1, waiting for transfers between devices, on_device(): grad_weight, grad_bias = lax.psum((weight_term, bias_term), ('row', 'col'))  136 us
    reduce_scatter x1, waiting for transfers between devices, on_device(): lax.psum_scatter(partial_value, 'col', scatter_dimension=0, tiled=True)  95.3 us
    psum x1, blocking collectives, on_device(): grad_weight, grad_bias = lax.psum((weight_term, bias_term), ('row', 'col'))  64.4 us
    scatter-add x1, other arithmetic, build_dense(): return dense.at[index_out, index_in].add(tiles)  26.8 us
    all_gather x1, waiting for transfers between devices, on_device(): row_grad = lax.all_gather(grad_own, 'col', axis=0, tiled=True)  26.6 us
    dot_general x1, local copies, waits for them, and re-layouts, on_device(): jnp.einsum('ijab,iah->jbh', dense, row_grad, preferred_element_type=jnp.f...  22.4 us
    dot_general x1, local copies, waits for them, and re-layouts, on_device(): jnp.einsum('ijab,jbh->iah', dense, column_feats, preferred_element_type=j...  16.8 us
    all_gather x1, blocking collectives, on_device(): column_feats = lax.all_gather(projected, 'row', axis=0, tiled=True)  12.3 us
  transfers between devices with their start and end apart: 4, of which 3 were waited for; matrix products, arithmetic and copies ran while one was open for 5% of the time, Pallas kernels for 0%

commit v1 on v0

v1 whole, which is shorter than its diff:
```python
import functools

import jax
import jax.numpy as jnp
from jax import lax
from jax.experimental import pallas as pl
from jax.experimental.pallas import tpu as pltpu
from jax.sharding import PartitionSpec as P

F32 = jnp.float32
BF16 = jnp.bfloat16
B = 128
VMEM = pl.BlockSpec(memory_space=pltpu.VMEM)
SMEM = pl.BlockSpec(memory_space=pltpu.SMEM)
TAIL = 272
UNROLL = 8


def at(y, z, core):
    return (y * 4 + z) * 2 + core


def col_shift(first, d):
    pairs = []
    for y in range(4):
        for z in range(4):
            for core in range(2):
                along_z = (core == 0) == first
                to = at(y, (z + d) % 4, core) if along_z else at((y + d) % 4, z, core)
                pairs.append((at(y, z, core), to))
    return pairs


def core_swap():
    return [(c, c ^ 1) for c in range(32)]


def row_shift(d):
    return [(r, (r + d) % 4) for r in range(4)]


def call(kernel, outs, n_smem, n_vmem, scratch=(), flops=0, nbytes=0):
    return pl.pallas_call(
        kernel,
        out_shape=outs,
        in_specs=[SMEM] * n_smem + [VMEM] * n_vmem,
        out_specs=jax.tree.map(lambda _: VMEM, outs),
        scratch_shapes=list(scratch),
        compiler_params=pltpu.CompilerParams(vmem_limit_bytes=24 * 2**20),
        cost_estimate=pl.CostEstimate(flops=flops, bytes_accessed=nbytes, transcendentals=0),
    )


def sds(rows, cols=B, dtype=BF16):
    return jax.ShapeDtypeStruct((rows, cols), dtype)


def forward_tiles(pos, src, x0, x1, x2, x3, adj, own, other, acc, xs):
    for k, x in enumerate((x0, x1, x2, x3)):
        xs[2 * k] = x[0:B]
        xs[2 * k + 1] = x[B : 2 * B]

    def clear(i, _):
        acc[i] = jnp.zeros((B, B), F32)
        return 0

    lax.fori_loop(0, 64, clear, 0)

    def body(g, _):
        parts = []
        for u in range(UNROLL):
            s = g * UNROLL + u
            parts.append(jnp.dot(adj[s], xs[src[s]], preferred_element_type=F32))
        for u in range(UNROLL):
            p = pos[g * UNROLL + u]
            acc[p] += parts[u]
        return 0

    lax.fori_loop(0, 128 // UNROLL, body, 0)

    def store(i, _):
        rows = pl.ds(pl.multiple_of(i * B, B), B)
        own[rows] = acc[i]
        other[rows] = acc[32 + i].astype(BF16)
        return 0

    lax.fori_loop(0, 32, store, 0)


def core_sum(own, got, m0, m1, m2, m3):
    m0[...] = own[0:1024] + got[0:1024].astype(F32)
    for k, m in ((1, m1), (2, m2), (3, m3)):
        rows = pl.ds(k * 1024, 1024)
        m[...] = (own[rows] + got[rows].astype(F32)).astype(BF16)


def first_sum(m0, r1, r2, r3, s0, s1, s2, s3):
    for k, s in enumerate((s0, s1, s2, s3)):
        rows = pl.ds(k * 256, 256)
        total = m0[rows] + (r1[rows].astype(F32) + r2[rows].astype(F32) + r3[rows].astype(F32))
        s[...] = total.astype(s.dtype)


def put_tail(msg, base, wg, bg):
    msg[pl.ds(base, 256)] = wg.astype(msg.dtype)
    if msg.dtype == F32:
        msg[pl.ds(base + 256, 16)] = jnp.concatenate([bg, jnp.zeros((14, B), F32)])
    else:
        high = bg.astype(BF16).astype(F32)
        low = bg - high
        block = jnp.concatenate([high, low, jnp.zeros((12, B), F32)])
        msg[pl.ds(base + 256, 16)] = block.astype(BF16)


def get_tail(msg, base):
    wg = msg[pl.ds(base, 256)].astype(F32)
    block = msg[pl.ds(base + 256, 16)].astype(F32)
    return wg, block[0:2] + block[2:4]


def local(s0, r1, r2, r3, weight, bias, cot, act, msg):
    y = s0[...] + (r1[...].astype(F32) + r2[...].astype(F32) + r3[...].astype(F32))
    y_high = y.astype(BF16)
    y_low = (y - y_high.astype(F32)).astype(BF16)
    w = weight[...]
    summed = jnp.dot(y_high, w, preferred_element_type=F32) + jnp.dot(
        y_low, w, preferred_element_type=F32
    )
    pre = summed + bias[...]
    sig = jax.nn.sigmoid(pre)
    act[...] = (pre * sig).astype(BF16)
    slope = sig * (1.0 + pre * (1.0 - sig))
    grad = (cot[...].astype(F32) * slope).astype(BF16)
    g = lax.dot_general(w, grad, (((1,), (1,)), ((), ())), preferred_element_type=F32)
    g = g.astype(BF16)
    msg[0:B] = g[:, 0:B]
    msg[B : 2 * B] = g[:, B : 2 * B]
    over_nodes = (((0,), (0,)), ((), ()))
    wg = lax.dot_general(y_high, grad, over_nodes, preferred_element_type=F32)
    wg += lax.dot_general(y_low, grad, over_nodes, preferred_element_type=F32)
    bg = jnp.sum(grad.astype(F32), axis=0, keepdims=True)
    put_tail(
        msg,
        256,
        jnp.concatenate([wg[:, 0:B], wg[:, B : 2 * B]]),
        jnp.concatenate([bg[:, 0:B], bg[:, B : 2 * B]]),
    )


def second_join(m0, r1, r2, r3, msg):
    wg, bg = get_tail(m0, 256)
    for r in (r1, r2, r3):
        wg_r, bg_r = get_tail(r, 256)
        wg += wg_r
        bg += bg_r
    for k, r in enumerate((m0, r3, r2, r1)):
        msg[pl.ds(k * 256, 256)] = r[0:256]
    put_tail(msg, 1024, wg, bg)


def backward_tiles(pos, src, *refs):
    pieces, (adj, m0, m1, m2, m3, acc, gs) = refs[:8], refs[8:]

    def load(i, _):
        rows = pl.ds(pl.multiple_of(i * B, B), B)
        for k, piece in enumerate(pieces):
            gs[k * 8 + i] = piece[rows]
        return 0

    lax.fori_loop(0, 8, load, 0)
    gs[64] = jnp.zeros((B, B), BF16)
    acc[...] = jnp.zeros((8, B, B), F32)

    def body(g, _):
        parts = []
        for u in range(UNROLL):
            s = g * UNROLL + u
            parts.append(jnp.dot(gs[pos[s]], adj[s], preferred_element_type=F32))
        for u in range(UNROLL):
            q = src[g * UNROLL + u]
            acc[q] += parts[u]
        return 0

    lax.fori_loop(0, 128 // UNROLL, body, 0)
    wg, bg = get_tail(pieces[0], 1024)
    for piece in pieces[1:]:
        wg_r, bg_r = get_tail(piece, 1024)
        wg += wg_r
        bg += bg_r
    for k, m in enumerate((m0, m1, m2, m3)):
        m[0:B] = acc[2 * k].astype(m.dtype)
        m[B : 2 * B] = acc[2 * k + 1].astype(m.dtype)
        put_tail(m, 256, wg, bg)


def last_sum(m0, r1, r2, r3, feat, wgrad, bgrad):
    for k in range(2):
        rows = pl.ds(k * B, B)
        total = m0[rows] + (r1[rows].astype(F32) + r2[rows].astype(F32) + r3[rows].astype(F32))
        feat[rows] = total.T.astype(BF16)
    wg, block = m0[pl.ds(256, 256)], m0[pl.ds(512, 16)]
    bg = block[0:2]
    for r in (r1, r2, r3):
        wg_r, bg_r = get_tail(r, 256)
        wg += wg_r
        bg += bg_r
    wgrad[:, 0:B] = wg[0:B]
    wgrad[:, B : 2 * B] = wg[B : 2 * B]
    bgrad[:, 0:B] = bg[0:1]
    bgrad[:, B : 2 * B] = bg[1:2]


def on_device(
    features, weight, bias_vector, adjacency, tile_rows, tile_cols, tile_count, cotangent
):
    r = lax.axis_index("row")
    c = lax.axis_index("col")
    core, z, y = c % 2, (c // 2) % 4, c // 8

    owner, sub = tile_rows[0, 0] // 2, tile_rows[0, 0] % 2
    core_to, z_to, y_to = owner % 2, (owner // 2) % 4, owner // 8
    dz, dy = (z_to - z) % 4, (y_to - y) % 4
    first = jnp.where(core_to == 0, dz, dy)
    second = jnp.where(core_to == 0, dy, dz)
    half = (core_to != core).astype(jnp.int32)
    pos = ((half * 4 + first) * 4 + second) * 2 + sub
    live = jnp.arange(pos.shape[0], dtype=jnp.int32) < tile_count[0, 0]
    pos = jnp.where(live, pos, 64)
    src = ((tile_cols[0, 0] // 2 - r) % 4) * 2 + tile_cols[0, 0] % 2
    adj = adjacency[0, 0]

    x1, x2, x3 = (lax.ppermute(features, "row", row_shift(d)) for d in (1, 2, 3))
    own, other = call(
        forward_tiles,
        (sds(4096, dtype=F32), sds(4096)),
        2,
        5,
        [pltpu.VMEM((65, B, B), F32), pltpu.VMEM((8, B, B), BF16)],
        flops=2 * 128 * B**3,
        nbytes=8 * 2**20,
    )(pos, src, features, x3, x2, x1, adj)
    got = lax.ppermute(other, "col", core_swap())
    m0, *ms = call(core_sum, (sds(1024, dtype=F32), sds(1024), sds(1024), sds(1024)), 0, 2)(own, got)
    rs = [lax.ppermute(m, "col", col_shift(True, d + 1)) for d, m in enumerate(ms)]
    s0, *ss = call(first_sum, (sds(256, dtype=F32), sds(256), sds(256), sds(256)), 0, 4)(m0, *rs)
    rs = [lax.ppermute(s, "col", col_shift(False, d + 1)) for d, s in enumerate(ss)]
    act, msg = call(local, (sds(256, 256), sds(256 + TAIL)), 0, 7)(
        s0, *rs, weight, bias_vector.reshape(1, 256), cotangent
    )
    rs = [lax.ppermute(msg, "col", col_shift(False, d)) for d in (1, 2, 3)]
    msg = call(second_join, sds(1024 + TAIL), 0, 4)(msg, *rs)
    rs = [lax.ppermute(msg, "col", col_shift(True, d)) for d in (1, 2, 3)]
    mine = (msg, rs[2], rs[1], rs[0])
    theirs = [lax.ppermute(m, "col", core_swap()) for m in mine]
    x_out = (sds(256 + TAIL, dtype=F32),) + (sds(256 + TAIL),) * 3
    m0, *ms = call(
        backward_tiles,
        x_out,
        2,
        9,
        [pltpu.VMEM((8, B, B), F32), pltpu.VMEM((65, B, B), BF16)],
        flops=2 * 128 * B**3,
        nbytes=8 * 2**20,
    )(pos, src, *mine, *theirs, adj)
    rs = [lax.ppermute(m, "row", row_shift(d + 1)) for d, m in enumerate(ms)]
    feat, wgrad, bgrad = call(
        last_sum, (sds(256, 128), sds(128, 256, F32), sds(1, 256, F32)), 0, 4
    )(m0, *rs)
    return (act, feat, wgrad, bgrad.reshape(256))


def solution(mesh):
    placed = (
        P(("row", "col"), None),
        P(),
        P(),
        P("row", "col", None, None, None),
        P("row", "col", None),
        P("row", "col", None),
        P("row", "col"),
        P(("row", "col"), None),
    )
    return jax.shard_map(
        on_device,
        mesh=mesh,
        in_specs=placed,
        out_specs=(P(("row", "col"), None), P(("row", "col"), None), P(), P()),
        check_vma=False,
    )
```

time: 453 us -> 86.3 us (0.19)
  waiting for transfers between devices: 257 us -> 27.4 us
  blocking collectives: 76.7 us -> 0 us
  local copies, waits for them, and re-layouts: 47.3 us -> 3.04 us
  starting transfers between devices: 0.16 us -> 41.5 us
  other arithmetic: 33.7 us -> 0.71 us
  matrix products: 21.9 us -> 0 us
  between operations: 14.5 us -> 1.37 us
  Pallas kernels: 0 us -> 11.9 us
    psum x1 -> x0, waiting for transfers between devices: 136 us -> none  [on_device(): grad_weight, grad_bias = lax.psum((weight_term, bias_term), ('row', 'col'))]
    reduce_scatter x2 -> x0, waiting for transfers between devices: 95.3 us -> none  [the longest x1 95.3 us: on_device(): lax.psum_scatter(partial_value, 'col', scatter_dimension=0, tiled=True)]
    psum x1 -> x0, blocking collectives: 64.4 us -> none  [on_device(): grad_weight, grad_bias = lax.psum((weight_term, bias_term), ('row', 'col'))]
    ppermute x0 -> x23, starting transfers between devices: none -> 41.5 us  [the longest x4 13.4 us: on_device(): theirs = [lax.ppermute(m, 'col', core_swap()) for m in mine]]
    dot_general x2 -> x0, local copies, waits for them, and re-layouts: 39.2 us -> none  [the longest x1 22.4 us: on_device(): jnp.einsum('ijab,iah->jbh', dense, row_grad, preferred_element_type=jnp.f...]
    ppermute x0 -> x23, waiting for transfers between devices: none -> 27.4 us  [the longest x3 6.55 us: on_device(): rs = [lax.ppermute(m, 'row', row_shift(d + 1)) for d, m in enumerate(ms)]]
    scatter-add x1 -> x0, other arithmetic: 26.8 us -> none  [build_dense(): return dense.at[index_out, index_in].add(tiles)]
    all_gather x1 -> x0, waiting for transfers between devices: 26.6 us -> none  [on_device(): row_grad = lax.all_gather(grad_own, 'col', axis=0, tiled=True)]
  transfers between devices with their start and end apart: 4 -> 23, of which waited for: 3 -> 14; matrix products, arithmetic and copies ran while one was open for 5% -> 1% of each run, Pallas kernels for 0% -> 0%
where the time goes in v1:
time: 86.3 us; the launch traced here: 86 us
  starting transfers between devices  41.5 us (48%)
  waiting for transfers between devices  27.4 us (32%)
  Pallas kernels  11.9 us (14%)
  local copies, waits for them, and re-layouts  3.04 us (4%)
  between operations  1.37 us (2%)
    ppermute x4, starting transfers between devices, on_device(): theirs = [lax.ppermute(m, 'col', core_swap()) for m in mine]  13.4 us
    ppermute x3, waiting for transfers between devices, on_device(): rs = [lax.ppermute(m, 'row', row_shift(d + 1)) for d, m in enumerate(ms)]  6.55 us
    ppermute x3, waiting for transfers between devices, on_device(): rs = [lax.ppermute(msg, 'col', col_shift(False, d)) for d in (1, 2, 3)]  6.08 us
    ppermute x3, waiting for transfers between devices, on_device(): lax.ppermute(m, 'col', col_shift(True, d + 1))  5.79 us
    ppermute x3, starting transfers between devices, on_device(): lax.ppermute(s, 'col', col_shift(False, d + 1))  5.45 us
    pallas_call x1, Pallas kernels, on_device(): call(forward_tiles, (sds(4096, dtype=F32), sds(4096)), 2, 5, [pltpu.VMEM(...  5.19 us
    ppermute x3, starting transfers between devices, on_device(): lax.ppermute(features, 'row', row_shift(d))  5.12 us
    ppermute x3, starting transfers between devices, on_device(): lax.ppermute(m, 'col', col_shift(True, d + 1))  5.06 us
  transfers between devices with their start and end apart: 23, of which 14 were waited for; matrix products, arithmetic and copies ran while one was open for 1% of the time, Pallas kernels for 0%

profile of v1, /device:TPU:1, one launch (start us, length us, event | category | flops | bytes accessed | tf_op | source)
XLA Modules:
  0.0 86.0 jit_solution(13496254323946218597)
XLA Ops:
  0.6 3.7 %collective-permute-start.1 = (bf16[256,128]{1,0:T(8,128)(2,1)}, bf16[256,128]{1,0:T(8,128)(2,1)S(1)}, u32[]{:S(2)}, u32[]{:S(2)}) collective-permute-start(bf16[256,128]{1,0:T(8,128)(2,1)} %x0.1), channel_id=1, source_target_pairs={{0,64},{32,96},{64,0},{96,32},{1,65},{33,97},{65,1},{97,33},{2,66}... | collective-permute-start | bytes 196616 | tf_op jit(solution)/shard_map/ppermute | solution.py:232
  8.3 1.4 %collective-permute-done.2.x3 = bf16[256,128]{1,0:T(8,128)(2,1)S(1)} collective-permute-done((bf16[256,128]{1,0:T(8,128)(2,1)}, bf16[256,128]{1,0:T(8,128)(2,1)S(1)}, u32[]{:S(2)}, u32[]{:S(2)}) %collective-permute-start.2) | collective-permute-done | bytes 65568 | tf_op jit(solution)/shard_map/ppermute | solution.py:232
  9.7 2.2 %copy-done = bf16[1,1,128,128,128]{4,3,2,1,0:T(8,128)(2,1)S(1)} copy-done((bf16[1,1,128,128,128]{4,3,2,1,0:T(8,128)(2,1)S(1)}, bf16[1,1,128,128,128]{4,3,2,1,0:T(8,128)(2,1)}, u32[]{:S(2)}) %copy-start) | copy-done | bytes 4194328
  12.7 5.2 %shard_map.111 = (f32[4096,128]{1,0:T(8,128)S(1)}, bf16[4096,128]{1,0:T(8,128)(2,1)S(1)}) custom-call(s32[128]{0:T(128)S(1)} %get-tuple-element.42.pos, s32[128]{0:T(128)S(1)} %get-tuple-element.43.src, bf16[256,128]{1,0:T(8,128)(2,1)S(1)} %copy-done.3, bf16[256,128]{1,0:T(8,128)(2,1)S(1)} %collective-permute-done.x1, ...), custom_call_target="tpu_custom_call" | custom-call | flops 536870912 | bytes 8388608 | tf_op jit(solution)/shard_map/pallas_call | solution.py:233
  17.9 2.5 %collective-permute-start.3 = (bf16[4096,128]{1,0:T(8,128)(2,1)S(1)}, bf16[4096,128]{1,0:T(8,128)(2,1)S(1)}, u32[]{:S(2)}, u32[]{:S(2)}) collective-permute-start(bf16[4096,128]{1,0:T(8,128)(2,1)S(1)} %get-tuple-element.24), channel_id=1, source_target_pairs={{0,1},{1,0},{2,3},{3,2},{4,5},{5,4},{6,7},{7,6},{8,9},{9,8},{10,11... | collective-permute-start | bytes 3145736 | tf_op jit(solution)/shard_map/ppermute | solution.py:242
  20.4 2.3 %collective-permute-done.3.got = bf16[4096,128]{1,0:T(8,128)(2,1)S(1)} collective-permute-done((bf16[4096,128]{1,0:T(8,128)(2,1)S(1)}, bf16[4096,128]{1,0:T(8,128)(2,1)S(1)}, u32[]{:S(2)}, u32[]{:S(2)}) %collective-permute-start.3) | collective-permute-done | bytes 1048608 | tf_op jit(solution)/shard_map/ppermute | solution.py:242
  22.9 1.4 %collective-permute-start.4 = (bf16[1024,128]{1,0:T(8,128)(2,1)S(1)}, bf16[1024,128]{1,0:T(8,128)(2,1)S(1)}, u32[]{:S(2)}, u32[]{:S(2)}) collective-permute-start(bf16[1024,128]{1,0:T(8,128)(2,1)S(1)} %get-tuple-element.26), channel_id=1, source_target_pairs={{0,2},{1,9},{2,4},{3,11},{4,6},{5,13},{6,0},{7,15},{8,10},{9,17},{... | collective-permute-start | bytes 786440 | tf_op jit(solution)/shard_map/ppermute | solution.py:244
  24.2 2.6 %collective-permute-start.5 = (bf16[1024,128]{1,0:T(8,128)(2,1)S(1)}, bf16[1024,128]{1,0:T(8,128)(2,1)S(1)}, u32[]{:S(2)}, u32[]{:S(2)}) collective-permute-start(bf16[1024,128]{1,0:T(8,128)(2,1)S(1)} %get-tuple-element.27), channel_id=1, source_target_pairs={{0,4},{1,17},{2,6},{3,19},{4,0},{5,21},{6,2},{7,23},{8,12},{9,25},... | collective-permute-start | bytes 786440 | tf_op jit(solution)/shard_map/ppermute | solution.py:244
  27.9 1.8 %collective-permute-done.4.r1 = bf16[1024,128]{1,0:T(8,128)(2,1)S(1)} collective-permute-done((bf16[1024,128]{1,0:T(8,128)(2,1)S(1)}, bf16[1024,128]{1,0:T(8,128)(2,1)S(1)}, u32[]{:S(2)}, u32[]{:S(2)}) %collective-permute-start.4) | collective-permute-done | bytes 262176 | tf_op jit(solution)/shard_map/ppermute | solution.py:244
  29.7 4.0 %collective-permute-done.5.r2 = bf16[1024,128]{1,0:T(8,128)(2,1)S(1)} collective-permute-done((bf16[1024,128]{1,0:T(8,128)(2,1)S(1)}, bf16[1024,128]{1,0:T(8,128)(2,1)S(1)}, u32[]{:S(2)}, u32[]{:S(2)}) %collective-permute-start.5) | collective-permute-done | bytes 262176 | tf_op jit(solution)/shard_map/ppermute | solution.py:244
  33.8 1.4 %collective-permute-start.7 = (bf16[256,128]{1,0:T(8,128)(2,1)S(1)}, bf16[256,128]{1,0:T(8,128)(2,1)S(1)}, u32[]{:S(2)}, u32[]{:S(2)}) collective-permute-start(bf16[256,128]{1,0:T(8,128)(2,1)S(1)} %get-tuple-element.30), channel_id=1, source_target_pairs={{0,8},{1,3},{2,10},{3,5},{4,12},{5,7},{6,14},{7,1},{8,16},{9,11},{... | collective-permute-start | bytes 196616 | tf_op jit(solution)/shard_map/ppermute | solution.py:246
  35.2 3.3 %collective-permute-start.8 = (bf16[256,128]{1,0:T(8,128)(2,1)S(1)}, bf16[256,128]{1,0:T(8,128)(2,1)S(1)}, u32[]{:S(2)}, u32[]{:S(2)}) collective-permute-start(bf16[256,128]{1,0:T(8,128)(2,1)S(1)} %get-tuple-element.31), channel_id=1, source_target_pairs={{0,16},{1,5},{2,18},{3,7},{4,20},{5,1},{6,22},{7,3},{8,24},{9,13},... | collective-permute-start | bytes 196616 | tf_op jit(solution)/shard_map/ppermute | solution.py:246
  39.3 1.6 %collective-permute-done.8.r2 = bf16[256,128]{1,0:T(8,128)(2,1)S(1)} collective-permute-done((bf16[256,128]{1,0:T(8,128)(2,1)S(1)}, bf16[256,128]{1,0:T(8,128)(2,1)S(1)}, u32[]{:S(2)}, u32[]{:S(2)}) %collective-permute-start.8) | collective-permute-done | bytes 65568 | tf_op jit(solution)/shard_map/ppermute | solution.py:246
  42.6 1.9 %collective-permute-start.12 = (bf16[528,128]{1,0:T(8,128)(2,1)S(1)}, bf16[528,128]{1,0:T(8,128)(2,1)S(1)}, u32[]{:S(2)}, u32[]{:S(2)}) collective-permute-start(bf16[528,128]{1,0:T(8,128)(2,1)S(1)} %get-tuple-element.34.m0), channel_id=1, source_target_pairs={{0,24},{1,7},{2,26},{3,1},{4,28},{5,3},{6,30},{7,5},{8,0},{9,15},{... | collective-permute-start | bytes 405512 | tf_op jit(solution)/shard_map/ppermute | solution.py:250
  45.3 2.7 %collective-permute-done.12.r3 = bf16[528,128]{1,0:T(8,128)(2,1)S(1)} collective-permute-done((bf16[528,128]{1,0:T(8,128)(2,1)S(1)}, bf16[528,128]{1,0:T(8,128)(2,1)S(1)}, u32[]{:S(2)}, u32[]{:S(2)}) %collective-permute-start.12) | collective-permute-done | bytes 135200 | tf_op jit(solution)/shard_map/ppermute | solution.py:250
  48.0 2.1 %collective-permute-done.11.r2 = bf16[528,128]{1,0:T(8,128)(2,1)S(1)} collective-permute-done((bf16[528,128]{1,0:T(8,128)(2,1)S(1)}, bf16[528,128]{1,0:T(8,128)(2,1)S(1)}, u32[]{:S(2)}, u32[]{:S(2)}) %collective-permute-start.11) | collective-permute-done | bytes 135200 | tf_op jit(solution)/shard_map/ppermute | solution.py:250
  50.1 1.3 %collective-permute-done.10.r1 = bf16[528,128]{1,0:T(8,128)(2,1)S(1)} collective-permute-done((bf16[528,128]{1,0:T(8,128)(2,1)S(1)}, bf16[528,128]{1,0:T(8,128)(2,1)S(1)}, u32[]{:S(2)}, u32[]{:S(2)}) %collective-permute-start.10) | collective-permute-done | bytes 135200 | tf_op jit(solution)/shard_map/ppermute | solution.py:250
  52.7 2.3 %collective-permute-start.14 = (bf16[1296,128]{1,0:T(8,128)(2,1)S(1)}, bf16[1296,128]{1,0:T(8,128)(2,1)S(1)}, u32[]{:S(2)}, u32[]{:S(2)}) collective-permute-start(bf16[1296,128]{1,0:T(8,128)(2,1)S(1)} %shard_map.115.refs_0_), channel_id=1, source_target_pairs={{0,4},{1,17},{2,6},{3,19},{4,0},{5,21},{6,2},{7,23},{8,12},{9,25},... | collective-permute-start | bytes 995336 | tf_op jit(solution)/shard_map/ppermute | solution.py:252
  56.1 6.4 %collective-permute-start.16 = (bf16[1296,128]{1,0:T(8,128)(2,1)S(1)}, bf16[1296,128]{1,0:T(8,128)(2,1)S(1)}, u32[]{:S(2)}, u32[]{:S(2)}) collective-permute-start(bf16[1296,128]{1,0:T(8,128)(2,1)S(1)} %shard_map.115.refs_0_), channel_id=1, source_target_pairs={{0,1},{1,0},{2,3},{3,2},{4,5},{5,4},{6,7},{7,6},{8,9},{9,8},{10,11... | collective-permute-start | bytes 995336 | tf_op jit(solution)/shard_map/ppermute | solution.py:254
  62.5 2.3 %collective-permute-start.19 = (bf16[1296,128]{1,0:T(8,128)(2,1)S(1)}, bf16[1296,128]{1,0:T(8,128)(2,1)S(1)}, u32[]{:S(2)}, u32[]{:S(2)}) collective-permute-start(bf16[1296,128]{1,0:T(8,128)(2,1)S(1)} %collective-permute-done.15.refs_3_), channel_id=1, source_target_pairs={{0,1},{1,0},{2,3},{3,2},{4,5},{5,4},{6,7},{7,6},{8,9},{9,8},{10,11... | collective-permute-start | bytes 995336 | tf_op jit(solution)/shard_map/ppermute | solution.py:254
  64.7 4.8 %collective-permute-start.18 = (bf16[1296,128]{1,0:T(8,128)(2,1)S(1)}, bf16[1296,128]{1,0:T(8,128)(2,1)S(1)}, u32[]{:S(2)}, u32[]{:S(2)}) collective-permute-start(bf16[1296,128]{1,0:T(8,128)(2,1)S(1)} %collective-permute-done.14.refs_2_), channel_id=1, source_target_pairs={{0,1},{1,0},{2,3},{3,2},{4,5},{5,4},{6,7},{7,6},{8,9},{9,8},{10,11... | collective-permute-start | bytes 995336 | tf_op jit(solution)/shard_map/ppermute | solution.py:254
  71.2 4.7 %shard_map.116 = (f32[528,128]{1,0:T(8,128)S(1)}, bf16[528,128]{1,0:T(8,128)(2,1)S(1)}, bf16[528,128]{1,0:T(8,128)(2,1)S(1)}, bf16[528,128]{1,0:T(8,128)(2,1)S(1)}) custom-call(s32[128]{0:T(128)S(1)} %get-tuple-element.42.pos, s32[128]{0:T(128)S(1)} %get-tuple-element.43.src, bf16[1296,128]{1,0:T(8,128)(2,1)S(1)} %shard_map.115.refs_0_, ...), custom_call_target="tpu_custom_call" | custom-call | flops 536870912 | bytes 8388608 | tf_op jit(solution)/shard_map/pallas_call | solution.py:256
  77.0 1.6 %collective-permute-start.22 = (bf16[528,128]{1,0:T(8,128)(2,1)S(1)}, bf16[528,128]{1,0:T(8,128)(2,1)S(1)}, u32[]{:S(2)}, u32[]{:S(2)}) collective-permute-start(bf16[528,128]{1,0:T(8,128)(2,1)S(1)} %get-tuple-element.38), channel_id=1, source_target_pairs={{0,96},{32,0},{64,32},{96,64},{1,97},{33,1},{65,33},{97,65},{2,98}... | collective-permute-start | bytes 405512 | tf_op jit(solution)/shard_map/ppermute | solution.py:265
  78.7 6.4 %collective-permute-done.20.r1 = bf16[528,128]{1,0:T(8,128)(2,1)S(1)} collective-permute-done((bf16[528,128]{1,0:T(8,128)(2,1)S(1)}, bf16[528,128]{1,0:T(8,128)(2,1)S(1)}, u32[]{:S(2)}, u32[]{:S(2)}) %collective-permute-start.20) | collective-permute-done | bytes 135200 | tf_op jit(solution)/shard_map/ppermute | solution.py:265
  (42 shorter events, 14.9 us)
Async XLA Ops:
  0.6 6.5 %collective-permute-start.1 = (bf16[256,128]{1,0:T(8,128)(2,1)}, bf16[256,128]{1,0:T(8,128)(2,1)S(1)}, u32[]{:S(2)}, u32[]{:S(2)}) collective-permute-start(bf16[256,128]{1,0:T(8,128)(2,1)} %x0.1), channel_id=1, source_target_pairs={{0,64},{32,96},{64,0},{96,32},{1,65},{33,97},{65,1},{97,33},{2,66}... | collective-permute-start | bytes 196616 | tf_op jit(solution)/shard_map/ppermute | solution.py:232
  4.3 4.0 %collective-permute-start = (bf16[256,128]{1,0:T(8,128)(2,1)}, bf16[256,128]{1,0:T(8,128)(2,1)S(1)}, u32[]{:S(2)}, u32[]{:S(2)}) collective-permute-start(bf16[256,128]{1,0:T(8,128)(2,1)} %x0.1), channel_id=1, source_target_pairs={{0,96},{32,0},{64,32},{96,64},{1,97},{33,1},{65,33},{97,65},{2,98}... | collective-permute-start | bytes 196616 | tf_op jit(solution)/shard_map/ppermute | solution.py:232
  5.1 4.5 %collective-permute-start.2 = (bf16[256,128]{1,0:T(8,128)(2,1)}, bf16[256,128]{1,0:T(8,128)(2,1)S(1)}, u32[]{:S(2)}, u32[]{:S(2)}) collective-permute-start(bf16[256,128]{1,0:T(8,128)(2,1)} %x0.1), channel_id=1, source_target_pairs={{0,32},{32,64},{64,96},{96,0},{1,33},{33,65},{65,97},{97,1},{2,34}... | collective-permute-start | bytes 196616 | tf_op jit(solution)/shard_map/ppermute | solution.py:232
  12.7 58.5 %copy-start.1 = (bf16[1,1,128,128,128]{4,3,2,1,0:T(8,128)(2,1)S(1)}, bf16[1,1,128,128,128]{4,3,2,1,0:T(8,128)(2,1)}, u32[]{:S(2)}) copy-start(bf16[1,1,128,128,128]{4,3,2,1,0:T(8,128)(2,1)} %param.11) | copy-start | bytes 12582916
  17.9 4.8 %collective-permute-start.3 = (bf16[4096,128]{1,0:T(8,128)(2,1)S(1)}, bf16[4096,128]{1,0:T(8,128)(2,1)S(1)}, u32[]{:S(2)}, u32[]{:S(2)}) collective-permute-start(bf16[4096,128]{1,0:T(8,128)(2,1)S(1)} %get-tuple-element.24), channel_id=1, source_target_pairs={{0,1},{1,0},{2,3},{3,2},{4,5},{5,4},{6,7},{7,6},{8,9},{9,8},{10,11... | collective-permute-start | bytes 3145736 | tf_op jit(solution)/shard_map/ppermute | solution.py:242
  22.9 6.9 %collective-permute-start.4 = (bf16[1024,128]{1,0:T(8,128)(2,1)S(1)}, bf16[1024,128]{1,0:T(8,128)(2,1)S(1)}, u32[]{:S(2)}, u32[]{:S(2)}) collective-permute-start(bf16[1024,128]{1,0:T(8,128)(2,1)S(1)} %get-tuple-element.26), channel_id=1, source_target_pairs={{0,2},{1,9},{2,4},{3,11},{4,6},{5,13},{6,0},{7,15},{8,10},{9,17},{... | collective-permute-start | bytes 786440 | tf_op jit(solution)/shard_map/ppermute | solution.py:244
  24.2 9.5 %collective-permute-start.5 = (bf16[1024,128]{1,0:T(8,128)(2,1)S(1)}, bf16[1024,128]{1,0:T(8,128)(2,1)S(1)}, u32[]{:S(2)}, u32[]{:S(2)}) collective-permute-start(bf16[1024,128]{1,0:T(8,128)(2,1)S(1)} %get-tuple-element.27), channel_id=1, source_target_pairs={{0,4},{1,17},{2,6},{3,19},{4,0},{5,21},{6,2},{7,23},{8,12},{9,25},... | collective-permute-start | bytes 786440 | tf_op jit(solution)/shard_map/ppermute | solution.py:244
  26.8 6.9 %collective-permute-start.6 = (bf16[1024,128]{1,0:T(8,128)(2,1)S(1)}, bf16[1024,128]{1,0:T(8,128)(2,1)S(1)}, u32[]{:S(2)}, u32[]{:S(2)}) collective-permute-start(bf16[1024,128]{1,0:T(8,128)(2,1)S(1)} %get-tuple-element.28), channel_id=1, source_target_pairs={{0,6},{1,25},{2,0},{3,27},{4,2},{5,29},{6,4},{7,31},{8,14},{9,1},{... | collective-permute-start | bytes 786440 | tf_op jit(solution)/shard_map/ppermute | solution.py:244
  33.8 5.4 %collective-permute-start.7 = (bf16[256,128]{1,0:T(8,128)(2,1)S(1)}, bf16[256,128]{1,0:T(8,128)(2,1)S(1)}, u32[]{:S(2)}, u32[]{:S(2)}) collective-permute-start(bf16[256,128]{1,0:T(8,128)(2,1)S(1)} %get-tuple-element.30), channel_id=1, source_target_pairs={{0,8},{1,3},{2,10},{3,5},{4,12},{5,7},{6,14},{7,1},{8,16},{9,11},{... | collective-permute-start | bytes 196616 | tf_op jit(solution)/shard_map/ppermute | solution.py:246
  35.2 5.7 %collective-permute-start.8 = (bf16[256,128]{1,0:T(8,128)(2,1)S(1)}, bf16[256,128]{1,0:T(8,128)(2,1)S(1)}, u32[]{:S(2)}, u32[]{:S(2)}) collective-permute-start(bf16[256,128]{1,0:T(8,128)(2,1)S(1)} %get-tuple-element.31), channel_id=1, source_target_pairs={{0,16},{1,5},{2,18},{3,7},{4,20},{5,1},{6,22},{7,3},{8,24},{9,13},... | collective-permute-start | bytes 196616 | tf_op jit(solution)/shard_map/ppermute | solution.py:246
  38.5 3.1 %collective-permute-start.9 = (bf16[256,128]{1,0:T(8,128)(2,1)S(1)}, bf16[256,128]{1,0:T(8,128)(2,1)S(1)}, u32[]{:S(2)}, u32[]{:S(2)}) collective-permute-start(bf16[256,128]{1,0:T(8,128)(2,1)S(1)} %get-tuple-element.32), channel_id=1, source_target_pairs={{0,24},{1,7},{2,26},{3,1},{4,28},{5,3},{6,30},{7,5},{8,0},{9,15},{... | collective-permute-start | bytes 196616 | tf_op jit(solution)/shard_map/ppermute | solution.py:246
  42.6 5.3 %collective-permute-start.12 = (bf16[528,128]{1,0:T(8,128)(2,1)S(1)}, bf16[528,128]{1,0:T(8,128)(2,1)S(1)}, u32[]{:S(2)}, u32[]{:S(2)}) collective-permute-start(bf16[528,128]{1,0:T(8,128)(2,1)S(1)} %get-tuple-element.34.m0), channel_id=1, source_target_pairs={{0,24},{1,7},{2,26},{3,1},{4,28},{5,3},{6,30},{7,5},{8,0},{9,15},{... | collective-permute-start | bytes 405512 | tf_op jit(solution)/shard_map/ppermute | solution.py:250
  44.6 5.5 %collective-permute-start.11 = (bf16[528,128]{1,0:T(8,128)(2,1)S(1)}, bf16[528,128]{1,0:T(8,128)(2,1)S(1)}, u32[]{:S(2)}, u32[]{:S(2)}) collective-permute-start(bf16[528,128]{1,0:T(8,128)(2,1)S(1)} %get-tuple-element.34.m0), channel_id=1, source_target_pairs={{0,16},{1,5},{2,18},{3,7},{4,20},{5,1},{6,22},{7,3},{8,24},{9,13},... | collective-permute-start | bytes 405512 | tf_op jit(solution)/shard_map/ppermute | solution.py:250
  44.9 6.5 %collective-permute-start.10 = (bf16[528,128]{1,0:T(8,128)(2,1)S(1)}, bf16[528,128]{1,0:T(8,128)(2,1)S(1)}, u32[]{:S(2)}, u32[]{:S(2)}) collective-permute-start(bf16[528,128]{1,0:T(8,128)(2,1)S(1)} %get-tuple-element.34.m0), channel_id=1, source_target_pairs={{0,8},{1,3},{2,10},{3,5},{4,12},{5,7},{6,14},{7,1},{8,16},{9,11},{... | collective-permute-start | bytes 405512 | tf_op jit(solution)/shard_map/ppermute | solution.py:250
  51.5 11.0 %collective-permute-start.15 = (bf16[1296,128]{1,0:T(8,128)(2,1)S(1)}, bf16[1296,128]{1,0:T(8,128)(2,1)S(1)}, u32[]{:S(2)}, u32[]{:S(2)}) collective-permute-start(bf16[1296,128]{1,0:T(8,128)(2,1)S(1)} %shard_map.115.refs_0_), channel_id=1, source_target_pairs={{0,2},{1,9},{2,4},{3,11},{4,6},{5,13},{6,0},{7,15},{8,10},{9,17},{... | collective-permute-start | bytes 995336 | tf_op jit(solution)/shard_map/ppermute | solution.py:252
  52.7 12.1 %collective-permute-start.14 = (bf16[1296,128]{1,0:T(8,128)(2,1)S(1)}, bf16[1296,128]{1,0:T(8,128)(2,1)S(1)}, u32[]{:S(2)}, u32[]{:S(2)}) collective-permute-start(bf16[1296,128]{1,0:T(8,128)(2,1)S(1)} %shard_map.115.refs_0_), channel_id=1, source_target_pairs={{0,4},{1,17},{2,6},{3,19},{4,0},{5,21},{6,2},{7,23},{8,12},{9,25},... | collective-permute-start | bytes 995336 | tf_op jit(solution)/shard_map/ppermute | solution.py:252
  54.9 14.6 %collective-permute-start.13 = (bf16[1296,128]{1,0:T(8,128)(2,1)S(1)}, bf16[1296,128]{1,0:T(8,128)(2,1)S(1)}, u32[]{:S(2)}, u32[]{:S(2)}) collective-permute-start(bf16[1296,128]{1,0:T(8,128)(2,1)S(1)} %shard_map.115.refs_0_), channel_id=1, source_target_pairs={{0,6},{1,25},{2,0},{3,27},{4,2},{5,29},{6,4},{7,31},{8,14},{9,1},{... | collective-permute-start | bytes 995336 | tf_op jit(solution)/shard_map/ppermute | solution.py:252
  56.1 13.5 %collective-permute-start.16 = (bf16[1296,128]{1,0:T(8,128)(2,1)S(1)}, bf16[1296,128]{1,0:T(8,128)(2,1)S(1)}, u32[]{:S(2)}, u32[]{:S(2)}) collective-permute-start(bf16[1296,128]{1,0:T(8,128)(2,1)S(1)} %shard_map.115.refs_0_), channel_id=1, source_target_pairs={{0,1},{1,0},{2,3},{3,2},{4,5},{5,4},{6,7},{7,6},{8,9},{9,8},{10,11... | collective-permute-start | bytes 995336 | tf_op jit(solution)/shard_map/ppermute | solution.py:254
  62.5 7.1 %collective-permute-start.19 = (bf16[1296,128]{1,0:T(8,128)(2,1)S(1)}, bf16[1296,128]{1,0:T(8,128)(2,1)S(1)}, u32[]{:S(2)}, u32[]{:S(2)}) collective-permute-start(bf16[1296,128]{1,0:T(8,128)(2,1)S(1)} %collective-permute-done.15.refs_3_), channel_id=1, source_target_pairs={{0,1},{1,0},{2,3},{3,2},{4,5},{5,4},{6,7},{7,6},{8,9},{9,8},{10,11... | collective-permute-start | bytes 995336 | tf_op jit(solution)/shard_map/ppermute | solution.py:254
  64.7 6.0 %collective-permute-start.18 = (bf16[1296,128]{1,0:T(8,128)(2,1)S(1)}, bf16[1296,128]{1,0:T(8,128)(2,1)S(1)}, u32[]{:S(2)}, u32[]{:S(2)}) collective-permute-start(bf16[1296,128]{1,0:T(8,128)(2,1)S(1)} %collective-permute-done.14.refs_2_), channel_id=1, source_target_pairs={{0,1},{1,0},{2,3},{3,2},{4,5},{5,4},{6,7},{7,6},{8,9},{9,8},{10,11... | collective-permute-start | bytes 995336 | tf_op jit(solution)/shard_map/ppermute | solution.py:254
  69.5 1.7 %collective-permute-start.17 = (bf16[1296,128]{1,0:T(8,128)(2,1)S(1)}, bf16[1296,128]{1,0:T(8,128)(2,1)S(1)}, u32[]{:S(2)}, u32[]{:S(2)}) collective-permute-start(bf16[1296,128]{1,0:T(8,128)(2,1)S(1)} %collective-permute-done.13.refs_1_), channel_id=1, source_target_pairs={{0,1},{1,0},{2,3},{3,2},{4,5},{5,4},{6,7},{7,6},{8,9},{9,8},{10,11... | collective-permute-start | bytes 995336 | tf_op jit(solution)/shard_map/ppermute | solution.py:254
  75.9 9.2 %collective-permute-start.20 = (bf16[528,128]{1,0:T(8,128)(2,1)S(1)}, bf16[528,128]{1,0:T(8,128)(2,1)S(1)}, u32[]{:S(2)}, u32[]{:S(2)}) collective-permute-start(bf16[528,128]{1,0:T(8,128)(2,1)S(1)} %get-tuple-element.36), channel_id=1, source_target_pairs={{0,32},{32,64},{64,96},{96,0},{1,33},{33,65},{65,97},{97,1},{2,34}... | collective-permute-start | bytes 405512 | tf_op jit(solution)/shard_map/ppermute | solution.py:265
  76.0 9.1 %collective-permute-start.21 = (bf16[528,128]{1,0:T(8,128)(2,1)S(1)}, bf16[528,128]{1,0:T(8,128)(2,1)S(1)}, u32[]{:S(2)}, u32[]{:S(2)}) collective-permute-start(bf16[528,128]{1,0:T(8,128)(2,1)S(1)} %get-tuple-element.37), channel_id=1, source_target_pairs={{0,64},{32,96},{64,0},{96,32},{1,65},{33,97},{65,1},{97,33},{2,66}... | collective-permute-start | bytes 405512 | tf_op jit(solution)/shard_map/ppermute | solution.py:265
  77.0 8.2 %collective-permute-start.22 = (bf16[528,128]{1,0:T(8,128)(2,1)S(1)}, bf16[528,128]{1,0:T(8,128)(2,1)S(1)}, u32[]{:S(2)}, u32[]{:S(2)}) collective-permute-start(bf16[528,128]{1,0:T(8,128)(2,1)S(1)} %get-tuple-element.38), channel_id=1, source_target_pairs={{0,96},{32,0},{64,32},{96,64},{1,97},{33,1},{65,33},{97,65},{2,98}... | collective-permute-start | bytes 405512 | tf_op jit(solution)/shard_map/ppermute | solution.py:265
  (5 other events, 89.9 us)

commit v2 on v0

v2 whole, which is shorter than its diff:
```python
import functools

import jax
import jax.numpy as jnp
from jax import lax
from jax.experimental import pallas as pl
from jax.experimental.pallas import tpu as pltpu
from jax.sharding import PartitionSpec as P

F32 = jnp.float32
BF16 = jnp.bfloat16
B = 128
VMEM = pl.BlockSpec(memory_space=pltpu.VMEM)
SMEM = pl.BlockSpec(memory_space=pltpu.SMEM)
ANY = pl.BlockSpec(memory_space=pl.ANY)
TAIL = 272
UNROLL = 16
LEAD = 2**24
WIDTH = 144
TAB = 384
BACKWARD_TAB = 512


def at(y, z, core):
    return (y * 4 + z) * 2 + core


def col_shift(first, d):
    pairs = []
    for y in range(4):
        for z in range(4):
            for core in range(2):
                along_z = (core == 0) == first
                to = at(y, (z + d) % 4, core) if along_z else at((y + d) % 4, z, core)
                pairs.append((at(y, z, core), to))
    return pairs


def core_swap():
    return [(c, c ^ 1) for c in range(32)]


def row_shift(d):
    return [(r, (r + d) % 4) for r in range(4)]


def call(kernel, outs, ins, scratch=(), tiles=0, nbytes=0):
    return pl.pallas_call(
        kernel,
        out_shape=outs,
        in_specs=ins,
        out_specs=jax.tree.map(lambda _: VMEM, outs),
        scratch_shapes=list(scratch),
        compiler_params=pltpu.CompilerParams(vmem_limit_bytes=24 * 2**20),
        cost_estimate=pl.CostEstimate(
            flops=2 * tiles * B**3, bytes_accessed=nbytes + tiles * 2**16, transcendentals=0
        ),
    )


def sds(rows, cols=B, dtype=BF16):
    return jax.ShapeDtypeStruct((rows, cols), dtype)


def permute(arrays, axis, pairs):
    arrays = lax.optimization_barrier(tuple(arrays))
    return [lax.ppermute(a, axis, p) for a, p in zip(arrays, pairs)]


ORDER = (2, 1, 3)


def live_slots(count, live):
    slot = lax.broadcasted_iota(jnp.int32, (1, 128), 1)
    live[...] = (slot < count[0, 0]).astype(jnp.int32)


def sort_tiles(rows, cols, live, forward_tab, backward_tab):
    r, c = lax.axis_index("row"), lax.axis_index("col")
    core, z, y = c % 2, (c // 2) % 4, c // 8
    rows, cols = rows[...], cols[...]
    owner, sub = rows // 2, rows % 2
    core_to, z_to, y_to = owner % 2, (owner // 2) % 4, owner // 8
    dz, dy = (z_to - z + 4) % 4, (y_to - y + 4) % 4
    first = jnp.where(core_to == 0, dz, dy)
    second = jnp.where(core_to == 0, dy, dz)
    pos = (first * 4 + second) * 2 + sub
    half = (core_to != core).astype(jnp.int32)
    ahead = (cols // 2 - r + 4) % 4
    slot = lax.broadcasted_iota(jnp.int32, (1, 128), 1)

    def table(key, keys, take, to, pad, width):
        key = jnp.where(live[...] == 1, key, keys)
        is_key = [jnp.where(key == k, 1.0, 0.0) for k in range(keys)]
        is_key = jnp.concatenate(is_key + [jnp.zeros((8 - keys, 128), F32)]).astype(BF16)
        low = lax.broadcasted_iota(jnp.int32, (128, 128), 0)
        high = lax.broadcasted_iota(jnp.int32, (128, 128), 1)
        before = jnp.where(low < high, 1.0, 0.0).astype(BF16)
        rank = jnp.dot(is_key, before, preferred_element_type=F32)
        place = jnp.full((1, 128), -1.0, F32)
        for k in range(keys):
            place = jnp.where(key == k, rank[k : k + 1] + float(k * WIDTH), place)
        place = jnp.broadcast_to(place, (8, 128)).T[:, 0:1].astype(jnp.int32)
        spots = lax.broadcasted_iota(jnp.int32, (128, width), 1)
        at_spot = jnp.where(place == spots, 1.0, 0.0).astype(BF16)
        fields = [slot.astype(F32), take.astype(F32), to.astype(F32), jnp.ones((1, 128), F32)]
        fields = jnp.concatenate(fields + [jnp.zeros((4, 128), F32)]).astype(BF16)
        found = jnp.dot(fields, at_spot, preferred_element_type=F32).astype(jnp.int32)
        entry = found[0:1] + found[1:2] * 2**8 + found[2:3] * 2**16
        entry = jnp.where(found[3:4] > 0, entry, pad * 2**16)
        total = jnp.sum(is_key.astype(F32), axis=1, keepdims=True).astype(jnp.int32)
        for k in range(keys):
            groups = (total[k : k + 1] + (UNROLL - 1)) // UNROLL
            entry = jnp.where(spots[0:1] == keys * WIDTH + k, groups, entry)
        return entry

    forward_tab[...] = table(1 - half, 2, ahead * 2 + cols % 2, pos, 32, TAB)
    key = jnp.where(half == 0, 0, jnp.where(ahead == 0, 2, 1))
    backward_tab[...] = table(key, 3, pos, ahead * 2 + cols % 2, 8, BACKWARD_TAB)


def hold(x, adj, x_held, tiles):
    x_held[...] = x[...]

    def copy(i, _):
        tiles[i] = adj[i]
        return 0

    lax.fori_loop(0, 128, copy, 0, unroll=8)


def each_tile(tab, key, keys, adj, product, acc):
    def body(g, _):
        parts = []
        for u in range(UNROLL):
            e = tab[0, key * WIDTH + g * UNROLL + u]
            parts.append((product(adj[e & 127], (e >> 8) & 63), e >> 16))
        for part, to in parts:
            acc[to] += part
        return 0

    lax.fori_loop(0, tab[0, keys * WIDTH + key], body, 0)


def load_blocks(refs, rows, to):
    for k, ref in enumerate(refs):
        for i in range(rows // B):
            to[k * (rows // B) + i] = ref[i * B : (i + 1) * B]


def forward_tiles(key, tab, x0, x1, x2, x3, adj, out, *scratch):
    acc, xs = scratch if key == 0 else (out, scratch[0])
    load_blocks([x0, x1, x2, x3], 256, xs)

    def clear(i, _):
        acc[i] = jnp.zeros((B, B), F32)
        return 0

    lax.fori_loop(0, 32, clear, 0)
    each_tile(tab, key, 2, adj, lambda t, i: jnp.dot(t, xs[i], preferred_element_type=F32), acc)
    if key == 0:

        def store(i, _):
            out[pl.ds(pl.multiple_of(i * B, B), B)] = acc[i].astype(BF16)
            return 0

        lax.fori_loop(0, 32, store, 0)


def core_sum(acc, got, m0, m1, m2, m3):
    for k, m in enumerate((m0, m1, m2, m3)):
        for i in range(8):
            rows = pl.ds((k * 8 + i) * B, B)
            total = acc[k * 8 + i] + got[rows].astype(F32)
            m[i * B : (i + 1) * B] = total.astype(m.dtype)


def first_sum(m0, r1, r2, r3, cot, total, msg):
    for i in range(0, 1024, 256):
        rows = pl.ds(i, 256)
        t = m0[rows] + (r1[rows].astype(F32) + r2[rows].astype(F32) + r3[rows].astype(F32))
        total[rows] = t
        msg[rows] = t.astype(BF16)
    msg[1024:1280] = cot[:, 0:B]
    msg[1280:1536] = cot[:, B : 2 * B]


def put_tail(msg, base, wg, bg):
    msg[pl.ds(base, 256)] = wg.astype(msg.dtype)
    if msg.dtype == F32:
        msg[pl.ds(base + 256, 16)] = jnp.concatenate([bg, jnp.zeros((14, B), F32)])
    else:
        high = bg.astype(BF16).astype(F32)
        low = bg - high
        block = jnp.concatenate([high, low, jnp.zeros((12, B), F32)])
        msg[pl.ds(base + 256, 16)] = block.astype(BF16)


def get_tail(msg, base):
    wg = msg[pl.ds(base, 256)].astype(F32)
    block = msg[pl.ds(base + 256, 16)].astype(F32)
    return wg, block[0:2] + block[2:4]


def local(s0, r1, r2, r3, weight, bias, cot, act, msg):
    w = weight[...]
    over_nodes = (((0,), (0,)), ((), ()))
    wg, bg = jnp.zeros((B, 256), F32), jnp.zeros((1, 256), F32)
    for k, r in enumerate((None, r3, r2, r1)):
        if k == 0:
            c = cot[...]
        else:
            c = jnp.concatenate([r[1024:1280], r[1280:1536]], axis=1)
        y = s0[pl.ds(k * 256, 256)]
        for d, r in ((1, r1), (2, r2), (3, r3)):
            y += r[pl.ds((k + d) % 4 * 256, 256)].astype(F32)
        y_high = y.astype(BF16)
        y_low = (y - y_high.astype(F32)).astype(BF16)
        summed = jnp.dot(y_high, w, preferred_element_type=F32) + jnp.dot(
            y_low, w, preferred_element_type=F32
        )
        pre = summed + bias[...]
        sig = jax.nn.sigmoid(pre)
        if k == 0:
            act[...] = (pre * sig).astype(BF16)
        slope = sig * (1.0 + pre * (1.0 - sig))
        grad = (c.astype(F32) * slope).astype(BF16)
        g = lax.dot_general(w, grad, (((1,), (1,)), ((), ())), preferred_element_type=F32)
        g = g.astype(BF16)
        msg[pl.ds(k * 256, B)] = g[:, 0:B]
        msg[pl.ds(k * 256 + B, B)] = g[:, B : 2 * B]
        wg += lax.dot_general(y_high, grad, over_nodes, preferred_element_type=F32)
        wg += lax.dot_general(y_low, grad, over_nodes, preferred_element_type=F32)
        bg += jnp.sum(grad.astype(F32), axis=0, keepdims=True)
    put_tail(
        msg,
        1024,
        jnp.concatenate([wg[:, 0:B], wg[:, B : 2 * B]]),
        jnp.concatenate([bg[:, 0:B], bg[:, B : 2 * B]]),
    )


def sum_tails(pieces):
    wg, bg = get_tail(pieces[0], 1024)
    for piece in pieces[1:]:
        wg_r, bg_r = get_tail(piece, 1024)
        wg += wg_r
        bg += bg_r
    return wg, bg


def backward_tiles(key, tab, adj, *refs):
    def product(t, i):
        return jnp.dot(gs[i], t, preferred_element_type=F32)

    if key == 0:
        pieces, (acc, tail, gs) = refs[:4], refs[4:]
        load_blocks(pieces, 1024, gs)
        acc[...] = jnp.zeros((9, B, B), F32)
        each_tile(tab, 0, 3, adj, product, acc)
        put_tail(tail, 0, *sum_tails(pieces))
        return
    if key == 1:
        pieces, (acc_in, tail_in, m1, m2, m3, gs, tail, acc) = refs[:4], refs[4:]
        outs = (m1, m2, m3)
        load_blocks(pieces, 1024, gs)
        wg, bg = sum_tails(pieces)
        put_tail(tail, 0, tail_in[0:256] + wg, tail_in[256:258] + bg)
    else:
        gs, acc_in, tail, m0, acc = refs
        outs = (m0,)
    first = 2 if key == 1 else 0
    last = first + 2 * len(outs)
    acc[first:last] = acc_in[first:last]
    each_tile(tab, key, 3, adj, product, acc)
    for k, m in enumerate(outs):
        m[0:B] = acc[first + 2 * k].astype(m.dtype)
        m[B : 2 * B] = acc[first + 2 * k + 1].astype(m.dtype)
        put_tail(m, 256, tail[0:256], tail[256:258])


def last_sum(m0, r1, r2, r3, feat, wgrad, bgrad):
    for k in range(2):
        rows = pl.ds(k * B, B)
        total = m0[rows] + (r1[rows].astype(F32) + r2[rows].astype(F32) + r3[rows].astype(F32))
        feat[rows] = total.T.astype(BF16)
    wg, block = m0[pl.ds(256, 256)], m0[pl.ds(512, 16)]
    bg = block[0:2]
    for r in (r1, r2, r3):
        wg_r, bg_r = get_tail(r, 256)
        wg += wg_r
        bg += bg_r
    wgrad[:, 0:B] = wg[0:B]
    wgrad[:, B : 2 * B] = wg[B : 2 * B]
    bgrad[:, 0:B] = bg[0:1]
    bgrad[:, B : 2 * B] = bg[1:2]


def on_device(
    features, weight, bias_vector, adjacency, tile_rows, tile_cols, tile_count, cotangent
):
    adj = adjacency[0, 0]
    x2, x1, x3 = permute([features] * 3, "row", [row_shift(d) for d in ORDER])
    live = call(live_slots, sds(1, 128, jnp.int32), [SMEM], nbytes=LEAD)(tile_count)
    forward_tab, backward_tab = call(
        sort_tiles,
        (sds(1, TAB, jnp.int32), sds(1, BACKWARD_TAB, jnp.int32)),
        [VMEM] * 3,
    )(tile_rows[0], tile_cols[0], live)
    x0, tiles = call(
        hold, (sds(256), jax.ShapeDtypeStruct((128, B, B), BF16)), [VMEM, VMEM]
    )(features, adj)
    xs = (x0, x3, x2, x1)
    half = jax.ShapeDtypeStruct((33, B, B), F32)
    other = call(
        functools.partial(forward_tiles, 0),
        sds(4096),
        [SMEM] + [VMEM] * 5,
        [pltpu.VMEM((33, B, B), F32), pltpu.VMEM((8, B, B), BF16)],
        tiles=64,
    )(forward_tab, *xs, tiles)
    got = lax.ppermute(other, "col", core_swap())
    acc = call(
        functools.partial(forward_tiles, 1),
        half,
        [SMEM] + [VMEM] * 5,
        [pltpu.VMEM((8, B, B), BF16)],
    )(forward_tab, *xs, tiles)
    ms = call(core_sum, (sds(1024, dtype=F32),) + (sds(1024),) * 3, [VMEM] * 2)(acc, got)
    r2, r1, r3 = permute([ms[d] for d in ORDER], "col", [col_shift(True, d) for d in ORDER])
    total, msg = call(first_sum, (sds(1024, dtype=F32), sds(1536)), [VMEM] * 5)(
        ms[0], r1, r2, r3, cotangent
    )
    r2, r1, r3 = permute([msg] * 3, "col", [col_shift(False, d) for d in ORDER])
    act, msg = call(local, (sds(256, 256), sds(1024 + TAIL)), [VMEM] * 7)(
        total, r1, r2, r3, weight, bias_vector.reshape(1, 256), cotangent
    )
    r2, r1, r3 = permute([msg] * 3, "col", [col_shift(True, d) for d in ORDER])
    mine = (msg, r3, r2, r1)
    theirs = [lax.ppermute(m, "col", core_swap()) for m in mine]
    out, tail = sds(256 + TAIL), sds(TAIL, dtype=F32)
    sums, blocks = (jax.ShapeDtypeStruct(s, t) for s, t in (((9, B, B), F32), ((32, B, B), BF16)))
    sums, tail = call(
        functools.partial(backward_tiles, 0),
        (sums, tail),
        [SMEM] + [VMEM] * 5,
        [pltpu.VMEM((32, B, B), BF16)],
        tiles=64,
    )(backward_tab, adj, *mine)
    *ms, blocks, tail = call(
        functools.partial(backward_tiles, 1),
        (out, out, out, blocks, sds(TAIL, dtype=F32)),
        [SMEM] + [VMEM] * 7,
        [pltpu.VMEM((9, B, B), F32)],
        tiles=48,
    )(backward_tab, adj, *theirs, sums, tail)
    m = call(
        functools.partial(backward_tiles, 2),
        sds(256 + TAIL, dtype=F32),
        [SMEM] + [VMEM] * 4,
        [pltpu.VMEM((9, B, B), F32)],
    )(backward_tab, adj, blocks, sums, tail)
    ms = [ms[d - 1] for d in ORDER]
    rs = [lax.ppermute(a, "row", row_shift(d)) for a, d in zip(ms, ORDER)]
    feat, wgrad, bgrad = call(
        last_sum, (sds(256, 128), sds(128, 256, F32), sds(1, 256, F32)), [VMEM] * 4
    )(m, *rs)
    return (act, feat, wgrad, bgrad.reshape(256))


def solution(mesh):
    placed = (
        P(("row", "col"), None),
        P(),
        P(),
        P("row", "col", None, None, None),
        P("row", "col", None),
        P("row", "col", None),
        P("row", "col"),
        P(("row", "col"), None),
    )
    return jax.shard_map(
        on_device,
        mesh=mesh,
        in_specs=placed,
        out_specs=(P(("row", "col"), None), P(("row", "col"), None), P(), P()),
        check_vma=False,
    )
```

time: 453 us -> 73.2 us (0.16)
  waiting for transfers between devices: 257 us -> 23.9 us
  blocking collectives: 76.7 us -> 0 us
  local copies, waits for them, and re-layouts: 47.3 us -> 3.06 us
  starting transfers between devices: 0.16 us -> 34.8 us
  other arithmetic: 33.7 us -> 0 us
  matrix products: 21.9 us -> 0 us
  between operations: 14.5 us -> 1.5 us
  Pallas kernels: 0 us -> 9.76 us
    psum x1 -> x0, waiting for transfers between devices: 136 us -> none  [on_device(): grad_weight, grad_bias = lax.psum((weight_term, bias_term), ('row', 'col'))]
    reduce_scatter x2 -> x0, waiting for transfers between devices: 95.3 us -> none  [the longest x1 95.3 us: on_device(): lax.psum_scatter(partial_value, 'col', scatter_dimension=0, tiled=True)]
    psum x1 -> x0, blocking collectives: 64.4 us -> none  [on_device(): grad_weight, grad_bias = lax.psum((weight_term, bias_term), ('row', 'col'))]
    dot_general x2 -> x0, local copies, waits for them, and re-layouts: 39.2 us -> none  [the longest x1 22.4 us: on_device(): jnp.einsum('ijab,iah->jbh', dense, row_grad, preferred_element_type=jnp.f...]
    ppermute x0 -> x20, starting transfers between devices: none -> 34.8 us  [the longest x12 17.9 us: permute(): return [lax.ppermute(a, axis, p) for a, p in zip(arrays, pairs)]]
    scatter-add x1 -> x0, other arithmetic: 26.8 us -> none  [build_dense(): return dense.at[index_out, index_in].add(tiles)]
    all_gather x1 -> x0, waiting for transfers between devices: 26.6 us -> none  [on_device(): row_grad = lax.all_gather(grad_own, 'col', axis=0, tiled=True)]
    ppermute x0 -> x20, waiting for transfers between devices: none -> 23.9 us  [the longest x12 17.9 us: permute(): return [lax.ppermute(a, axis, p) for a, p in zip(arrays, pairs)]]
  transfers between devices with their start and end apart: 4 -> 20, of which waited for: 3 -> 10; matrix products, arithmetic and copies ran while one was open for 5% -> 0% of each run, Pallas kernels for 0% -> 6%
where the time goes in v2:
time: 73.2 us; the launch traced here: 73 us
  starting transfers between devices  34.8 us (48%)
  waiting for transfers between devices  23.9 us (33%)
  Pallas kernels  9.76 us (13%)
  local copies, waits for them, and re-layouts  3.06 us (4%)
  between operations  1.5 us (2%)
    ppermute x12, waiting for transfers between devices, permute(): return [lax.ppermute(a, axis, p) for a, p in zip(arrays, pairs)]  17.9 us
    ppermute x12, starting transfers between devices, permute(): return [lax.ppermute(a, axis, p) for a, p in zip(arrays, pairs)]  17.9 us
    ppermute x4, starting transfers between devices, on_device(): theirs = [lax.ppermute(m, 'col', core_swap()) for m in mine]  10.3 us
    ppermute x3, waiting for transfers between devices, on_device(): rs = [lax.ppermute(a, 'row', row_shift(d)) for a, d in zip(ms, ORDER)]  5.07 us
    ppermute x3, starting transfers between devices, on_device(): rs = [lax.ppermute(a, 'row', row_shift(d)) for a, d in zip(ms, ORDER)]  4.47 us
    unnamed x16, local copies, waits for them, and re-layouts  3.06 us
    ppermute x1, starting transfers between devices, on_device(): got = lax.ppermute(other, 'col', core_swap())  2.09 us
    pallas_call x1, Pallas kernels, on_device(): call(functools.partial(forward_tiles, 0), sds(4096), [SMEM] + [VMEM] * 5,...  1.61 us
  transfers between devices with their start and end apart: 20, of which 10 were waited for; matrix products, arithmetic and copies ran while one was open for 0% of the time, Pallas kernels for 6%

profile of v2, /device:TPU:1, one launch (start us, length us, event | category | flops | bytes accessed | tf_op | source)
XLA Modules:
  0.0 73.0 jit_solution(3944871985371461953)
XLA Ops:
  0.7 3.4 %collective-permute-start = (bf16[256,128]{1,0:T(8,128)(2,1)}, bf16[256,128]{1,0:T(8,128)(2,1)S(1)}, u32[]{:S(2)}, u32[]{:S(2)}) collective-permute-start(bf16[256,128]{1,0:T(8,128)(2,1)} %x.1), channel_id=1, source_target_pairs={{0,96},{32,0},{64,32},{96,64},{1,97},{33,1},{65,33},{97,65},{2,98}... | collective-permute-start | bytes 196616 | tf_op jit(solution)/shard_map/ppermute | solution.py:67
  5.8 2.2 %copy-done = bf16[1,1,128,128,128]{4,3,2,1,0:T(8,128)(2,1)S(1)} copy-done((bf16[1,1,128,128,128]{4,3,2,1,0:T(8,128)(2,1)S(1)}, bf16[1,1,128,128,128]{4,3,2,1,0:T(8,128)(2,1)}, u32[]{:S(2)}) %copy-start) | copy-done | bytes 4194328
  10.0 1.6 %shard_map.115 = bf16[4096,128]{1,0:T(8,128)(2,1)S(1)} custom-call(s32[1,384]{1,0:T(1,128)S(1)} %get-tuple-element.38.tab, bf16[256,128]{1,0:T(8,128)(2,1)S(1)} %get-tuple-element.39.x0, bf16[256,128]{1,0:T(8,128)(2,1)S(1)} %collective-permute-done.x1, bf16[256,128]{1,0:T(8,128)(2,1)S(1)} %collective-permute-done.1.x2, ...), custom_call_target="tpu_custom_call" | custom-call | flops 268435456 | bytes 4194304 | tf_op jit(solution)/shard_map/pallas_call | solution.py:315
  11.6 2.1 %collective-permute-start.3 = (bf16[4096,128]{1,0:T(8,128)(2,1)S(1)}, bf16[4096,128]{1,0:T(8,128)(2,1)S(1)}, u32[]{:S(2)}, u32[]{:S(2)}) collective-permute-start(bf16[4096,128]{1,0:T(8,128)(2,1)S(1)} %shard_map.115), channel_id=1, source_target_pairs={{0,1},{1,0},{2,3},{3,2},{4,5},{5,4},{6,7},{7,6},{8,9},{9,8},{10,11... | collective-permute-start | bytes 3145736 | tf_op jit(solution)/shard_map/ppermute | solution.py:322
  13.7 1.4 %shard_map.114.acc = f32[33,128,128]{2,1,0:T(8,128)S(1)} custom-call(s32[1,384]{1,0:T(1,128)S(1)} %get-tuple-element.38.tab, bf16[256,128]{1,0:T(8,128)(2,1)S(1)} %get-tuple-element.39.x0, bf16[256,128]{1,0:T(8,128)(2,1)S(1)} %collective-permute-done.x1, bf16[256,128]{1,0:T(8,128)(2,1)S(1)} %collective-permute-done.1.x2, ...), custom_call_target="tpu_custom_call" | custom-call | tf_op jit(solution)/shard_map/pallas_call | solution.py:323
  16.3 1.7 %collective-permute-start.4 = (bf16[1024,128]{1,0:T(8,128)(2,1)S(1)}, bf16[1024,128]{1,0:T(8,128)(2,1)S(1)}, u32[]{:S(2)}, u32[]{:S(2)}) collective-permute-start(bf16[1024,128]{1,0:T(8,128)(2,1)S(1)} %get-tuple-element.48), channel_id=1, source_target_pairs={{0,2},{1,9},{2,4},{3,11},{4,6},{5,13},{6,0},{7,15},{8,10},{9,17},{... | collective-permute-start | bytes 786440 | tf_op jit(solution)/shard_map/ppermute | solution.py:67
  17.9 2.6 %collective-permute-start.5 = (bf16[1024,128]{1,0:T(8,128)(2,1)S(1)}, bf16[1024,128]{1,0:T(8,128)(2,1)S(1)}, u32[]{:S(2)}, u32[]{:S(2)}) collective-permute-start(bf16[1024,128]{1,0:T(8,128)(2,1)S(1)} %get-tuple-element.49), channel_id=1, source_target_pairs={{0,4},{1,17},{2,6},{3,19},{4,0},{5,21},{6,2},{7,23},{8,12},{9,25},... | collective-permute-start | bytes 786440 | tf_op jit(solution)/shard_map/ppermute | solution.py:67
  21.3 2.1 %collective-permute-done.4.r1 = bf16[1024,128]{1,0:T(8,128)(2,1)S(1)} collective-permute-done((bf16[1024,128]{1,0:T(8,128)(2,1)S(1)}, bf16[1024,128]{1,0:T(8,128)(2,1)S(1)}, u32[]{:S(2)}, u32[]{:S(2)}) %collective-permute-start.4) | collective-permute-done | bytes 262176 | tf_op jit(solution)/shard_map/ppermute | solution.py:67
  23.4 4.0 %collective-permute-done.5.r2 = bf16[1024,128]{1,0:T(8,128)(2,1)S(1)} collective-permute-done((bf16[1024,128]{1,0:T(8,128)(2,1)S(1)}, bf16[1024,128]{1,0:T(8,128)(2,1)S(1)}, u32[]{:S(2)}, u32[]{:S(2)}) %collective-permute-start.5) | collective-permute-done | bytes 262176 | tf_op jit(solution)/shard_map/ppermute | solution.py:67
  27.6 1.1 %collective-permute-start.7 = (bf16[1536,128]{1,0:T(8,128)(2,1)S(1)}, bf16[1536,128]{1,0:T(8,128)(2,1)S(1)}, u32[]{:S(2)}, u32[]{:S(2)}) collective-permute-start(bf16[1536,128]{1,0:T(8,128)(2,1)S(1)} %get-tuple-element.55), channel_id=1, source_target_pairs={{0,8},{1,3},{2,10},{3,5},{4,12},{5,7},{6,14},{7,1},{8,16},{9,11},{... | collective-permute-start | bytes 1179656 | tf_op jit(solution)/shard_map/ppermute | solution.py:67
  28.6 2.9 %collective-permute-start.8 = (bf16[1536,128]{1,0:T(8,128)(2,1)S(1)}, bf16[1536,128]{1,0:T(8,128)(2,1)S(1)}, u32[]{:S(2)}, u32[]{:S(2)}) collective-permute-start(bf16[1536,128]{1,0:T(8,128)(2,1)S(1)} %get-tuple-element.55), channel_id=1, source_target_pairs={{0,16},{1,5},{2,18},{3,7},{4,20},{5,1},{6,22},{7,3},{8,24},{9,13},... | collective-permute-start | bytes 1179656 | tf_op jit(solution)/shard_map/ppermute | solution.py:67
  32.6 3.2 %collective-permute-done.7.r1 = bf16[1536,128]{1,0:T(8,128)(2,1)S(1)} collective-permute-done((bf16[1536,128]{1,0:T(8,128)(2,1)S(1)}, bf16[1536,128]{1,0:T(8,128)(2,1)S(1)}, u32[]{:S(2)}, u32[]{:S(2)}) %collective-permute-start.7) | collective-permute-done | bytes 393248 | tf_op jit(solution)/shard_map/ppermute | solution.py:67
  35.9 5.4 %collective-permute-done.8.r2 = bf16[1536,128]{1,0:T(8,128)(2,1)S(1)} collective-permute-done((bf16[1536,128]{1,0:T(8,128)(2,1)S(1)}, bf16[1536,128]{1,0:T(8,128)(2,1)S(1)}, u32[]{:S(2)}, u32[]{:S(2)}) %collective-permute-start.8) | collective-permute-done | bytes 393248 | tf_op jit(solution)/shard_map/ppermute | solution.py:67
  42.3 2.2 %collective-permute-start.11 = (bf16[1296,128]{1,0:T(8,128)(2,1)S(1)}, bf16[1296,128]{1,0:T(8,128)(2,1)S(1)}, u32[]{:S(2)}, u32[]{:S(2)}) collective-permute-start(bf16[1296,128]{1,0:T(8,128)(2,1)S(1)} %get-tuple-element.61.refs_0_), channel_id=1, source_target_pairs={{0,6},{1,25},{2,0},{3,27},{4,2},{5,29},{6,4},{7,31},{8,14},{9,1},{... | collective-permute-start | bytes 995336 | tf_op jit(solution)/shard_map/ppermute | solution.py:67
  45.6 3.4 %collective-permute-start.10 = (bf16[1296,128]{1,0:T(8,128)(2,1)S(1)}, bf16[1296,128]{1,0:T(8,128)(2,1)S(1)}, u32[]{:S(2)}, u32[]{:S(2)}) collective-permute-start(bf16[1296,128]{1,0:T(8,128)(2,1)S(1)} %get-tuple-element.61.refs_0_), channel_id=1, source_target_pairs={{0,1},{1,0},{2,3},{3,2},{4,5},{5,4},{6,7},{7,6},{8,9},{9,8},{10,11... | collective-permute-start | bytes 995336 | tf_op jit(solution)/shard_map/ppermute | solution.py:340
  49.0 3.1 %collective-permute-done.11.refs_1_ = bf16[1296,128]{1,0:T(8,128)(2,1)S(1)} collective-permute-done((bf16[1296,128]{1,0:T(8,128)(2,1)S(1)}, bf16[1296,128]{1,0:T(8,128)(2,1)S(1)}, u32[]{:S(2)}, u32[]{:S(2)}) %collective-permute-start.11) | collective-permute-done | bytes 331808 | tf_op jit(solution)/shard_map/ppermute | solution.py:67
  52.0 3.1 %collective-permute-start.12 = (bf16[1296,128]{1,0:T(8,128)(2,1)S(1)}, bf16[1296,128]{1,0:T(8,128)(2,1)S(1)}, u32[]{:S(2)}, u32[]{:S(2)}) collective-permute-start(bf16[1296,128]{1,0:T(8,128)(2,1)S(1)} %collective-permute-done.11.refs_1_), channel_id=1, source_target_pairs={{0,1},{1,0},{2,3},{3,2},{4,5},{5,4},{6,7},{7,6},{8,9},{9,8},{10,11... | collective-permute-start | bytes 995336 | tf_op jit(solution)/shard_map/ppermute | solution.py:340
  55.7 3.3 %collective-permute-start.16 = (bf16[1296,128]{1,0:T(8,128)(2,1)S(1)}, bf16[1296,128]{1,0:T(8,128)(2,1)S(1)}, u32[]{:S(2)}, u32[]{:S(2)}) collective-permute-start(bf16[1296,128]{1,0:T(8,128)(2,1)S(1)} %collective-permute-done.15.refs_3_), channel_id=1, source_target_pairs={{0,1},{1,0},{2,3},{3,2},{4,5},{5,4},{6,7},{7,6},{8,9},{9,8},{10,11... | collective-permute-start | bytes 995336 | tf_op jit(solution)/shard_map/ppermute | solution.py:340
  59.1 1.3 %shard_map.119 = (f32[9,128,128]{2,1,0:T(8,128)S(1)}, f32[272,128]{1,0:T(8,128)S(1)}) custom-call(s32[1,512]{1,0:T(1,128)S(1)} %get-tuple-element.57.tab, bf16[128,128,128]{2,1,0:T(8,128)(2,1)S(1)} %bitcast.6, bf16[1296,128]{1,0:T(8,128)(2,1)S(1)} %get-tuple-element.61.refs_0_, bf16[1296,128]{1,0:T(8,128)(2,1)S(1)} %collective-permute-done.11.refs_1_, ...), custom_call_target="tpu_custom_call" | custom-call | flops 268435456 | bytes 4194304 | tf_op jit(solution)/shard_map/pallas_call | solution.py:343
  60.4 1.4 %shard_map.120 = (bf16[528,128]{1,0:T(8,128)(2,1)S(1)}, bf16[528,128]{1,0:T(8,128)(2,1)S(1)}, bf16[528,128]{1,0:T(8,128)(2,1)S(1)}, bf16[32,128,128]{2,1,0:T(8,128)(2,1)S(1)}, f32[272,128]{1,0:T(8,128)S(1)}) custom-call(s32[1,512]{1,0:T(1,128)S(1)} %get-tuple-element.57.tab, bf16[128,128,128]{2,1,0:T(8,128)(2,1)S(1)} %bitcast.7, ...), custom_call_target="tpu_custom_call" | custom-call | flops 201326592 | bytes 3145728 | tf_op jit(solution)/shard_map/pallas_call | solution.py:350
  61.8 1.5 %collective-permute-start.17 = (bf16[528,128]{1,0:T(8,128)(2,1)S(1)}, bf16[528,128]{1,0:T(8,128)(2,1)S(1)}, u32[]{:S(2)}, u32[]{:S(2)}) collective-permute-start(bf16[528,128]{1,0:T(8,128)(2,1)S(1)} %get-tuple-element.66), channel_id=1, source_target_pairs={{0,64},{32,96},{64,0},{96,32},{1,65},{33,97},{65,1},{97,33},{2,66}... | collective-permute-start | bytes 405512 | tf_op jit(solution)/shard_map/ppermute | solution.py:364
  63.3 2.0 %collective-permute-start.18 = (bf16[528,128]{1,0:T(8,128)(2,1)S(1)}, bf16[528,128]{1,0:T(8,128)(2,1)S(1)}, u32[]{:S(2)}, u32[]{:S(2)}) collective-permute-start(bf16[528,128]{1,0:T(8,128)(2,1)S(1)} %get-tuple-element.67), channel_id=1, source_target_pairs={{0,32},{32,64},{64,96},{96,0},{1,33},{33,65},{65,97},{97,1},{2,34}... | collective-permute-start | bytes 405512 | tf_op jit(solution)/shard_map/ppermute | solution.py:364
  67.2 1.1 %collective-permute-done.17.r1 = bf16[528,128]{1,0:T(8,128)(2,1)S(1)} collective-permute-done((bf16[528,128]{1,0:T(8,128)(2,1)S(1)}, bf16[528,128]{1,0:T(8,128)(2,1)S(1)}, u32[]{:S(2)}, u32[]{:S(2)}) %collective-permute-start.17) | collective-permute-done | bytes 135200 | tf_op jit(solution)/shard_map/ppermute | solution.py:364
  68.3 3.5 %collective-permute-done.18.r2 = bf16[528,128]{1,0:T(8,128)(2,1)S(1)} collective-permute-done((bf16[528,128]{1,0:T(8,128)(2,1)S(1)}, bf16[528,128]{1,0:T(8,128)(2,1)S(1)}, u32[]{:S(2)}, u32[]{:S(2)}) %collective-permute-start.18) | collective-permute-done | bytes 135200 | tf_op jit(solution)/shard_map/ppermute | solution.py:364
  (44 shorter events, 12.0 us)
Async XLA Ops:
  0.7 9.3 %collective-permute-start = (bf16[256,128]{1,0:T(8,128)(2,1)}, bf16[256,128]{1,0:T(8,128)(2,1)S(1)}, u32[]{:S(2)}, u32[]{:S(2)}) collective-permute-start(bf16[256,128]{1,0:T(8,128)(2,1)} %x.1), channel_id=1, source_target_pairs={{0,96},{32,0},{64,32},{96,64},{1,97},{33,1},{65,33},{97,65},{2,98}... | collective-permute-start | bytes 196616 | tf_op jit(solution)/shard_map/ppermute | solution.py:67
  4.0 5.9 %collective-permute-start.1 = (bf16[256,128]{1,0:T(8,128)(2,1)}, bf16[256,128]{1,0:T(8,128)(2,1)S(1)}, u32[]{:S(2)}, u32[]{:S(2)}) collective-permute-start(bf16[256,128]{1,0:T(8,128)(2,1)} %x.1), channel_id=1, source_target_pairs={{0,64},{32,96},{64,0},{96,32},{1,65},{33,97},{65,1},{97,33},{2,66}... | collective-permute-start | bytes 196616 | tf_op jit(solution)/shard_map/ppermute | solution.py:67
  4.5 5.4 %collective-permute-start.2 = (bf16[256,128]{1,0:T(8,128)(2,1)}, bf16[256,128]{1,0:T(8,128)(2,1)S(1)}, u32[]{:S(2)}, u32[]{:S(2)}) collective-permute-start(bf16[256,128]{1,0:T(8,128)(2,1)} %x.1), channel_id=1, source_target_pairs={{0,32},{32,64},{64,96},{96,0},{1,33},{33,65},{65,97},{97,1},{2,34}... | collective-permute-start | bytes 196616 | tf_op jit(solution)/shard_map/ppermute | solution.py:67
  11.6 15.9 %copy-start.2 = (bf16[256,256]{1,0:T(8,128)(2,1)S(1)}, bf16[256,256]{1,0:T(8,128)(2,1)}, u32[]{:S(2)}) copy-start(bf16[256,256]{1,0:T(8,128)(2,1)} %cot.3) | copy-start | bytes 393220
  11.6 29.7 %copy-start.4 = (bf16[128,256]{1,0:T(8,128)(2,1)S(1)}, bf16[128,256]{1,0:T(8,128)(2,1)}, u32[]{:S(2)}) copy-start(bf16[128,256]{1,0:T(8,128)(2,1)} %weight.1) | copy-start | bytes 196612
  11.6 29.7 %copy-start.5 = (f32[256]{0:T(256)S(1)}, f32[256]{0:T(256)}, u32[]{:S(2)}) copy-start(f32[256]{0:T(256)} %param.10) | copy-start | bytes 3076
  11.6 4.4 %collective-permute-start.3 = (bf16[4096,128]{1,0:T(8,128)(2,1)S(1)}, bf16[4096,128]{1,0:T(8,128)(2,1)S(1)}, u32[]{:S(2)}, u32[]{:S(2)}) collective-permute-start(bf16[4096,128]{1,0:T(8,128)(2,1)S(1)} %shard_map.115), channel_id=1, source_target_pairs={{0,1},{1,0},{2,3},{3,2},{4,5},{5,4},{6,7},{7,6},{8,9},{9,8},{10,11... | collective-permute-start | bytes 3145736 | tf_op jit(solution)/shard_map/ppermute | solution.py:322
  15.1 44.0 %copy-start.1 = (bf16[1,1,128,128,128]{4,3,2,1,0:T(8,128)(2,1)S(1)}, bf16[1,1,128,128,128]{4,3,2,1,0:T(8,128)(2,1)}, u32[]{:S(2)}) copy-start(bf16[1,1,128,128,128]{4,3,2,1,0:T(8,128)(2,1)} %param.11) | copy-start | bytes 12582916
  16.3 7.2 %collective-permute-start.4 = (bf16[1024,128]{1,0:T(8,128)(2,1)S(1)}, bf16[1024,128]{1,0:T(8,128)(2,1)S(1)}, u32[]{:S(2)}, u32[]{:S(2)}) collective-permute-start(bf16[1024,128]{1,0:T(8,128)(2,1)S(1)} %get-tuple-element.48), channel_id=1, source_target_pairs={{0,2},{1,9},{2,4},{3,11},{4,6},{5,13},{6,0},{7,15},{8,10},{9,17},{... | collective-permute-start | bytes 786440 | tf_op jit(solution)/shard_map/ppermute | solution.py:67
  17.9 9.5 %collective-permute-start.5 = (bf16[1024,128]{1,0:T(8,128)(2,1)S(1)}, bf16[1024,128]{1,0:T(8,128)(2,1)S(1)}, u32[]{:S(2)}, u32[]{:S(2)}) collective-permute-start(bf16[1024,128]{1,0:T(8,128)(2,1)S(1)} %get-tuple-element.49), channel_id=1, source_target_pairs={{0,4},{1,17},{2,6},{3,19},{4,0},{5,21},{6,2},{7,23},{8,12},{9,25},... | collective-permute-start | bytes 786440 | tf_op jit(solution)/shard_map/ppermute | solution.py:67
  20.6 6.9 %collective-permute-start.6 = (bf16[1024,128]{1,0:T(8,128)(2,1)S(1)}, bf16[1024,128]{1,0:T(8,128)(2,1)S(1)}, u32[]{:S(2)}, u32[]{:S(2)}) collective-permute-start(bf16[1024,128]{1,0:T(8,128)(2,1)S(1)} %get-tuple-element.50), channel_id=1, source_target_pairs={{0,6},{1,25},{2,0},{3,27},{4,2},{5,29},{6,4},{7,31},{8,14},{9,1},{... | collective-permute-start | bytes 786440 | tf_op jit(solution)/shard_map/ppermute | solution.py:67
  27.6 8.3 %collective-permute-start.7 = (bf16[1536,128]{1,0:T(8,128)(2,1)S(1)}, bf16[1536,128]{1,0:T(8,128)(2,1)S(1)}, u32[]{:S(2)}, u32[]{:S(2)}) collective-permute-start(bf16[1536,128]{1,0:T(8,128)(2,1)S(1)} %get-tuple-element.55), channel_id=1, source_target_pairs={{0,8},{1,3},{2,10},{3,5},{4,12},{5,7},{6,14},{7,1},{8,16},{9,11},{... | collective-permute-start | bytes 1179656 | tf_op jit(solution)/shard_map/ppermute | solution.py:67
  28.6 12.6 %collective-permute-start.8 = (bf16[1536,128]{1,0:T(8,128)(2,1)S(1)}, bf16[1536,128]{1,0:T(8,128)(2,1)S(1)}, u32[]{:S(2)}, u32[]{:S(2)}) collective-permute-start(bf16[1536,128]{1,0:T(8,128)(2,1)S(1)} %get-tuple-element.55), channel_id=1, source_target_pairs={{0,16},{1,5},{2,18},{3,7},{4,20},{5,1},{6,22},{7,3},{8,24},{9,13},... | collective-permute-start | bytes 1179656 | tf_op jit(solution)/shard_map/ppermute | solution.py:67
  31.6 9.7 %collective-permute-start.9 = (bf16[1536,128]{1,0:T(8,128)(2,1)S(1)}, bf16[1536,128]{1,0:T(8,128)(2,1)S(1)}, u32[]{:S(2)}, u32[]{:S(2)}) collective-permute-start(bf16[1536,128]{1,0:T(8,128)(2,1)S(1)} %get-tuple-element.55), channel_id=1, source_target_pairs={{0,24},{1,7},{2,26},{3,1},{4,28},{5,3},{6,30},{7,5},{8,0},{9,15},{... | collective-permute-start | bytes 1179656 | tf_op jit(solution)/shard_map/ppermute | solution.py:67
  42.3 9.8 %collective-permute-start.11 = (bf16[1296,128]{1,0:T(8,128)(2,1)S(1)}, bf16[1296,128]{1,0:T(8,128)(2,1)S(1)}, u32[]{:S(2)}, u32[]{:S(2)}) collective-permute-start(bf16[1296,128]{1,0:T(8,128)(2,1)S(1)} %get-tuple-element.61.refs_0_), channel_id=1, source_target_pairs={{0,6},{1,25},{2,0},{3,27},{4,2},{5,29},{6,4},{7,31},{8,14},{9,1},{... | collective-permute-start | bytes 995336 | tf_op jit(solution)/shard_map/ppermute | solution.py:67
  44.4 10.7 %collective-permute-start.13 = (bf16[1296,128]{1,0:T(8,128)(2,1)S(1)}, bf16[1296,128]{1,0:T(8,128)(2,1)S(1)}, u32[]{:S(2)}, u32[]{:S(2)}) collective-permute-start(bf16[1296,128]{1,0:T(8,128)(2,1)S(1)} %get-tuple-element.61.refs_0_), channel_id=1, source_target_pairs={{0,4},{1,17},{2,6},{3,19},{4,0},{5,21},{6,2},{7,23},{8,12},{9,25},... | collective-permute-start | bytes 995336 | tf_op jit(solution)/shard_map/ppermute | solution.py:67
  45.3 10.5 %collective-permute-start.15 = (bf16[1296,128]{1,0:T(8,128)(2,1)S(1)}, bf16[1296,128]{1,0:T(8,128)(2,1)S(1)}, u32[]{:S(2)}, u32[]{:S(2)}) collective-permute-start(bf16[1296,128]{1,0:T(8,128)(2,1)S(1)} %get-tuple-element.61.refs_0_), channel_id=1, source_target_pairs={{0,2},{1,9},{2,4},{3,11},{4,6},{5,13},{6,0},{7,15},{8,10},{9,17},{... | collective-permute-start | bytes 995336 | tf_op jit(solution)/shard_map/ppermute | solution.py:67
  45.6 14.8 %collective-permute-start.10 = (bf16[1296,128]{1,0:T(8,128)(2,1)S(1)}, bf16[1296,128]{1,0:T(8,128)(2,1)S(1)}, u32[]{:S(2)}, u32[]{:S(2)}) collective-permute-start(bf16[1296,128]{1,0:T(8,128)(2,1)S(1)} %get-tuple-element.61.refs_0_), channel_id=1, source_target_pairs={{0,1},{1,0},{2,3},{3,2},{4,5},{5,4},{6,7},{7,6},{8,9},{9,8},{10,11... | collective-permute-start | bytes 995336 | tf_op jit(solution)/shard_map/ppermute | solution.py:340
  52.0 8.4 %collective-permute-start.12 = (bf16[1296,128]{1,0:T(8,128)(2,1)S(1)}, bf16[1296,128]{1,0:T(8,128)(2,1)S(1)}, u32[]{:S(2)}, u32[]{:S(2)}) collective-permute-start(bf16[1296,128]{1,0:T(8,128)(2,1)S(1)} %collective-permute-done.11.refs_1_), channel_id=1, source_target_pairs={{0,1},{1,0},{2,3},{3,2},{4,5},{5,4},{6,7},{7,6},{8,9},{9,8},{10,11... | collective-permute-start | bytes 995336 | tf_op jit(solution)/shard_map/ppermute | solution.py:340
  55.1 5.3 %collective-permute-start.14 = (bf16[1296,128]{1,0:T(8,128)(2,1)S(1)}, bf16[1296,128]{1,0:T(8,128)(2,1)S(1)}, u32[]{:S(2)}, u32[]{:S(2)}) collective-permute-start(bf16[1296,128]{1,0:T(8,128)(2,1)S(1)} %collective-permute-done.13.refs_2_), channel_id=1, source_target_pairs={{0,1},{1,0},{2,3},{3,2},{4,5},{5,4},{6,7},{7,6},{8,9},{9,8},{10,11... | collective-permute-start | bytes 995336 | tf_op jit(solution)/shard_map/ppermute | solution.py:340
  55.7 4.7 %collective-permute-start.16 = (bf16[1296,128]{1,0:T(8,128)(2,1)S(1)}, bf16[1296,128]{1,0:T(8,128)(2,1)S(1)}, u32[]{:S(2)}, u32[]{:S(2)}) collective-permute-start(bf16[1296,128]{1,0:T(8,128)(2,1)S(1)} %collective-permute-done.15.refs_3_), channel_id=1, source_target_pairs={{0,1},{1,0},{2,3},{3,2},{4,5},{5,4},{6,7},{7,6},{8,9},{9,8},{10,11... | collective-permute-start | bytes 995336 | tf_op jit(solution)/shard_map/ppermute | solution.py:340
  61.8 6.4 %collective-permute-start.17 = (bf16[528,128]{1,0:T(8,128)(2,1)S(1)}, bf16[528,128]{1,0:T(8,128)(2,1)S(1)}, u32[]{:S(2)}, u32[]{:S(2)}) collective-permute-start(bf16[528,128]{1,0:T(8,128)(2,1)S(1)} %get-tuple-element.66), channel_id=1, source_target_pairs={{0,64},{32,96},{64,0},{96,32},{1,65},{33,97},{65,1},{97,33},{2,66}... | collective-permute-start | bytes 405512 | tf_op jit(solution)/shard_map/ppermute | solution.py:364
  63.3 8.5 %collective-permute-start.18 = (bf16[528,128]{1,0:T(8,128)(2,1)S(1)}, bf16[528,128]{1,0:T(8,128)(2,1)S(1)}, u32[]{:S(2)}, u32[]{:S(2)}) collective-permute-start(bf16[528,128]{1,0:T(8,128)(2,1)S(1)} %get-tuple-element.67), channel_id=1, source_target_pairs={{0,32},{32,64},{64,96},{96,0},{1,33},{33,65},{65,97},{97,1},{2,34}... | collective-permute-start | bytes 405512 | tf_op jit(solution)/shard_map/ppermute | solution.py:364
  65.3 6.9 %collective-permute-start.19 = (bf16[528,128]{1,0:T(8,128)(2,1)S(1)}, bf16[528,128]{1,0:T(8,128)(2,1)S(1)}, u32[]{:S(2)}, u32[]{:S(2)}) collective-permute-start(bf16[528,128]{1,0:T(8,128)(2,1)S(1)} %get-tuple-element.68), channel_id=1, source_target_pairs={{0,96},{32,0},{64,32},{96,64},{1,97},{33,1},{65,33},{97,65},{2,98}... | collective-permute-start | bytes 405512 | tf_op jit(solution)/shard_map/ppermute | solution.py:364
  (4 other events, 20.1 us)

commit v3 on v2

--- a/solution.py
+++ b/solution.py
@@ -15,10 +15,9 @@
 ANY = pl.BlockSpec(memory_space=pl.ANY)
 TAIL = 272
 UNROLL = 16
-LEAD = 2**24
 WIDTH = 144
 TAB = 384
-BACKWARD_TAB = 512
+BACKWARD_TAB = 640
 
 
 def at(y, z, core):
@@ -44,14 +43,15 @@
     return [(r, (r + d) % 4) for r in range(4)]
 
 
-def call(kernel, outs, ins, scratch=(), tiles=0, nbytes=0):
+def call(kernel, outs, ins, scratch=(), tiles=0, nbytes=0, aliases=None, limit=24):
     return pl.pallas_call(
         kernel,
         out_shape=outs,
         in_specs=ins,
         out_specs=jax.tree.map(lambda _: VMEM, outs),
         scratch_shapes=list(scratch),
-        compiler_params=pltpu.CompilerParams(vmem_limit_bytes=24 * 2**20),
+        input_output_aliases=aliases or {},
+        compiler_params=pltpu.CompilerParams(vmem_limit_bytes=limit * 2**20),
         cost_estimate=pl.CostEstimate(
             flops=2 * tiles * B**3, bytes_accessed=nbytes + tiles * 2**16, transcendentals=0
         ),
@@ -64,18 +64,13 @@
 
 def permute(arrays, axis, pairs):
     arrays = lax.optimization_barrier(tuple(arrays))
-    return [lax.ppermute(a, axis, p) for a, p in zip(arrays, pairs)]
-
-
-ORDER = (2, 1, 3)
-
-
-def live_slots(count, live):
-    slot = lax.broadcasted_iota(jnp.int32, (1, 128), 1)
-    live[...] = (slot < count[0, 0]).astype(jnp.int32)
-
-
-def sort_tiles(rows, cols, live, forward_tab, backward_tab):
+    return lax.optimization_barrier([lax.ppermute(a, axis, p) for a, p in zip(arrays, pairs)])
+
+
+ORDER = (1, 3, 2)
+
+
+def sort_tiles(rows, cols, count, forward_tab, backward_tab):
     r, c = lax.axis_index("row"), lax.axis_index("col")
     core, z, y = c % 2, (c // 2) % 4, c // 8
     rows, cols = rows[...], cols[...]
@@ -90,7 +85,7 @@
     slot = lax.broadcasted_iota(jnp.int32, (1, 128), 1)
 
     def table(key, keys, take, to, pad, width):
-        key = jnp.where(live[...] == 1, key, keys)
+        key = jnp.where(slot < count[0, 0], key, keys)
         is_key = [jnp.where(key == k, 1.0, 0.0) for k in range(keys)]
         is_key = jnp.concatenate(is_key + [jnp.zeros((8 - keys, 128), F32)]).astype(BF16)
         low = lax.broadcasted_iota(jnp.int32, (128, 128), 0)
@@ -115,18 +110,30 @@
         return entry
 
     forward_tab[...] = table(1 - half, 2, ahead * 2 + cols % 2, pos, 32, TAB)
-    key = jnp.where(half == 0, 0, jnp.where(ahead == 0, 2, 1))
-    backward_tab[...] = table(key, 3, pos, ahead * 2 + cols % 2, 8, BACKWARD_TAB)
-
-
-def hold(x, adj, x_held, tiles):
-    x_held[...] = x[...]
-
-    def copy(i, _):
-        tiles[i] = adj[i]
+    late = (first == 1).astype(jnp.int32)
+    key = jnp.where(half + late < 2, half + late, jnp.where(ahead == 0, 3, 2))
+    take = half * 32 + pos
+    backward_tab[...] = table(key, 4, take, ahead * 2 + cols % 2, 8, BACKWARD_TAB)
+
+
+def hold(adj, tiles, acc0, acc1, sem):
+    n = sem.shape[0]
+    parts = [pl.ds(k * (128 // n), 128 // n) for k in range(n)]
+    copies = [
+        pltpu.make_async_copy(adj.at[part], tiles.at[part], sem.at[k])
+        for k, part in enumerate(parts)
+    ]
+    for copy in copies:
+        copy.start()
+
+    def block(i, _):
+        acc0[i] = jnp.zeros((B, B), F32)
+        acc1[i] = jnp.zeros((B, B), F32)
         return 0
 
-    lax.fori_loop(0, 128, copy, 0, unroll=8)
+    lax.fori_loop(0, 32, block, 0, unroll=4)
+    for copy in copies:
+        copy.wait()
 
 
 def each_tile(tab, key, keys, adj, product, acc):
@@ -148,23 +155,24 @@
             to[k * (rows // B) + i] = ref[i * B : (i + 1) * B]
 
 
-def forward_tiles(key, tab, x0, x1, x2, x3, adj, out, *scratch):
-    acc, xs = scratch if key == 0 else (out, scratch[0])
-    load_blocks([x0, x1, x2, x3], 256, xs)
-
-    def clear(i, _):
-        acc[i] = jnp.zeros((B, B), F32)
-        return 0
-
-    lax.fori_loop(0, 32, clear, 0)
+def forward_tiles(key, tab, x0, x1, x2, x3, adj, _, acc, *refs):
+    *out, xs, sem = refs
+    copies = [
+        pltpu.make_async_copy(x0.at[pl.ds(k * B, B)], xs.at[k], sem.at[k]) for k in range(2)
+    ]
+    for copy in copies:
+        copy.start()
+    load_blocks([x1, x2, x3], 256, xs.at[pl.ds(2, 6)])
+    for copy in copies:
+        copy.wait()
     each_tile(tab, key, 2, adj, lambda t, i: jnp.dot(t, xs[i], preferred_element_type=F32), acc)
     if key == 0:
 
         def store(i, _):
-            out[pl.ds(pl.multiple_of(i * B, B), B)] = acc[i].astype(BF16)
+            out[0][pl.ds(pl.multiple_of(i * B, B), B)] = acc[i].astype(BF16)
             return 0
 
-        lax.fori_loop(0, 32, store, 0)
+        lax.fori_loop(0, 32, store, 0, unroll=4)
 
 
 def core_sum(acc, got, m0, m1, m2, m3):
@@ -249,34 +257,36 @@
     return wg, bg
 
 
-def backward_tiles(key, tab, adj, *refs):
+def backward_tiles(key, places, tab, adj, *refs):
     def product(t, i):
         return jnp.dot(gs[i], t, preferred_element_type=F32)
 
-    if key == 0:
-        pieces, (acc, tail, gs) = refs[:4], refs[4:]
-        load_blocks(pieces, 1024, gs)
-        acc[...] = jnp.zeros((9, B, B), F32)
-        each_tile(tab, 0, 3, adj, product, acc)
-        put_tail(tail, 0, *sum_tails(pieces))
+    pieces, refs, gs = refs[: len(places)], refs[len(places) : -1], refs[-1]
+    for place, piece in zip(places, pieces):
+        load_blocks([piece], 1024, gs.at[pl.ds(place * 8, 8)])
+    if key < 2:
+        if key == 0:
+            acc, tail = refs
+            acc[...] = jnp.zeros((9, B, B), F32)
+        else:
+            _, tail_in, acc, tail = refs
+        each_tile(tab, key, 4, adj, product, acc)
+        wg, bg = sum_tails(pieces)
+        if key == 1:
+            wg, bg = wg + tail_in[0:256], bg + tail_in[256:258]
+        put_tail(tail, 0, wg, bg)
         return
-    if key == 1:
-        pieces, (acc_in, tail_in, m1, m2, m3, gs, tail, acc) = refs[:4], refs[4:]
-        outs = (m1, m2, m3)
-        load_blocks(pieces, 1024, gs)
-        wg, bg = sum_tails(pieces)
-        put_tail(tail, 0, tail_in[0:256] + wg, tail_in[256:258] + bg)
-    else:
-        gs, acc_in, tail, m0, acc = refs
-        outs = (m0,)
-    first = 2 if key == 1 else 0
+    acc_in, tail_in, *outs, acc = refs
+    first = 2 if key == 2 else 0
     last = first + 2 * len(outs)
     acc[first:last] = acc_in[first:last]
-    each_tile(tab, key, 3, adj, product, acc)
+    each_tile(tab, key, 4, adj, product, acc)
+    wg, bg = sum_tails(pieces)
+    wg, bg = wg + tail_in[0:256], bg + tail_in[256:258]
     for k, m in enumerate(outs):
         m[0:B] = acc[first + 2 * k].astype(m.dtype)
         m[B : 2 * B] = acc[first + 2 * k + 1].astype(m.dtype)
-        put_tail(m, 256, tail[0:256], tail[256:258])
+        put_tail(m, 256, wg, bg)
 
 
 def last_sum(m0, r1, r2, r3, feat, wgrad, bgrad):
@@ -300,66 +310,69 @@
     features, weight, bias_vector, adjacency, tile_rows, tile_cols, tile_count, cotangent
 ):
     adj = adjacency[0, 0]
-    x2, x1, x3 = permute([features] * 3, "row", [row_shift(d) for d in ORDER])
-    live = call(live_slots, sds(1, 128, jnp.int32), [SMEM], nbytes=LEAD)(tile_count)
+    x1, x3, x2 = permute([features] * 3, "row", [row_shift(d) for d in ORDER])
     forward_tab, backward_tab = call(
         sort_tiles,
         (sds(1, TAB, jnp.int32), sds(1, BACKWARD_TAB, jnp.int32)),
-        [VMEM] * 3,
-    )(tile_rows[0], tile_cols[0], live)
-    x0, tiles = call(
-        hold, (sds(256), jax.ShapeDtypeStruct((128, B, B), BF16)), [VMEM, VMEM]
-    )(features, adj)
-    xs = (x0, x3, x2, x1)
+        [VMEM, VMEM, SMEM],
+    )(tile_rows[0], tile_cols[0], tile_count)
     half = jax.ShapeDtypeStruct((33, B, B), F32)
-    other = call(
+    tiles, acc0, acc1 = call(
+        hold,
+        (jax.ShapeDtypeStruct((128, B, B), BF16), half, half),
+        [ANY],
+        [pltpu.SemaphoreType.DMA((8,))],
+        limit=43,
+    )(adj)
+    xs = (features, x3, x2, x1)
+    scratch = [pltpu.VMEM((8, B, B), BF16), pltpu.SemaphoreType.DMA((2,))]
+    _, other = call(
         functools.partial(forward_tiles, 0),
-        sds(4096),
-        [SMEM] + [VMEM] * 5,
-        [pltpu.VMEM((33, B, B), F32), pltpu.VMEM((8, B, B), BF16)],
+        (half, sds(4096)),
+        [SMEM, ANY] + [VMEM] * 5,
+        scratch,
         tiles=64,
-    )(forward_tab, *xs, tiles)
+        aliases={6: 0},
+    )(forward_tab, *xs, tiles, acc0)
     got = lax.ppermute(other, "col", core_swap())
     acc = call(
         functools.partial(forward_tiles, 1),
         half,
-        [SMEM] + [VMEM] * 5,
-        [pltpu.VMEM((8, B, B), BF16)],
-    )(forward_tab, *xs, tiles)
+        [SMEM, ANY] + [VMEM] * 5,
+        scratch,
+        aliases={6: 0},
+    )(forward_tab, *xs, tiles, acc1)
     ms = call(core_sum, (sds(1024, dtype=F32),) + (sds(1024),) * 3, [VMEM] * 2)(acc, got)
-    r2, r1, r3 = permute([ms[d] for d in ORDER], "col", [col_shift(True, d) for d in ORDER])
+    r1, r3, r2 = permute([ms[d] for d in ORDER], "col", [col_shift(True, d) for d in ORDER])
     total, msg = call(first_sum, (sds(1024, dtype=F32), sds(1536)), [VMEM] * 5)(
         ms[0], r1, r2, r3, cotangent
     )
-    r2, r1, r3 = permute([msg] * 3, "col", [col_shift(False, d) for d in ORDER])
+    r1, r3, r2 = permute([msg] * 3, "col", [col_shift(False, d) for d in ORDER])
     act, msg = call(local, (sds(256, 256), sds(1024 + TAIL)), [VMEM] * 7)(
         total, r1, r2, r3, weight, bias_vector.reshape(1, 256), cotangent
     )
-    r2, r1, r3 = permute([msg] * 3, "col", [col_shift(True, d) for d in ORDER])
+    r1, r3, r2 = permute([msg] * 3, "col", [col_shift(True, d) for d in ORDER])
     mine = (msg, r3, r2, r1)
     theirs = [lax.ppermute(m, "col", core_swap()) for m in mine]
     out, tail = sds(256 + TAIL), sds(TAIL, dtype=F32)
-    sums, blocks = (jax.ShapeDtypeStruct(s, t) for s, t in (((9, B, B), F32), ((32, B, B), BF16)))
-    sums, tail = call(
-        functools.partial(backward_tiles, 0),
-        (sums, tail),
-        [SMEM] + [VMEM] * 5,
-        [pltpu.VMEM((32, B, B), BF16)],
-        tiles=64,
-    )(backward_tab, adj, *mine)
-    *ms, blocks, tail = call(
-        functools.partial(backward_tiles, 1),
-        (out, out, out, blocks, sds(TAIL, dtype=F32)),
-        [SMEM] + [VMEM] * 7,
-        [pltpu.VMEM((9, B, B), F32)],
-        tiles=48,
-    )(backward_tab, adj, *theirs, sums, tail)
-    m = call(
-        functools.partial(backward_tiles, 2),
-        sds(256 + TAIL, dtype=F32),
-        [SMEM] + [VMEM] * 4,
-        [pltpu.VMEM((9, B, B), F32)],
-    )(backward_tab, adj, blocks, sums, tail)
+    sums = jax.ShapeDtypeStruct((9, B, B), F32)
+    blocks, acc = pltpu.VMEM((64, B, B), BF16), pltpu.VMEM((9, B, B), F32)
+
+    def backward(key, places, outs, scratch, tiles, aliases, *extra):
+        pieces = [(mine + tuple(theirs))[p] for p in places]
+        return call(
+            functools.partial(backward_tiles, key, places),
+            outs,
+            [SMEM] + [VMEM] * (1 + len(places) + len(extra)),
+            scratch,
+            tiles=tiles,
+            aliases=aliases,
+        )(backward_tab, adj, *pieces, *extra)
+
+    state = backward(0, (0, 2, 3), (sums, tail), [blocks], 48, None)
+    state = backward(1, (1, 4, 6, 7), (sums, tail), [blocks], 64, {6: 0}, *state)
+    ms = backward(2, (5,), (out,) * 3, [acc, blocks], 16, None, *state)
+    (m,) = backward(3, (5,), (sds(256 + TAIL, dtype=F32),), [acc, blocks], 0, None, *state)
     ms = [ms[d - 1] for d in ORDER]
     rs = [lax.ppermute(a, "row", row_shift(d)) for a, d in zip(ms, ORDER)]
     feat, wgrad, bgrad = call(

time: 73.2 us -> 71.6 us (0.978)
  starting transfers between devices: 34.8 us -> 28.7 us
  Pallas kernels: 9.76 us -> 13.6 us
  waiting for transfers between devices: 23.9 us -> 27.3 us
  local copies, waits for them, and re-layouts: 3.06 us -> 0.04 us
    ppermute x4, starting transfers between devices: 10.3 us -> 6.35 us  [on_device(): theirs = [lax.ppermute(m, 'col', core_swap()) for m in mine]]
    pallas_call x7, Pallas kernels: 6.88 us -> 10.8 us  [the longest x4 5.2 us: backward(): call(functools.partial(backward_tiles, key, places), outs, [SMEM] + [VMEM...]
    ppermute x12, waiting for transfers between devices: 17.9 us -> 21.4 us  [permute(): lax.ppermute(a, axis, p)]
    unnamed x16 -> x14, local copies, waits for them, and re-layouts: 3.06 us -> 0.04 us
    ppermute x3, starting transfers between devices: 4.47 us -> 2.74 us  [on_device(): rs = [lax.ppermute(a, 'row', row_shift(d)) for a, d in zip(ms, ORDER)]]
  transfers between devices with their start and end apart: 20 -> 20, of which waited for: 10 -> 13; matrix products, arithmetic and copies ran while one was open for 0% -> 0% of each run, Pallas kernels for 6% -> 12%
where the time goes in v3:
time: 71.6 us; the launch traced here: 71 us
  starting transfers between devices  28.7 us (40%)
  waiting for transfers between devices  27.3 us (38%)
  Pallas kernels  13.6 us (19%)
  between operations  1.5 us (2%)
    ppermute x12, waiting for transfers between devices, permute(): lax.ppermute(a, axis, p)  21.4 us
    ppermute x12, starting transfers between devices, permute(): lax.ppermute(a, axis, p)  17.9 us
    ppermute x4, starting transfers between devices, on_device(): theirs = [lax.ppermute(m, 'col', core_swap()) for m in mine]  6.35 us
    ppermute x3, waiting for transfers between devices, on_device(): rs = [lax.ppermute(a, 'row', row_shift(d)) for a, d in zip(ms, ORDER)]  5.22 us
    pallas_call x4, Pallas kernels, backward(): call(functools.partial(backward_tiles, key, places), outs, [SMEM] + [VMEM...  5.2 us
    ppermute x3, starting transfers between devices, on_device(): rs = [lax.ppermute(a, 'row', row_shift(d)) for a, d in zip(ms, ORDER)]  2.74 us
    pallas_call x1, Pallas kernels, on_device(): call(hold, (jax.ShapeDtypeStruct((128, B, B), BF16), half, half), [ANY],...  2.22 us
    pallas_call x1, Pallas kernels, on_device(): call(functools.partial(forward_tiles, 0), (half, sds(4096)), [SMEM, ANY]...  1.73 us
  transfers between devices with their start and end apart: 20, of which 13 were waited for; matrix products, arithmetic and copies ran while one was open for 0% of the time, Pallas kernels for 12%

profile of v3, /device:TPU:1, one launch (start us, length us, event | category | flops | bytes accessed | tf_op | source)
XLA Modules:
  0.0 71.0 jit_solution(16667277388409115500)
XLA Ops:
  0.7 2.1 %collective-permute-start = (bf16[256,128]{1,0:T(8,128)(2,1)}, bf16[256,128]{1,0:T(8,128)(2,1)S(1)}, u32[]{:S(2)}, u32[]{:S(2)}) collective-permute-start(bf16[256,128]{1,0:T(8,128)(2,1)} %x0.3), channel_id=1, source_target_pairs={{0,32},{32,64},{64,96},{96,0},{1,33},{33,65},{65,97},{97,1},{2,34}... | collective-permute-start | bytes 196616 | tf_op jit(solution)/shard_map/ppermute | solution.py:67
  4.1 1.6 %collective-permute-start.2 = (bf16[256,128]{1,0:T(8,128)(2,1)}, bf16[256,128]{1,0:T(8,128)(2,1)S(1)}, u32[]{:S(2)}, u32[]{:S(2)}) collective-permute-start(bf16[256,128]{1,0:T(8,128)(2,1)} %x0.3), channel_id=1, source_target_pairs={{0,64},{32,96},{64,0},{96,32},{1,65},{33,97},{65,1},{97,33},{2,66}... | collective-permute-start | bytes 196616 | tf_op jit(solution)/shard_map/ppermute | solution.py:67
  6.4 2.2 %shard_map.112 = (bf16[128,128,128]{2,1,0:T(8,128)(2,1)S(1)}, f32[33,128,128]{2,1,0:T(8,128)S(1)}, f32[33,128,128]{2,1,0:T(8,128)S(1)}) custom-call(bf16[128,128,128]{2,1,0:T(8,128)(2,1)} %bitcast.5), custom_call_target="tpu_custom_call" | custom-call | tf_op jit(solution)/shard_map/pallas_call | solution.py:320
  9.5 1.7 %shard_map.114 = (f32[33,128,128]{2,1,0:T(8,128)S(1)}, bf16[4096,128]{1,0:T(8,128)(2,1)S(1)}) custom-call(s32[1,384]{1,0:T(1,128)S(1)} %get-tuple-element.52.tab, bf16[256,128]{1,0:T(8,128)(2,1)S(1)} %copy-done.2, bf16[256,128]{1,0:T(8,128)(2,1)S(1)} %collective-permute-done.1.x1, ...), custom_call_target="tpu_custom_call", output_to_operand_aliasing={{0}: (6, {})} | custom-call | flops 268435456 | bytes 4194304 | tf_op jit(solution)/shard_map/pallas_call | solution.py:329
  11.2 1.7 %collective-permute-start.3 = (bf16[4096,128]{1,0:T(8,128)(2,1)S(1)}, bf16[4096,128]{1,0:T(8,128)(2,1)S(1)}, u32[]{:S(2)}, u32[]{:S(2)}) collective-permute-start(bf16[4096,128]{1,0:T(8,128)(2,1)S(1)} %get-tuple-element.62), channel_id=1, source_target_pairs={{0,1},{1,0},{2,3},{3,2},{4,5},{5,4},{6,7},{7,6},{8,9},{9,8},{10,11... | collective-permute-start | bytes 3145736 | tf_op jit(solution)/shard_map/ppermute | solution.py:337
  12.9 1.6 %shard_map.113.acc = f32[33,128,128]{2,1,0:T(8,128)S(1)} custom-call(s32[1,384]{1,0:T(1,128)S(1)} %get-tuple-element.52.tab, bf16[256,128]{1,0:T(8,128)(2,1)S(1)} %copy-done.2, bf16[256,128]{1,0:T(8,128)(2,1)S(1)} %collective-permute-done.1.x1, bf16[256,128]{1,0:T(8,128)(2,1)S(1)} %collective-permute-done.2.x2, ...), custom_call_target="tpu_custom_call", output_to_operand_aliasing={{}: (6, {})} | custom-call | tf_op jit(solution)/shard_map/pallas_call | solution.py:338
  15.3 1.8 %collective-permute-start.4 = (bf16[1024,128]{1,0:T(8,128)(2,1)S(1)}, bf16[1024,128]{1,0:T(8,128)(2,1)S(1)}, u32[]{:S(2)}, u32[]{:S(2)}) collective-permute-start(bf16[1024,128]{1,0:T(8,128)(2,1)S(1)} %get-tuple-element.67), channel_id=1, source_target_pairs={{0,2},{1,9},{2,4},{3,11},{4,6},{5,13},{6,0},{7,15},{8,10},{9,17},{... | collective-permute-start | bytes 786440 | tf_op jit(solution)/shard_map/ppermute | solution.py:67
  17.1 1.8 %collective-permute-start.5 = (bf16[1024,128]{1,0:T(8,128)(2,1)S(1)}, bf16[1024,128]{1,0:T(8,128)(2,1)S(1)}, u32[]{:S(2)}, u32[]{:S(2)}) collective-permute-start(bf16[1024,128]{1,0:T(8,128)(2,1)S(1)} %get-tuple-element.68), channel_id=1, source_target_pairs={{0,6},{1,25},{2,0},{3,27},{4,2},{5,29},{6,4},{7,31},{8,14},{9,1},{... | collective-permute-start | bytes 786440 | tf_op jit(solution)/shard_map/ppermute | solution.py:67
  20.5 2.4 %collective-permute-done.4.r1 = bf16[1024,128]{1,0:T(8,128)(2,1)S(1)} collective-permute-done((bf16[1024,128]{1,0:T(8,128)(2,1)S(1)}, bf16[1024,128]{1,0:T(8,128)(2,1)S(1)}, u32[]{:S(2)}, u32[]{:S(2)}) %collective-permute-start.4) | collective-permute-done | bytes 262176 | tf_op jit(solution)/shard_map/ppermute | solution.py:67
  22.9 2.2 %collective-permute-done.5.r3 = bf16[1024,128]{1,0:T(8,128)(2,1)S(1)} collective-permute-done((bf16[1024,128]{1,0:T(8,128)(2,1)S(1)}, bf16[1024,128]{1,0:T(8,128)(2,1)S(1)}, u32[]{:S(2)}, u32[]{:S(2)}) %collective-permute-start.5) | collective-permute-done | bytes 262176 | tf_op jit(solution)/shard_map/ppermute | solution.py:67
  25.1 1.8 %collective-permute-done.6.r2 = bf16[1024,128]{1,0:T(8,128)(2,1)S(1)} collective-permute-done((bf16[1024,128]{1,0:T(8,128)(2,1)S(1)}, bf16[1024,128]{1,0:T(8,128)(2,1)S(1)}, u32[]{:S(2)}, u32[]{:S(2)}) %collective-permute-start.6) | collective-permute-done | bytes 262176 | tf_op jit(solution)/shard_map/ppermute | solution.py:67
  28.1 2.2 %collective-permute-start.8 = (bf16[1536,128]{1,0:T(8,128)(2,1)S(1)}, bf16[1536,128]{1,0:T(8,128)(2,1)S(1)}, u32[]{:S(2)}, u32[]{:S(2)}) collective-permute-start(bf16[1536,128]{1,0:T(8,128)(2,1)S(1)} %get-tuple-element.77), channel_id=1, source_target_pairs={{0,24},{1,7},{2,26},{3,1},{4,28},{5,3},{6,30},{7,5},{8,0},{9,15},{... | collective-permute-start | bytes 1179656 | tf_op jit(solution)/shard_map/ppermute | solution.py:67
  31.6 4.1 %collective-permute-done.7.r1 = bf16[1536,128]{1,0:T(8,128)(2,1)S(1)} collective-permute-done((bf16[1536,128]{1,0:T(8,128)(2,1)S(1)}, bf16[1536,128]{1,0:T(8,128)(2,1)S(1)}, u32[]{:S(2)}, u32[]{:S(2)}) %collective-permute-start.7) | collective-permute-done | bytes 393248 | tf_op jit(solution)/shard_map/ppermute | solution.py:67
  35.7 3.6 %collective-permute-done.8.r3 = bf16[1536,128]{1,0:T(8,128)(2,1)S(1)} collective-permute-done((bf16[1536,128]{1,0:T(8,128)(2,1)S(1)}, bf16[1536,128]{1,0:T(8,128)(2,1)S(1)}, u32[]{:S(2)}, u32[]{:S(2)}) %collective-permute-start.8) | collective-permute-done | bytes 393248 | tf_op jit(solution)/shard_map/ppermute | solution.py:67
  39.3 1.8 %collective-permute-done.9.r2 = bf16[1536,128]{1,0:T(8,128)(2,1)S(1)} collective-permute-done((bf16[1536,128]{1,0:T(8,128)(2,1)S(1)}, bf16[1536,128]{1,0:T(8,128)(2,1)S(1)}, u32[]{:S(2)}, u32[]{:S(2)}) %collective-permute-start.9) | collective-permute-done | bytes 393248 | tf_op jit(solution)/shard_map/ppermute | solution.py:67
  42.8 2.0 %collective-permute-start.11 = (bf16[1296,128]{1,0:T(8,128)(2,1)S(1)}, bf16[1296,128]{1,0:T(8,128)(2,1)S(1)}, u32[]{:S(2)}, u32[]{:S(2)}) collective-permute-start(bf16[1296,128]{1,0:T(8,128)(2,1)S(1)} %get-tuple-element.86.refs_0_), channel_id=1, source_target_pairs={{0,6},{1,25},{2,0},{3,27},{4,2},{5,29},{6,4},{7,31},{8,14},{9,1},{... | collective-permute-start | bytes 995336 | tf_op jit(solution)/shard_map/ppermute | solution.py:67
  45.2 2.9 %collective-permute-start.14 = (bf16[1296,128]{1,0:T(8,128)(2,1)S(1)}, bf16[1296,128]{1,0:T(8,128)(2,1)S(1)}, u32[]{:S(2)}, u32[]{:S(2)}) collective-permute-start(bf16[1296,128]{1,0:T(8,128)(2,1)S(1)} %get-tuple-element.86.refs_0_), channel_id=1, source_target_pairs={{0,1},{1,0},{2,3},{3,2},{4,5},{5,4},{6,7},{7,6},{8,9},{9,8},{10,11... | collective-permute-start | bytes 995336 | tf_op jit(solution)/shard_map/ppermute | solution.py:356
  49.6 2.8 %collective-permute-done.11.refs_0_ = bf16[1296,128]{1,0:T(8,128)(2,1)S(1)} collective-permute-done((bf16[1296,128]{1,0:T(8,128)(2,1)S(1)}, bf16[1296,128]{1,0:T(8,128)(2,1)S(1)}, u32[]{:S(2)}, u32[]{:S(2)}) %collective-permute-start.11) | collective-permute-done | bytes 331808 | tf_op jit(solution)/shard_map/ppermute | solution.py:67
  53.6 2.9 %collective-permute-start.15 = (bf16[1296,128]{1,0:T(8,128)(2,1)S(1)}, bf16[1296,128]{1,0:T(8,128)(2,1)S(1)}, u32[]{:S(2)}, u32[]{:S(2)}) collective-permute-start(bf16[1296,128]{1,0:T(8,128)(2,1)S(1)} %collective-permute-done.12.refs_1_), channel_id=1, source_target_pairs={{0,1},{1,0},{2,3},{3,2},{4,5},{5,4},{6,7},{7,6},{8,9},{9,8},{10,11... | collective-permute-start | bytes 995336 | tf_op jit(solution)/shard_map/ppermute | solution.py:356
  57.0 1.6 %shard_map.118 = (f32[9,128,128]{2,1,0:T(8,128)S(1)}, f32[272,128]{1,0:T(8,128)S(1)}) custom-call(s32[1,640]{1,0:T(1,128)S(1)} %get-tuple-element.82.tab, bf16[128,128,128]{2,1,0:T(8,128)(2,1)S(1)} %bitcast.6, bf16[1296,128]{1,0:T(8,128)(2,1)S(1)} %get-tuple-element.86.refs_0_, bf16[1296,128]{1,0:T(8,128)(2,1)S(1)} %collective-permute-done.12.refs_1_, ...), custom_call_target="tpu_custom_call" | custom-call | flops 201326592 | bytes 3145728 | tf_op jit(solution)/shard_map/pallas_call | solution.py:363
  58.7 1.6 %shard_map.119 = (f32[9,128,128]{2,1,0:T(8,128)S(1)}, f32[272,128]{1,0:T(8,128)S(1)}) custom-call(s32[1,640]{1,0:T(1,128)S(1)} %get-tuple-element.82.tab, bf16[128,128,128]{2,1,0:T(8,128)(2,1)S(1)} %bitcast.7, bf16[1296,128]{1,0:T(8,128)(2,1)S(1)} %collective-permute-done.11.refs_0_, ...), custom_call_target="tpu_custom_call", output_to_operand_aliasing={{0}: (6, {})} | custom-call | flops 268435456 | bytes 4194304 | tf_op jit(solution)/shard_map/pallas_call | solution.py:363
  61.4 2.7 %collective-permute-start.18 = (bf16[528,128]{1,0:T(8,128)(2,1)S(1)}, bf16[528,128]{1,0:T(8,128)(2,1)S(1)}, u32[]{:S(2)}, u32[]{:S(2)}) collective-permute-start(bf16[528,128]{1,0:T(8,128)(2,1)S(1)} %get-tuple-element.95), channel_id=1, source_target_pairs={{0,96},{32,0},{64,32},{96,64},{1,97},{33,1},{65,33},{97,65},{2,98}... | collective-permute-start | bytes 405512 | tf_op jit(solution)/shard_map/ppermute | solution.py:377
  65.0 2.9 %collective-permute-done.17.r1 = bf16[528,128]{1,0:T(8,128)(2,1)S(1)} collective-permute-done((bf16[528,128]{1,0:T(8,128)(2,1)S(1)}, bf16[528,128]{1,0:T(8,128)(2,1)S(1)}, u32[]{:S(2)}, u32[]{:S(2)}) %collective-permute-start.17) | collective-permute-done | bytes 135200 | tf_op jit(solution)/shard_map/ppermute | solution.py:377
  67.9 1.7 %collective-permute-done.18.r2 = bf16[528,128]{1,0:T(8,128)(2,1)S(1)} collective-permute-done((bf16[528,128]{1,0:T(8,128)(2,1)S(1)}, bf16[528,128]{1,0:T(8,128)(2,1)S(1)}, u32[]{:S(2)}, u32[]{:S(2)}) %collective-permute-start.18) | collective-permute-done | bytes 135200 | tf_op jit(solution)/shard_map/ppermute | solution.py:377
  (42 shorter events, 15.7 us)
Async XLA Ops:
  0.7 8.8 %collective-permute-start = (bf16[256,128]{1,0:T(8,128)(2,1)}, bf16[256,128]{1,0:T(8,128)(2,1)S(1)}, u32[]{:S(2)}, u32[]{:S(2)}) collective-permute-start(bf16[256,128]{1,0:T(8,128)(2,1)} %x0.3), channel_id=1, source_target_pairs={{0,32},{32,64},{64,96},{96,0},{1,33},{33,65},{65,97},{97,1},{2,34}... | collective-permute-start | bytes 196616 | tf_op jit(solution)/shard_map/ppermute | solution.py:67
  2.8 6.7 %collective-permute-start.1 = (bf16[256,128]{1,0:T(8,128)(2,1)}, bf16[256,128]{1,0:T(8,128)(2,1)S(1)}, u32[]{:S(2)}, u32[]{:S(2)}) collective-permute-start(bf16[256,128]{1,0:T(8,128)(2,1)} %x0.3), channel_id=1, source_target_pairs={{0,96},{32,0},{64,32},{96,64},{1,97},{33,1},{65,33},{97,65},{2,98}... | collective-permute-start | bytes 196616 | tf_op jit(solution)/shard_map/ppermute | solution.py:67
  4.1 5.3 %collective-permute-start.2 = (bf16[256,128]{1,0:T(8,128)(2,1)}, bf16[256,128]{1,0:T(8,128)(2,1)S(1)}, u32[]{:S(2)}, u32[]{:S(2)}) collective-permute-start(bf16[256,128]{1,0:T(8,128)(2,1)} %x0.3), channel_id=1, source_target_pairs={{0,64},{32,96},{64,0},{96,32},{1,65},{33,97},{65,1},{97,33},{2,66}... | collective-permute-start | bytes 196616 | tf_op jit(solution)/shard_map/ppermute | solution.py:67
  11.2 3.9 %collective-permute-start.3 = (bf16[4096,128]{1,0:T(8,128)(2,1)S(1)}, bf16[4096,128]{1,0:T(8,128)(2,1)S(1)}, u32[]{:S(2)}, u32[]{:S(2)}) collective-permute-start(bf16[4096,128]{1,0:T(8,128)(2,1)S(1)} %get-tuple-element.62), channel_id=1, source_target_pairs={{0,1},{1,0},{2,3},{3,2},{4,5},{5,4},{6,7},{7,6},{8,9},{9,8},{10,11... | collective-permute-start | bytes 3145736 | tf_op jit(solution)/shard_map/ppermute | solution.py:337
  14.5 12.4 %copy-start.1 = (bf16[256,256]{1,0:T(8,128)(2,1)S(1)}, bf16[256,256]{1,0:T(8,128)(2,1)}, u32[]{:S(2)}) copy-start(bf16[256,256]{1,0:T(8,128)(2,1)} %cot.3) | copy-start | bytes 393220
  14.5 26.6 %copy-start.3 = (bf16[128,256]{1,0:T(8,128)(2,1)S(1)}, bf16[128,256]{1,0:T(8,128)(2,1)}, u32[]{:S(2)}) copy-start(bf16[128,256]{1,0:T(8,128)(2,1)} %weight.1) | copy-start | bytes 196612
  14.5 26.6 %copy-start.4 = (f32[256]{0:T(256)S(1)}, f32[256]{0:T(256)}, u32[]{:S(2)}) copy-start(f32[256]{0:T(256)} %param.10) | copy-start | bytes 3076
  15.2 41.9 %copy-start = (bf16[1,1,128,128,128]{4,3,2,1,0:T(8,128)(2,1)S(1)}, bf16[1,1,128,128,128]{4,3,2,1,0:T(8,128)(2,1)}, u32[]{:S(2)}) copy-start(bf16[1,1,128,128,128]{4,3,2,1,0:T(8,128)(2,1)} %param.11) | copy-start | bytes 12582916
  15.3 7.5 %collective-permute-start.4 = (bf16[1024,128]{1,0:T(8,128)(2,1)S(1)}, bf16[1024,128]{1,0:T(8,128)(2,1)S(1)}, u32[]{:S(2)}, u32[]{:S(2)}) collective-permute-start(bf16[1024,128]{1,0:T(8,128)(2,1)S(1)} %get-tuple-element.67), channel_id=1, source_target_pairs={{0,2},{1,9},{2,4},{3,11},{4,6},{5,13},{6,0},{7,15},{8,10},{9,17},{... | collective-permute-start | bytes 786440 | tf_op jit(solution)/shard_map/ppermute | solution.py:67
  17.1 7.9 %collective-permute-start.5 = (bf16[1024,128]{1,0:T(8,128)(2,1)S(1)}, bf16[1024,128]{1,0:T(8,128)(2,1)S(1)}, u32[]{:S(2)}, u32[]{:S(2)}) collective-permute-start(bf16[1024,128]{1,0:T(8,128)(2,1)S(1)} %get-tuple-element.68), channel_id=1, source_target_pairs={{0,6},{1,25},{2,0},{3,27},{4,2},{5,29},{6,4},{7,31},{8,14},{9,1},{... | collective-permute-start | bytes 786440 | tf_op jit(solution)/shard_map/ppermute | solution.py:67
  18.9 8.0 %collective-permute-start.6 = (bf16[1024,128]{1,0:T(8,128)(2,1)S(1)}, bf16[1024,128]{1,0:T(8,128)(2,1)S(1)}, u32[]{:S(2)}, u32[]{:S(2)}) collective-permute-start(bf16[1024,128]{1,0:T(8,128)(2,1)S(1)} %get-tuple-element.69), channel_id=1, source_target_pairs={{0,4},{1,17},{2,6},{3,19},{4,0},{5,21},{6,2},{7,23},{8,12},{9,25},... | collective-permute-start | bytes 786440 | tf_op jit(solution)/shard_map/ppermute | solution.py:67
  27.0 8.7 %collective-permute-start.7 = (bf16[1536,128]{1,0:T(8,128)(2,1)S(1)}, bf16[1536,128]{1,0:T(8,128)(2,1)S(1)}, u32[]{:S(2)}, u32[]{:S(2)}) collective-permute-start(bf16[1536,128]{1,0:T(8,128)(2,1)S(1)} %get-tuple-element.77), channel_id=1, source_target_pairs={{0,8},{1,3},{2,10},{3,5},{4,12},{5,7},{6,14},{7,1},{8,16},{9,11},{... | collective-permute-start | bytes 1179656 | tf_op jit(solution)/shard_map/ppermute | solution.py:67
  28.1 11.1 %collective-permute-start.8 = (bf16[1536,128]{1,0:T(8,128)(2,1)S(1)}, bf16[1536,128]{1,0:T(8,128)(2,1)S(1)}, u32[]{:S(2)}, u32[]{:S(2)}) collective-permute-start(bf16[1536,128]{1,0:T(8,128)(2,1)S(1)} %get-tuple-element.77), channel_id=1, source_target_pairs={{0,24},{1,7},{2,26},{3,1},{4,28},{5,3},{6,30},{7,5},{8,0},{9,15},{... | collective-permute-start | bytes 1179656 | tf_op jit(solution)/shard_map/ppermute | solution.py:67
  30.3 10.8 %collective-permute-start.9 = (bf16[1536,128]{1,0:T(8,128)(2,1)S(1)}, bf16[1536,128]{1,0:T(8,128)(2,1)S(1)}, u32[]{:S(2)}, u32[]{:S(2)}) collective-permute-start(bf16[1536,128]{1,0:T(8,128)(2,1)S(1)} %get-tuple-element.77), channel_id=1, source_target_pairs={{0,16},{1,5},{2,18},{3,7},{4,20},{5,1},{6,22},{7,3},{8,24},{9,13},... | collective-permute-start | bytes 1179656 | tf_op jit(solution)/shard_map/ppermute | solution.py:67
  42.1 7.5 %collective-permute-start.10 = (bf16[1296,128]{1,0:T(8,128)(2,1)S(1)}, bf16[1296,128]{1,0:T(8,128)(2,1)S(1)}, u32[]{:S(2)}, u32[]{:S(2)}) collective-permute-start(bf16[1296,128]{1,0:T(8,128)(2,1)S(1)} %get-tuple-element.86.refs_0_), channel_id=1, source_target_pairs={{0,2},{1,9},{2,4},{3,11},{4,6},{5,13},{6,0},{7,15},{8,10},{9,17},{... | collective-permute-start | bytes 995336 | tf_op jit(solution)/shard_map/ppermute | solution.py:67
  42.8 9.6 %collective-permute-start.11 = (bf16[1296,128]{1,0:T(8,128)(2,1)S(1)}, bf16[1296,128]{1,0:T(8,128)(2,1)S(1)}, u32[]{:S(2)}, u32[]{:S(2)}) collective-permute-start(bf16[1296,128]{1,0:T(8,128)(2,1)S(1)} %get-tuple-element.86.refs_0_), channel_id=1, source_target_pairs={{0,6},{1,25},{2,0},{3,27},{4,2},{5,29},{6,4},{7,31},{8,14},{9,1},{... | collective-permute-start | bytes 995336 | tf_op jit(solution)/shard_map/ppermute | solution.py:67
  44.9 8.7 %collective-permute-start.12 = (bf16[1296,128]{1,0:T(8,128)(2,1)S(1)}, bf16[1296,128]{1,0:T(8,128)(2,1)S(1)}, u32[]{:S(2)}, u32[]{:S(2)}) collective-permute-start(bf16[1296,128]{1,0:T(8,128)(2,1)S(1)} %get-tuple-element.86.refs_0_), channel_id=1, source_target_pairs={{0,4},{1,17},{2,6},{3,19},{4,0},{5,21},{6,2},{7,23},{8,12},{9,25},... | collective-permute-start | bytes 995336 | tf_op jit(solution)/shard_map/ppermute | solution.py:67
  45.2 13.4 %collective-permute-start.14 = (bf16[1296,128]{1,0:T(8,128)(2,1)S(1)}, bf16[1296,128]{1,0:T(8,128)(2,1)S(1)}, u32[]{:S(2)}, u32[]{:S(2)}) collective-permute-start(bf16[1296,128]{1,0:T(8,128)(2,1)S(1)} %get-tuple-element.86.refs_0_), channel_id=1, source_target_pairs={{0,1},{1,0},{2,3},{3,2},{4,5},{5,4},{6,7},{7,6},{8,9},{9,8},{10,11... | collective-permute-start | bytes 995336 | tf_op jit(solution)/shard_map/ppermute | solution.py:356
  53.6 5.1 %collective-permute-start.15 = (bf16[1296,128]{1,0:T(8,128)(2,1)S(1)}, bf16[1296,128]{1,0:T(8,128)(2,1)S(1)}, u32[]{:S(2)}, u32[]{:S(2)}) collective-permute-start(bf16[1296,128]{1,0:T(8,128)(2,1)S(1)} %collective-permute-done.12.refs_1_), channel_id=1, source_target_pairs={{0,1},{1,0},{2,3},{3,2},{4,5},{5,4},{6,7},{7,6},{8,9},{9,8},{10,11... | collective-permute-start | bytes 995336 | tf_op jit(solution)/shard_map/ppermute | solution.py:356
  56.5 2.2 %collective-permute-start.16 = (bf16[1296,128]{1,0:T(8,128)(2,1)S(1)}, bf16[1296,128]{1,0:T(8,128)(2,1)S(1)}, u32[]{:S(2)}, u32[]{:S(2)}) collective-permute-start(bf16[1296,128]{1,0:T(8,128)(2,1)S(1)} %collective-permute-done.10.refs_2_), channel_id=1, source_target_pairs={{0,1},{1,0},{2,3},{3,2},{4,5},{5,4},{6,7},{7,6},{8,9},{9,8},{10,11... | collective-permute-start | bytes 995336 | tf_op jit(solution)/shard_map/ppermute | solution.py:356
  56.5 3.8 %collective-permute-start.13 = (bf16[1296,128]{1,0:T(8,128)(2,1)S(1)}, bf16[1296,128]{1,0:T(8,128)(2,1)S(1)}, u32[]{:S(2)}, u32[]{:S(2)}) collective-permute-start(bf16[1296,128]{1,0:T(8,128)(2,1)S(1)} %collective-permute-done.11.refs_0_), channel_id=1, source_target_pairs={{0,1},{1,0},{2,3},{3,2},{4,5},{5,4},{6,7},{7,6},{8,9},{9,8},{10,11... | collective-permute-start | bytes 995336 | tf_op jit(solution)/shard_map/ppermute | solution.py:356
  61.3 6.6 %collective-permute-start.17 = (bf16[528,128]{1,0:T(8,128)(2,1)S(1)}, bf16[528,128]{1,0:T(8,128)(2,1)S(1)}, u32[]{:S(2)}, u32[]{:S(2)}) collective-permute-start(bf16[528,128]{1,0:T(8,128)(2,1)S(1)} %get-tuple-element.94), channel_id=1, source_target_pairs={{0,32},{32,64},{64,96},{96,0},{1,33},{33,65},{65,97},{97,1},{2,34}... | collective-permute-start | bytes 405512 | tf_op jit(solution)/shard_map/ppermute | solution.py:377
  61.4 8.2 %collective-permute-start.18 = (bf16[528,128]{1,0:T(8,128)(2,1)S(1)}, bf16[528,128]{1,0:T(8,128)(2,1)S(1)}, u32[]{:S(2)}, u32[]{:S(2)}) collective-permute-start(bf16[528,128]{1,0:T(8,128)(2,1)S(1)} %get-tuple-element.95), channel_id=1, source_target_pairs={{0,96},{32,0},{64,32},{96,64},{1,97},{33,1},{65,33},{97,65},{2,98}... | collective-permute-start | bytes 405512 | tf_op jit(solution)/shard_map/ppermute | solution.py:377
  64.1 6.2 %collective-permute-start.19 = (bf16[528,128]{1,0:T(8,128)(2,1)S(1)}, bf16[528,128]{1,0:T(8,128)(2,1)S(1)}, u32[]{:S(2)}, u32[]{:S(2)}) collective-permute-start(bf16[528,128]{1,0:T(8,128)(2,1)S(1)} %get-tuple-element.96), channel_id=1, source_target_pairs={{0,64},{32,96},{64,0},{96,32},{1,65},{33,97},{65,1},{97,33},{2,66}... | collective-permute-start | bytes 405512 | tf_op jit(solution)/shard_map/ppermute | solution.py:377
  (3 other events, 24.9 us)

commit v4 on v3

--- a/solution.py
+++ b/solution.py
@@ -24,14 +24,19 @@
     return (y * 4 + z) * 2 + core
 
 
+def ring_of(y, z, core):
+    return (core + y + z) % 2
+
+
 def col_shift(first, d):
     pairs = []
     for y in range(4):
         for z in range(4):
             for core in range(2):
-                along_z = (core == 0) == first
-                to = at(y, (z + d) % 4, core) if along_z else at((y + d) % 4, z, core)
-                pairs.append((at(y, z, core), to))
+                ring = ring_of(y, z, core)
+                along_z = (ring == 0) == first
+                to_y, to_z = (y, (z + d) % 4) if along_z else ((y + d) % 4, z)
+                pairs.append((at(y, z, core), at(to_y, to_z, ring_of(to_y, to_z, ring))))
     return pairs
 
 
@@ -77,10 +82,11 @@
     owner, sub = rows // 2, rows % 2
     core_to, z_to, y_to = owner % 2, (owner // 2) % 4, owner // 8
     dz, dy = (z_to - z + 4) % 4, (y_to - y + 4) % 4
-    first = jnp.where(core_to == 0, dz, dy)
-    second = jnp.where(core_to == 0, dy, dz)
+    ring_to = ring_of(y_to, z_to, core_to)
+    first = jnp.where(ring_to == 0, dz, dy)
+    second = jnp.where(ring_to == 0, dy, dz)
     pos = (first * 4 + second) * 2 + sub
-    half = (core_to != core).astype(jnp.int32)
+    half = (ring_to != ring_of(y, z, core)).astype(jnp.int32)
     ahead = (cols // 2 - r + 4) % 4
     slot = lax.broadcasted_iota(jnp.int32, (1, 128), 1)
 

time: 71.6 us -> 70.5 us (0.985); the launches traced: 71 us -> 69.1 us
  Pallas kernels: 13.6 us -> 11.7 us
  starting transfers between devices: 28.7 us -> 26.8 us
  waiting for transfers between devices: 27.3 us -> 29.1 us
    ppermute x4, starting transfers between devices: 6.35 us -> 1.05 us  [on_device(): theirs = [lax.ppermute(m, 'col', core_swap()) for m in mine]]
    ppermute x12, waiting for transfers between devices: 21.4 us -> 23.5 us  [permute(): lax.ppermute(a, axis, p)]
    ppermute x12, starting transfers between devices: 17.9 us -> 19.5 us  [permute(): lax.ppermute(a, axis, p)]
    pallas_call x4, Pallas kernels: 5.2 us -> 3.93 us  [backward(): call(functools.partial(backward_tiles, key, places), outs, [SMEM] + [VMEM...]
    ppermute x3, starting transfers between devices: 2.74 us -> 3.94 us  [on_device(): rs = [lax.ppermute(a, 'row', row_shift(d)) for a, d in zip(ms, ORDER)]]
    ppermute x3, waiting for transfers between devices: 5.22 us -> 4.49 us  [on_device(): rs = [lax.ppermute(a, 'row', row_shift(d)) for a, d in zip(ms, ORDER)]]
  transfers between devices with their start and end apart: 20 -> 20, of which waited for: 13 -> 13; matrix products, arithmetic and copies ran while one was open for 0% -> 0% of each run, Pallas kernels for 12% -> 10%
where the time goes in v4:
time: 70.5 us; the launch traced here: 69.1 us
  waiting for transfers between devices  29.1 us (41%)
  starting transfers between devices  26.8 us (38%)
  Pallas kernels  11.7 us (17%)
  between operations  1.48 us (2%)
    ppermute x12, waiting for transfers between devices, permute(): lax.ppermute(a, axis, p)  23.5 us
    ppermute x12, starting transfers between devices, permute(): lax.ppermute(a, axis, p)  19.5 us
    ppermute x3, waiting for transfers between devices, on_device(): rs = [lax.ppermute(a, 'row', row_shift(d)) for a, d in zip(ms, ORDER)]  4.49 us
    ppermute x3, starting transfers between devices, on_device(): rs = [lax.ppermute(a, 'row', row_shift(d)) for a, d in zip(ms, ORDER)]  3.94 us
    pallas_call x4, Pallas kernels, backward(): call(functools.partial(backward_tiles, key, places), outs, [SMEM] + [VMEM...  3.93 us
    ppermute x1, starting transfers between devices, on_device(): got = lax.ppermute(other, 'col', core_swap())  2.26 us
    pallas_call x1, Pallas kernels, on_device(): call(hold, (jax.ShapeDtypeStruct((128, B, B), BF16), half, half), [ANY],...  2.22 us
    pallas_call x1, Pallas kernels, on_device(): call(functools.partial(forward_tiles, 0), (half, sds(4096)), [SMEM, ANY]...  1.43 us
  transfers between devices with their start and end apart: 20, of which 13 were waited for; matrix products, arithmetic and copies ran while one was open for 0% of the time, Pallas kernels for 10%

profile of v4, /device:TPU:1, one launch (start us, length us, event | category | flops | bytes accessed | tf_op | source)
XLA Modules:
  0.0 69.1 jit_solution(5449783970617987377)
XLA Ops:
  0.7 2.1 %collective-permute-start = (bf16[256,128]{1,0:T(8,128)(2,1)}, bf16[256,128]{1,0:T(8,128)(2,1)S(1)}, u32[]{:S(2)}, u32[]{:S(2)}) collective-permute-start(bf16[256,128]{1,0:T(8,128)(2,1)} %x0.3), channel_id=1, source_target_pairs={{0,32},{32,64},{64,96},{96,0},{1,33},{33,65},{65,97},{97,1},{2,34}... | collective-permute-start | bytes 196616 | tf_op jit(solution)/shard_map/ppermute | solution.py:72
  2.8 1.3 %collective-permute-start.1 = (bf16[256,128]{1,0:T(8,128)(2,1)}, bf16[256,128]{1,0:T(8,128)(2,1)S(1)}, u32[]{:S(2)}, u32[]{:S(2)}) collective-permute-start(bf16[256,128]{1,0:T(8,128)(2,1)} %x0.3), channel_id=1, source_target_pairs={{0,96},{32,0},{64,32},{96,64},{1,97},{33,1},{65,33},{97,65},{2,98}... | collective-permute-start | bytes 196616 | tf_op jit(solution)/shard_map/ppermute | solution.py:72
  4.1 1.6 %collective-permute-start.2 = (bf16[256,128]{1,0:T(8,128)(2,1)}, bf16[256,128]{1,0:T(8,128)(2,1)S(1)}, u32[]{:S(2)}, u32[]{:S(2)}) collective-permute-start(bf16[256,128]{1,0:T(8,128)(2,1)} %x0.3), channel_id=1, source_target_pairs={{0,64},{32,96},{64,0},{96,32},{1,65},{33,97},{65,1},{97,33},{2,66}... | collective-permute-start | bytes 196616 | tf_op jit(solution)/shard_map/ppermute | solution.py:72
  6.4 2.2 %shard_map.112 = (bf16[128,128,128]{2,1,0:T(8,128)(2,1)S(1)}, f32[33,128,128]{2,1,0:T(8,128)S(1)}, f32[33,128,128]{2,1,0:T(8,128)S(1)}) custom-call(bf16[128,128,128]{2,1,0:T(8,128)(2,1)} %bitcast.5), custom_call_target="tpu_custom_call" | custom-call | tf_op jit(solution)/shard_map/pallas_call | solution.py:326
  9.5 1.4 %shard_map.114 = (f32[33,128,128]{2,1,0:T(8,128)S(1)}, bf16[4096,128]{1,0:T(8,128)(2,1)S(1)}) custom-call(s32[1,384]{1,0:T(1,128)S(1)} %get-tuple-element.52.tab, bf16[256,128]{1,0:T(8,128)(2,1)S(1)} %copy-done.2, bf16[256,128]{1,0:T(8,128)(2,1)S(1)} %collective-permute-done.1.x1, ...), custom_call_target="tpu_custom_call", output_to_operand_aliasing={{0}: (6, {})} | custom-call | flops 268435456 | bytes 4194304 | tf_op jit(solution)/shard_map/pallas_call | solution.py:335
  10.9 2.3 %collective-permute-start.3 = (bf16[4096,128]{1,0:T(8,128)(2,1)S(1)}, bf16[4096,128]{1,0:T(8,128)(2,1)S(1)}, u32[]{:S(2)}, u32[]{:S(2)}) collective-permute-start(bf16[4096,128]{1,0:T(8,128)(2,1)S(1)} %get-tuple-element.62), channel_id=1, source_target_pairs={{0,1},{1,0},{2,3},{3,2},{4,5},{5,4},{6,7},{7,6},{8,9},{9,8},{10,11... | collective-permute-start | bytes 3145736 | tf_op jit(solution)/shard_map/ppermute | solution.py:343
  13.2 1.3 %shard_map.113.acc = f32[33,128,128]{2,1,0:T(8,128)S(1)} custom-call(s32[1,384]{1,0:T(1,128)S(1)} %get-tuple-element.52.tab, bf16[256,128]{1,0:T(8,128)(2,1)S(1)} %copy-done.2, bf16[256,128]{1,0:T(8,128)(2,1)S(1)} %collective-permute-done.1.x1, bf16[256,128]{1,0:T(8,128)(2,1)S(1)} %collective-permute-done.2.x2, ...), custom_call_target="tpu_custom_call", output_to_operand_aliasing={{}: (6, {})} | custom-call | tf_op jit(solution)/shard_map/pallas_call | solution.py:344
  15.7 2.0 %collective-permute-start.4 = (bf16[1024,128]{1,0:T(8,128)(2,1)S(1)}, bf16[1024,128]{1,0:T(8,128)(2,1)S(1)}, u32[]{:S(2)}, u32[]{:S(2)}) collective-permute-start(bf16[1024,128]{1,0:T(8,128)(2,1)S(1)} %get-tuple-element.67), channel_id=1, source_target_pairs={{0,3},{1,8},{2,11},{3,4},{4,7},{5,12},{6,15},{7,0},{8,17},{9,10},{... | collective-permute-start | bytes 786440 | tf_op jit(solution)/shard_map/ppermute | solution.py:72
  18.7 2.1 %collective-permute-start.6 = (bf16[1024,128]{1,0:T(8,128)(2,1)S(1)}, bf16[1024,128]{1,0:T(8,128)(2,1)S(1)}, u32[]{:S(2)}, u32[]{:S(2)}) collective-permute-start(bf16[1024,128]{1,0:T(8,128)(2,1)S(1)} %get-tuple-element.69), channel_id=1, source_target_pairs={{0,4},{1,17},{2,18},{3,7},{4,0},{5,21},{6,22},{7,3},{8,24},{9,13},... | collective-permute-start | bytes 786440 | tf_op jit(solution)/shard_map/ppermute | solution.py:72
  20.8 2.3 %collective-permute-done.4.r1 = bf16[1024,128]{1,0:T(8,128)(2,1)S(1)} collective-permute-done((bf16[1024,128]{1,0:T(8,128)(2,1)S(1)}, bf16[1024,128]{1,0:T(8,128)(2,1)S(1)}, u32[]{:S(2)}, u32[]{:S(2)}) %collective-permute-start.4) | collective-permute-done | bytes 262176 | tf_op jit(solution)/shard_map/ppermute | solution.py:72
  23.6 2.9 %collective-permute-done.6.r2 = bf16[1024,128]{1,0:T(8,128)(2,1)S(1)} collective-permute-done((bf16[1024,128]{1,0:T(8,128)(2,1)S(1)}, bf16[1024,128]{1,0:T(8,128)(2,1)S(1)}, u32[]{:S(2)}, u32[]{:S(2)}) %collective-permute-start.6) | collective-permute-done | bytes 262176 | tf_op jit(solution)/shard_map/ppermute | solution.py:72
  26.7 2.9 %collective-permute-start.7 = (bf16[1536,128]{1,0:T(8,128)(2,1)S(1)}, bf16[1536,128]{1,0:T(8,128)(2,1)S(1)}, u32[]{:S(2)}, u32[]{:S(2)}) collective-permute-start(bf16[1536,128]{1,0:T(8,128)(2,1)S(1)} %get-tuple-element.77), channel_id=1, source_target_pairs={{0,9},{1,2},{2,5},{3,10},{4,13},{5,6},{6,1},{7,14},{8,11},{9,16},{... | collective-permute-start | bytes 1179656 | tf_op jit(solution)/shard_map/ppermute | solution.py:72
  29.6 1.9 %collective-permute-start.8 = (bf16[1536,128]{1,0:T(8,128)(2,1)S(1)}, bf16[1536,128]{1,0:T(8,128)(2,1)S(1)}, u32[]{:S(2)}, u32[]{:S(2)}) collective-permute-start(bf16[1536,128]{1,0:T(8,128)(2,1)S(1)} %get-tuple-element.77), channel_id=1, source_target_pairs={{0,25},{1,6},{2,1},{3,26},{4,29},{5,2},{6,5},{7,30},{8,15},{9,0},{... | collective-permute-start | bytes 1179656 | tf_op jit(solution)/shard_map/ppermute | solution.py:72
  31.5 1.1 %collective-permute-start.9 = (bf16[1536,128]{1,0:T(8,128)(2,1)S(1)}, bf16[1536,128]{1,0:T(8,128)(2,1)S(1)}, u32[]{:S(2)}, u32[]{:S(2)}) collective-permute-start(bf16[1536,128]{1,0:T(8,128)(2,1)S(1)} %get-tuple-element.77), channel_id=1, source_target_pairs={{0,16},{1,5},{2,6},{3,19},{4,20},{5,1},{6,2},{7,23},{8,12},{9,25},... | collective-permute-start | bytes 1179656 | tf_op jit(solution)/shard_map/ppermute | solution.py:72
  32.6 4.3 %collective-permute-done.7.r1 = bf16[1536,128]{1,0:T(8,128)(2,1)S(1)} collective-permute-done((bf16[1536,128]{1,0:T(8,128)(2,1)S(1)}, bf16[1536,128]{1,0:T(8,128)(2,1)S(1)}, u32[]{:S(2)}, u32[]{:S(2)}) %collective-permute-start.7) | collective-permute-done | bytes 393248 | tf_op jit(solution)/shard_map/ppermute | solution.py:72
  37.1 5.1 %collective-permute-done.9.r2 = bf16[1536,128]{1,0:T(8,128)(2,1)S(1)} collective-permute-done((bf16[1536,128]{1,0:T(8,128)(2,1)S(1)}, bf16[1536,128]{1,0:T(8,128)(2,1)S(1)}, u32[]{:S(2)}, u32[]{:S(2)}) %collective-permute-start.9) | collective-permute-done | bytes 393248 | tf_op jit(solution)/shard_map/ppermute | solution.py:72
  43.1 1.5 %collective-permute-start.10 = (bf16[1296,128]{1,0:T(8,128)(2,1)S(1)}, bf16[1296,128]{1,0:T(8,128)(2,1)S(1)}, u32[]{:S(2)}, u32[]{:S(2)}) collective-permute-start(bf16[1296,128]{1,0:T(8,128)(2,1)S(1)} %get-tuple-element.86.refs_0_), channel_id=1, source_target_pairs={{0,3},{1,8},{2,11},{3,4},{4,7},{5,12},{6,15},{7,0},{8,17},{9,10},{... | collective-permute-start | bytes 995336 | tf_op jit(solution)/shard_map/ppermute | solution.py:72
  44.6 1.6 %collective-permute-start.11 = (bf16[1296,128]{1,0:T(8,128)(2,1)S(1)}, bf16[1296,128]{1,0:T(8,128)(2,1)S(1)}, u32[]{:S(2)}, u32[]{:S(2)}) collective-permute-start(bf16[1296,128]{1,0:T(8,128)(2,1)S(1)} %get-tuple-element.86.refs_0_), channel_id=1, source_target_pairs={{0,7},{1,24},{2,27},{3,0},{4,3},{5,28},{6,31},{7,4},{8,1},{9,14},{... | collective-permute-start | bytes 995336 | tf_op jit(solution)/shard_map/ppermute | solution.py:72
  46.7 4.6 %collective-permute-done.10.refs_2_ = bf16[1296,128]{1,0:T(8,128)(2,1)S(1)} collective-permute-done((bf16[1296,128]{1,0:T(8,128)(2,1)S(1)}, bf16[1296,128]{1,0:T(8,128)(2,1)S(1)}, u32[]{:S(2)}, u32[]{:S(2)}) %collective-permute-start.10) | collective-permute-done | bytes 331808 | tf_op jit(solution)/shard_map/ppermute | solution.py:72
  51.4 3.4 %collective-permute-done.12.refs_1_ = bf16[1296,128]{1,0:T(8,128)(2,1)S(1)} collective-permute-done((bf16[1296,128]{1,0:T(8,128)(2,1)S(1)}, bf16[1296,128]{1,0:T(8,128)(2,1)S(1)}, u32[]{:S(2)}, u32[]{:S(2)}) %collective-permute-start.12) | collective-permute-done | bytes 331808 | tf_op jit(solution)/shard_map/ppermute | solution.py:72
  56.9 1.3 %shard_map.119 = (f32[9,128,128]{2,1,0:T(8,128)S(1)}, f32[272,128]{1,0:T(8,128)S(1)}) custom-call(s32[1,640]{1,0:T(1,128)S(1)} %get-tuple-element.82.tab, bf16[128,128,128]{2,1,0:T(8,128)(2,1)S(1)} %bitcast.7, bf16[1296,128]{1,0:T(8,128)(2,1)S(1)} %collective-permute-done.11.refs_0_, ...), custom_call_target="tpu_custom_call", output_to_operand_aliasing={{0}: (6, {})} | custom-call | flops 268435456 | bytes 4194304 | tf_op jit(solution)/shard_map/pallas_call | solution.py:369
  59.9 2.1 %collective-permute-start.18 = (bf16[528,128]{1,0:T(8,128)(2,1)S(1)}, bf16[528,128]{1,0:T(8,128)(2,1)S(1)}, u32[]{:S(2)}, u32[]{:S(2)}) collective-permute-start(bf16[528,128]{1,0:T(8,128)(2,1)S(1)} %get-tuple-element.95), channel_id=1, source_target_pairs={{0,96},{32,0},{64,32},{96,64},{1,97},{33,1},{65,33},{97,65},{2,98}... | collective-permute-start | bytes 405512 | tf_op jit(solution)/shard_map/ppermute | solution.py:383
  62.0 1.2 %collective-permute-start.19 = (bf16[528,128]{1,0:T(8,128)(2,1)S(1)}, bf16[528,128]{1,0:T(8,128)(2,1)S(1)}, u32[]{:S(2)}, u32[]{:S(2)}) collective-permute-start(bf16[528,128]{1,0:T(8,128)(2,1)S(1)} %get-tuple-element.96), channel_id=1, source_target_pairs={{0,64},{32,96},{64,0},{96,32},{1,65},{33,97},{65,1},{97,33},{2,66}... | collective-permute-start | bytes 405512 | tf_op jit(solution)/shard_map/ppermute | solution.py:383
  64.8 3.6 %collective-permute-done.19.r3 = bf16[528,128]{1,0:T(8,128)(2,1)S(1)} collective-permute-done((bf16[528,128]{1,0:T(8,128)(2,1)S(1)}, bf16[528,128]{1,0:T(8,128)(2,1)S(1)}, u32[]{:S(2)}, u32[]{:S(2)}) %collective-permute-start.19) | collective-permute-done | bytes 135200 | tf_op jit(solution)/shard_map/ppermute | solution.py:383
  (42 shorter events, 11.6 us)
Async XLA Ops:
  0.7 8.8 %collective-permute-start = (bf16[256,128]{1,0:T(8,128)(2,1)}, bf16[256,128]{1,0:T(8,128)(2,1)S(1)}, u32[]{:S(2)}, u32[]{:S(2)}) collective-permute-start(bf16[256,128]{1,0:T(8,128)(2,1)} %x0.3), channel_id=1, source_target_pairs={{0,32},{32,64},{64,96},{96,0},{1,33},{33,65},{65,97},{97,1},{2,34}... | collective-permute-start | bytes 196616 | tf_op jit(solution)/shard_map/ppermute | solution.py:72
  2.8 6.7 %collective-permute-start.1 = (bf16[256,128]{1,0:T(8,128)(2,1)}, bf16[256,128]{1,0:T(8,128)(2,1)S(1)}, u32[]{:S(2)}, u32[]{:S(2)}) collective-permute-start(bf16[256,128]{1,0:T(8,128)(2,1)} %x0.3), channel_id=1, source_target_pairs={{0,96},{32,0},{64,32},{96,64},{1,97},{33,1},{65,33},{97,65},{2,98}... | collective-permute-start | bytes 196616 | tf_op jit(solution)/shard_map/ppermute | solution.py:72
  4.1 5.4 %collective-permute-start.2 = (bf16[256,128]{1,0:T(8,128)(2,1)}, bf16[256,128]{1,0:T(8,128)(2,1)S(1)}, u32[]{:S(2)}, u32[]{:S(2)}) collective-permute-start(bf16[256,128]{1,0:T(8,128)(2,1)} %x0.3), channel_id=1, source_target_pairs={{0,64},{32,96},{64,0},{96,32},{1,65},{33,97},{65,1},{97,33},{2,66}... | collective-permute-start | bytes 196616 | tf_op jit(solution)/shard_map/ppermute | solution.py:72
  10.9 4.5 %collective-permute-start.3 = (bf16[4096,128]{1,0:T(8,128)(2,1)S(1)}, bf16[4096,128]{1,0:T(8,128)(2,1)S(1)}, u32[]{:S(2)}, u32[]{:S(2)}) collective-permute-start(bf16[4096,128]{1,0:T(8,128)(2,1)S(1)} %get-tuple-element.62), channel_id=1, source_target_pairs={{0,1},{1,0},{2,3},{3,2},{4,5},{5,4},{6,7},{7,6},{8,9},{9,8},{10,11... | collective-permute-start | bytes 3145736 | tf_op jit(solution)/shard_map/ppermute | solution.py:343
  14.5 12.0 %copy-start.1 = (bf16[256,256]{1,0:T(8,128)(2,1)S(1)}, bf16[256,256]{1,0:T(8,128)(2,1)}, u32[]{:S(2)}) copy-start(bf16[256,256]{1,0:T(8,128)(2,1)} %cot.3) | copy-start | bytes 393220
  14.5 27.7 %copy-start.3 = (bf16[128,256]{1,0:T(8,128)(2,1)S(1)}, bf16[128,256]{1,0:T(8,128)(2,1)}, u32[]{:S(2)}) copy-start(bf16[128,256]{1,0:T(8,128)(2,1)} %weight.1) | copy-start | bytes 196612
  14.5 27.6 %copy-start.4 = (f32[256]{0:T(256)S(1)}, f32[256]{0:T(256)}, u32[]{:S(2)}) copy-start(f32[256]{0:T(256)} %param.10) | copy-start | bytes 3076
  15.5 40.2 %copy-start = (bf16[1,1,128,128,128]{4,3,2,1,0:T(8,128)(2,1)S(1)}, bf16[1,1,128,128,128]{4,3,2,1,0:T(8,128)(2,1)}, u32[]{:S(2)}) copy-start(bf16[1,1,128,128,128]{4,3,2,1,0:T(8,128)(2,1)} %param.11) | copy-start | bytes 12582916
  15.7 7.4 %collective-permute-start.4 = (bf16[1024,128]{1,0:T(8,128)(2,1)S(1)}, bf16[1024,128]{1,0:T(8,128)(2,1)S(1)}, u32[]{:S(2)}, u32[]{:S(2)}) collective-permute-start(bf16[1024,128]{1,0:T(8,128)(2,1)S(1)} %get-tuple-element.67), channel_id=1, source_target_pairs={{0,3},{1,8},{2,11},{3,4},{4,7},{5,12},{6,15},{7,0},{8,17},{9,10},{... | collective-permute-start | bytes 786440 | tf_op jit(solution)/shard_map/ppermute | solution.py:72
  17.7 6.0 %collective-permute-start.5 = (bf16[1024,128]{1,0:T(8,128)(2,1)S(1)}, bf16[1024,128]{1,0:T(8,128)(2,1)S(1)}, u32[]{:S(2)}, u32[]{:S(2)}) collective-permute-start(bf16[1024,128]{1,0:T(8,128)(2,1)S(1)} %get-tuple-element.68), channel_id=1, source_target_pairs={{0,7},{1,24},{2,27},{3,0},{4,3},{5,28},{6,31},{7,4},{8,1},{9,14},{... | collective-permute-start | bytes 786440 | tf_op jit(solution)/shard_map/ppermute | solution.py:72
  18.7 7.9 %collective-permute-start.6 = (bf16[1024,128]{1,0:T(8,128)(2,1)S(1)}, bf16[1024,128]{1,0:T(8,128)(2,1)S(1)}, u32[]{:S(2)}, u32[]{:S(2)}) collective-permute-start(bf16[1024,128]{1,0:T(8,128)(2,1)S(1)} %get-tuple-element.69), channel_id=1, source_target_pairs={{0,4},{1,17},{2,18},{3,7},{4,0},{5,21},{6,22},{7,3},{8,24},{9,13},... | collective-permute-start | bytes 786440 | tf_op jit(solution)/shard_map/ppermute | solution.py:72
  26.7 10.2 %collective-permute-start.7 = (bf16[1536,128]{1,0:T(8,128)(2,1)S(1)}, bf16[1536,128]{1,0:T(8,128)(2,1)S(1)}, u32[]{:S(2)}, u32[]{:S(2)}) collective-permute-start(bf16[1536,128]{1,0:T(8,128)(2,1)S(1)} %get-tuple-element.77), channel_id=1, source_target_pairs={{0,9},{1,2},{2,5},{3,10},{4,13},{5,6},{6,1},{7,14},{8,11},{9,16},{... | collective-permute-start | bytes 1179656 | tf_op jit(solution)/shard_map/ppermute | solution.py:72
  29.6 7.5 %collective-permute-start.8 = (bf16[1536,128]{1,0:T(8,128)(2,1)S(1)}, bf16[1536,128]{1,0:T(8,128)(2,1)S(1)}, u32[]{:S(2)}, u32[]{:S(2)}) collective-permute-start(bf16[1536,128]{1,0:T(8,128)(2,1)S(1)} %get-tuple-element.77), channel_id=1, source_target_pairs={{0,25},{1,6},{2,1},{3,26},{4,29},{5,2},{6,5},{7,30},{8,15},{9,0},{... | collective-permute-start | bytes 1179656 | tf_op jit(solution)/shard_map/ppermute | solution.py:72
  31.5 10.7 %collective-permute-start.9 = (bf16[1536,128]{1,0:T(8,128)(2,1)S(1)}, bf16[1536,128]{1,0:T(8,128)(2,1)S(1)}, u32[]{:S(2)}, u32[]{:S(2)}) collective-permute-start(bf16[1536,128]{1,0:T(8,128)(2,1)S(1)} %get-tuple-element.77), channel_id=1, source_target_pairs={{0,16},{1,5},{2,6},{3,19},{4,20},{5,1},{6,2},{7,23},{8,12},{9,25},... | collective-permute-start | bytes 1179656 | tf_op jit(solution)/shard_map/ppermute | solution.py:72
  43.1 8.1 %collective-permute-start.10 = (bf16[1296,128]{1,0:T(8,128)(2,1)S(1)}, bf16[1296,128]{1,0:T(8,128)(2,1)S(1)}, u32[]{:S(2)}, u32[]{:S(2)}) collective-permute-start(bf16[1296,128]{1,0:T(8,128)(2,1)S(1)} %get-tuple-element.86.refs_0_), channel_id=1, source_target_pairs={{0,3},{1,8},{2,11},{3,4},{4,7},{5,12},{6,15},{7,0},{8,17},{9,10},{... | collective-permute-start | bytes 995336 | tf_op jit(solution)/shard_map/ppermute | solution.py:72
  44.6 6.8 %collective-permute-start.11 = (bf16[1296,128]{1,0:T(8,128)(2,1)S(1)}, bf16[1296,128]{1,0:T(8,128)(2,1)S(1)}, u32[]{:S(2)}, u32[]{:S(2)}) collective-permute-start(bf16[1296,128]{1,0:T(8,128)(2,1)S(1)} %get-tuple-element.86.refs_0_), channel_id=1, source_target_pairs={{0,7},{1,24},{2,27},{3,0},{4,3},{5,28},{6,31},{7,4},{8,1},{9,14},{... | collective-permute-start | bytes 995336 | tf_op jit(solution)/shard_map/ppermute | solution.py:72
  46.2 8.6 %collective-permute-start.12 = (bf16[1296,128]{1,0:T(8,128)(2,1)S(1)}, bf16[1296,128]{1,0:T(8,128)(2,1)S(1)}, u32[]{:S(2)}, u32[]{:S(2)}) collective-permute-start(bf16[1296,128]{1,0:T(8,128)(2,1)S(1)} %get-tuple-element.86.refs_0_), channel_id=1, source_target_pairs={{0,4},{1,17},{2,18},{3,7},{4,0},{5,21},{6,22},{7,3},{8,24},{9,13},... | collective-permute-start | bytes 995336 | tf_op jit(solution)/shard_map/ppermute | solution.py:72
  46.5 10.2 %collective-permute-start.14 = (bf16[1296,128]{1,0:T(8,128)(2,1)S(1)}, bf16[1296,128]{1,0:T(8,128)(2,1)S(1)}, u32[]{:S(2)}, u32[]{:S(2)}) collective-permute-start(bf16[1296,128]{1,0:T(8,128)(2,1)S(1)} %get-tuple-element.86.refs_0_), channel_id=1, source_target_pairs={{0,1},{1,0},{2,3},{3,2},{4,5},{5,4},{6,7},{7,6},{8,9},{9,8},{10,11... | collective-permute-start | bytes 995336 | tf_op jit(solution)/shard_map/ppermute | solution.py:362
  54.8 1.9 %collective-permute-start.15 = (bf16[1296,128]{1,0:T(8,128)(2,1)S(1)}, bf16[1296,128]{1,0:T(8,128)(2,1)S(1)}, u32[]{:S(2)}, u32[]{:S(2)}) collective-permute-start(bf16[1296,128]{1,0:T(8,128)(2,1)S(1)} %collective-permute-done.12.refs_1_), channel_id=1, source_target_pairs={{0,1},{1,0},{2,3},{3,2},{4,5},{5,4},{6,7},{7,6},{8,9},{9,8},{10,11... | collective-permute-start | bytes 995336 | tf_op jit(solution)/shard_map/ppermute | solution.py:362
  55.2 1.7 %collective-permute-start.16 = (bf16[1296,128]{1,0:T(8,128)(2,1)S(1)}, bf16[1296,128]{1,0:T(8,128)(2,1)S(1)}, u32[]{:S(2)}, u32[]{:S(2)}) collective-permute-start(bf16[1296,128]{1,0:T(8,128)(2,1)S(1)} %collective-permute-done.10.refs_2_), channel_id=1, source_target_pairs={{0,1},{1,0},{2,3},{3,2},{4,5},{5,4},{6,7},{7,6},{8,9},{9,8},{10,11... | collective-permute-start | bytes 995336 | tf_op jit(solution)/shard_map/ppermute | solution.py:362
  55.3 2.9 %collective-permute-start.13 = (bf16[1296,128]{1,0:T(8,128)(2,1)S(1)}, bf16[1296,128]{1,0:T(8,128)(2,1)S(1)}, u32[]{:S(2)}, u32[]{:S(2)}) collective-permute-start(bf16[1296,128]{1,0:T(8,128)(2,1)S(1)} %collective-permute-done.11.refs_0_), channel_id=1, source_target_pairs={{0,1},{1,0},{2,3},{3,2},{4,5},{5,4},{6,7},{7,6},{8,9},{9,8},{10,11... | collective-permute-start | bytes 995336 | tf_op jit(solution)/shard_map/ppermute | solution.py:362
  59.3 5.5 %collective-permute-start.17 = (bf16[528,128]{1,0:T(8,128)(2,1)S(1)}, bf16[528,128]{1,0:T(8,128)(2,1)S(1)}, u32[]{:S(2)}, u32[]{:S(2)}) collective-permute-start(bf16[528,128]{1,0:T(8,128)(2,1)S(1)} %get-tuple-element.94), channel_id=1, source_target_pairs={{0,32},{32,64},{64,96},{96,0},{1,33},{33,65},{65,97},{97,1},{2,34}... | collective-permute-start | bytes 405512 | tf_op jit(solution)/shard_map/ppermute | solution.py:383
  59.9 4.9 %collective-permute-start.18 = (bf16[528,128]{1,0:T(8,128)(2,1)S(1)}, bf16[528,128]{1,0:T(8,128)(2,1)S(1)}, u32[]{:S(2)}, u32[]{:S(2)}) collective-permute-start(bf16[528,128]{1,0:T(8,128)(2,1)S(1)} %get-tuple-element.95), channel_id=1, source_target_pairs={{0,96},{32,0},{64,32},{96,64},{1,97},{33,1},{65,33},{97,65},{2,98}... | collective-permute-start | bytes 405512 | tf_op jit(solution)/shard_map/ppermute | solution.py:383
  62.0 6.3 %collective-permute-start.19 = (bf16[528,128]{1,0:T(8,128)(2,1)S(1)}, bf16[528,128]{1,0:T(8,128)(2,1)S(1)}, u32[]{:S(2)}, u32[]{:S(2)}) collective-permute-start(bf16[528,128]{1,0:T(8,128)(2,1)S(1)} %get-tuple-element.96), channel_id=1, source_target_pairs={{0,64},{32,96},{64,0},{96,32},{1,65},{33,97},{65,1},{97,33},{2,66}... | collective-permute-start | bytes 405512 | tf_op jit(solution)/shard_map/ppermute | solution.py:383
  (3 other events, 24.9 us)

commit v5 on v4

--- a/solution.py
+++ b/solution.py
@@ -67,9 +67,10 @@
     return jax.ShapeDtypeStruct((rows, cols), dtype)
 
 
-def permute(arrays, axis, pairs):
+def permute(arrays, axis, pairs, together=True):
     arrays = lax.optimization_barrier(tuple(arrays))
-    return lax.optimization_barrier([lax.ppermute(a, axis, p) for a, p in zip(arrays, pairs)])
+    moved = [lax.ppermute(a, axis, p) for a, p in zip(arrays, pairs)]
+    return lax.optimization_barrier(moved) if together else moved
 
 
 ORDER = (1, 3, 2)
@@ -116,8 +117,9 @@
         return entry
 
     forward_tab[...] = table(1 - half, 2, ahead * 2 + cols % 2, pos, 32, TAB)
-    late = (first == 1).astype(jnp.int32)
-    key = jnp.where(half + late < 2, half + late, jnp.where(ahead == 0, 3, 2))
+    late = ((first == 1) | (first == 2)).astype(jnp.int32)
+    group = late + jnp.where(first == 0, 0, half)
+    key = jnp.where(group < 2, group, jnp.where(ahead == 0, 3, 2))
     take = half * 32 + pos
     backward_tab[...] = table(key, 4, take, ahead * 2 + cols % 2, 8, BACKWARD_TAB)
 
@@ -357,15 +359,17 @@
     act, msg = call(local, (sds(256, 256), sds(1024 + TAIL)), [VMEM] * 7)(
         total, r1, r2, r3, weight, bias_vector.reshape(1, 256), cotangent
     )
-    r1, r3, r2 = permute([msg] * 3, "col", [col_shift(True, d) for d in ORDER])
-    mine = (msg, r3, r2, r1)
-    theirs = [lax.ppermute(m, "col", core_swap()) for m in mine]
+    r1, r3, r2 = permute([msg] * 3, "col", [col_shift(True, d) for d in ORDER], False)
+    mine = [msg, r3, r2, r1]
+    theirs = [None] * 4
+    for k in (0, 3):
+        theirs[k] = lax.ppermute(mine[k], "col", core_swap())
     out, tail = sds(256 + TAIL), sds(TAIL, dtype=F32)
     sums = jax.ShapeDtypeStruct((9, B, B), F32)
     blocks, acc = pltpu.VMEM((64, B, B), BF16), pltpu.VMEM((9, B, B), F32)
 
     def backward(key, places, outs, scratch, tiles, aliases, *extra):
-        pieces = [(mine + tuple(theirs))[p] for p in places]
+        pieces = [(mine + theirs)[p] for p in places]
         return call(
             functools.partial(backward_tiles, key, places),
             outs,
@@ -375,10 +379,13 @@
             aliases=aliases,
         )(backward_tab, adj, *pieces, *extra)
 
-    state = backward(0, (0, 2, 3), (sums, tail), [blocks], 48, None)
-    state = backward(1, (1, 4, 6, 7), (sums, tail), [blocks], 64, {6: 0}, *state)
-    ms = backward(2, (5,), (out,) * 3, [acc, blocks], 16, None, *state)
-    (m,) = backward(3, (5,), (sds(256 + TAIL, dtype=F32),), [acc, blocks], 0, None, *state)
+    state = backward(0, (0, 3, 4), (sums, tail), [blocks], 48, None)
+    mine[1], mine[2], *state = lax.optimization_barrier((mine[1], mine[2], *state))
+    for k in (1, 2):
+        theirs[k] = lax.ppermute(mine[k], "col", core_swap())
+    state = backward(1, (1, 2, 7), (sums, tail), [blocks], 48, {5: 0}, *state)
+    ms = backward(2, (5, 6), (out,) * 3, [acc, blocks], 16, None, *state)
+    (m,) = backward(3, (5, 6), (sds(256 + TAIL, dtype=F32),), [acc, blocks], 0, None, *state)
     ms = [ms[d - 1] for d in ORDER]
     rs = [lax.ppermute(a, "row", row_shift(d)) for a, d in zip(ms, ORDER)]
     feat, wgrad, bgrad = call(

time: 70.5 us -> 68.8 us (0.976); the launches traced: 69.1 us -> 68.1 us
  waiting for transfers between devices: 29.1 us -> 25.3 us
  Pallas kernels: 11.7 us -> 14.2 us
    ppermute x16, waiting for transfers between devices: 23.7 us -> 20 us  [the longest x12 20 us: permute(): moved = [lax.ppermute(a, axis, p) for a, p in zip(arrays, pairs)]]
    ppermute x16, starting transfers between devices: 20.6 us -> 22.1 us  [the longest x12 21.1 us: permute(): moved = [lax.ppermute(a, axis, p) for a, p in zip(arrays, pairs)]]
    pallas_call x4, Pallas kernels: 3.93 us -> 5.16 us  [backward(): call(functools.partial(backward_tiles, key, places), outs, [SMEM] + [VMEM...]
    ppermute x1, starting transfers between devices: 2.26 us -> 1.34 us  [on_device(): got = lax.ppermute(other, 'col', core_swap())]
  transfers between devices with their start and end apart: 20 -> 20, of which waited for: 13 -> 12; matrix products, arithmetic and copies ran while one was open for 0% -> 0% of each run, Pallas kernels for 10% -> 13%
where the time goes in v5:
time: 68.8 us; the launch traced here: 68.1 us
  starting transfers between devices  27.1 us (39%)
  waiting for transfers between devices  25.3 us (37%)
  Pallas kernels  14.2 us (21%)
  between operations  1.48 us (2%)
    ppermute x12, starting transfers between devices, permute(): moved = [lax.ppermute(a, axis, p) for a, p in zip(arrays, pairs)]  21.1 us
    ppermute x12, waiting for transfers between devices, permute(): moved = [lax.ppermute(a, axis, p) for a, p in zip(arrays, pairs)]  20 us
    pallas_call x4, Pallas kernels, backward(): call(functools.partial(backward_tiles, key, places), outs, [SMEM] + [VMEM...  5.16 us
    ppermute x3, waiting for transfers between devices, on_device(): rs = [lax.ppermute(a, 'row', row_shift(d)) for a, d in zip(ms, ORDER)]  4.97 us
    ppermute x3, starting transfers between devices, on_device(): rs = [lax.ppermute(a, 'row', row_shift(d)) for a, d in zip(ms, ORDER)]  3.74 us
    pallas_call x1, Pallas kernels, on_device(): call(hold, (jax.ShapeDtypeStruct((128, B, B), BF16), half, half), [ANY],...  2.22 us
    pallas_call x1, Pallas kernels, on_device(): call(functools.partial(forward_tiles, 0), (half, sds(4096)), [SMEM, ANY]...  2.04 us
    pallas_call x1, Pallas kernels, on_device(): call(functools.partial(forward_tiles, 1), half, [SMEM, ANY] + [VMEM] * 5,...  1.91 us
  transfers between devices with their start and end apart: 20, of which 12 were waited for; matrix products, arithmetic and copies ran while one was open for 0% of the time, Pallas kernels for 13%

profile of v5, /device:TPU:1, one launch (start us, length us, event | category | flops | bytes accessed | tf_op | source)
XLA Modules:
  0.0 68.1 jit_solution(7954230666208939803)
XLA Ops:
  0.7 2.1 %collective-permute-start = (bf16[256,128]{1,0:T(8,128)(2,1)}, bf16[256,128]{1,0:T(8,128)(2,1)S(1)}, u32[]{:S(2)}, u32[]{:S(2)}) collective-permute-start(bf16[256,128]{1,0:T(8,128)(2,1)} %x0.3), channel_id=1, source_target_pairs={{0,32},{32,64},{64,96},{96,0},{1,33},{33,65},{65,97},{97,1},{2,34}... | collective-permute-start | bytes 196616 | tf_op jit(solution)/shard_map/ppermute | solution.py:72
  2.8 1.3 %collective-permute-start.1 = (bf16[256,128]{1,0:T(8,128)(2,1)}, bf16[256,128]{1,0:T(8,128)(2,1)S(1)}, u32[]{:S(2)}, u32[]{:S(2)}) collective-permute-start(bf16[256,128]{1,0:T(8,128)(2,1)} %x0.3), channel_id=1, source_target_pairs={{0,96},{32,0},{64,32},{96,64},{1,97},{33,1},{65,33},{97,65},{2,98}... | collective-permute-start | bytes 196616 | tf_op jit(solution)/shard_map/ppermute | solution.py:72
  4.1 1.6 %collective-permute-start.2 = (bf16[256,128]{1,0:T(8,128)(2,1)}, bf16[256,128]{1,0:T(8,128)(2,1)S(1)}, u32[]{:S(2)}, u32[]{:S(2)}) collective-permute-start(bf16[256,128]{1,0:T(8,128)(2,1)} %x0.3), channel_id=1, source_target_pairs={{0,64},{32,96},{64,0},{96,32},{1,65},{33,97},{65,1},{97,33},{2,66}... | collective-permute-start | bytes 196616 | tf_op jit(solution)/shard_map/ppermute | solution.py:72
  6.4 2.2 %shard_map.112 = (bf16[128,128,128]{2,1,0:T(8,128)(2,1)S(1)}, f32[33,128,128]{2,1,0:T(8,128)S(1)}, f32[33,128,128]{2,1,0:T(8,128)S(1)}) custom-call(bf16[128,128,128]{2,1,0:T(8,128)(2,1)} %bitcast.5), custom_call_target="tpu_custom_call" | custom-call | tf_op jit(solution)/shard_map/pallas_call | solution.py:328
  9.5 2.0 %shard_map.114 = (f32[33,128,128]{2,1,0:T(8,128)S(1)}, bf16[4096,128]{1,0:T(8,128)(2,1)S(1)}) custom-call(s32[1,384]{1,0:T(1,128)S(1)} %get-tuple-element.53.tab, bf16[256,128]{1,0:T(8,128)(2,1)S(1)} %copy-done.2, bf16[256,128]{1,0:T(8,128)(2,1)S(1)} %collective-permute-done.1.x1, ...), custom_call_target="tpu_custom_call", output_to_operand_aliasing={{0}: (6, {})} | custom-call | flops 268435456 | bytes 4194304 | tf_op jit(solution)/shard_map/pallas_call | solution.py:337
  12.9 1.9 %shard_map.113.acc = f32[33,128,128]{2,1,0:T(8,128)S(1)} custom-call(s32[1,384]{1,0:T(1,128)S(1)} %get-tuple-element.53.tab, bf16[256,128]{1,0:T(8,128)(2,1)S(1)} %copy-done.2, bf16[256,128]{1,0:T(8,128)(2,1)S(1)} %collective-permute-done.1.x1, bf16[256,128]{1,0:T(8,128)(2,1)S(1)} %collective-permute-done.2.x2, ...), custom_call_target="tpu_custom_call", output_to_operand_aliasing={{}: (6, {})} | custom-call | tf_op jit(solution)/shard_map/pallas_call | solution.py:346
  15.3 2.0 %collective-permute-start.4 = (bf16[1024,128]{1,0:T(8,128)(2,1)S(1)}, bf16[1024,128]{1,0:T(8,128)(2,1)S(1)}, u32[]{:S(2)}, u32[]{:S(2)}) collective-permute-start(bf16[1024,128]{1,0:T(8,128)(2,1)S(1)} %get-tuple-element.68), channel_id=1, source_target_pairs={{0,3},{1,8},{2,11},{3,4},{4,7},{5,12},{6,15},{7,0},{8,17},{9,10},{... | collective-permute-start | bytes 786440 | tf_op jit(solution)/shard_map/ppermute | solution.py:72
  18.6 1.9 %collective-permute-start.6 = (bf16[1024,128]{1,0:T(8,128)(2,1)S(1)}, bf16[1024,128]{1,0:T(8,128)(2,1)S(1)}, u32[]{:S(2)}, u32[]{:S(2)}) collective-permute-start(bf16[1024,128]{1,0:T(8,128)(2,1)S(1)} %get-tuple-element.70), channel_id=1, source_target_pairs={{0,4},{1,17},{2,18},{3,7},{4,0},{5,21},{6,22},{7,3},{8,24},{9,13},... | collective-permute-start | bytes 786440 | tf_op jit(solution)/shard_map/ppermute | solution.py:72
  20.5 2.4 %collective-permute-done.4.r1 = bf16[1024,128]{1,0:T(8,128)(2,1)S(1)} collective-permute-done((bf16[1024,128]{1,0:T(8,128)(2,1)S(1)}, bf16[1024,128]{1,0:T(8,128)(2,1)S(1)}, u32[]{:S(2)}, u32[]{:S(2)}) %collective-permute-start.4) | collective-permute-done | bytes 262176 | tf_op jit(solution)/shard_map/ppermute | solution.py:72
  23.5 3.1 %collective-permute-done.6.r2 = bf16[1024,128]{1,0:T(8,128)(2,1)S(1)} collective-permute-done((bf16[1024,128]{1,0:T(8,128)(2,1)S(1)}, bf16[1024,128]{1,0:T(8,128)(2,1)S(1)}, u32[]{:S(2)}, u32[]{:S(2)}) %collective-permute-start.6) | collective-permute-done | bytes 262176 | tf_op jit(solution)/shard_map/ppermute | solution.py:72
  26.7 2.9 %collective-permute-start.7 = (bf16[1536,128]{1,0:T(8,128)(2,1)S(1)}, bf16[1536,128]{1,0:T(8,128)(2,1)S(1)}, u32[]{:S(2)}, u32[]{:S(2)}) collective-permute-start(bf16[1536,128]{1,0:T(8,128)(2,1)S(1)} %get-tuple-element.78), channel_id=1, source_target_pairs={{0,9},{1,2},{2,5},{3,10},{4,13},{5,6},{6,1},{7,14},{8,11},{9,16},{... | collective-permute-start | bytes 1179656 | tf_op jit(solution)/shard_map/ppermute | solution.py:72
  29.6 1.6 %collective-permute-start.8 = (bf16[1536,128]{1,0:T(8,128)(2,1)S(1)}, bf16[1536,128]{1,0:T(8,128)(2,1)S(1)}, u32[]{:S(2)}, u32[]{:S(2)}) collective-permute-start(bf16[1536,128]{1,0:T(8,128)(2,1)S(1)} %get-tuple-element.78), channel_id=1, source_target_pairs={{0,25},{1,6},{2,1},{3,26},{4,29},{5,2},{6,5},{7,30},{8,15},{9,0},{... | collective-permute-start | bytes 1179656 | tf_op jit(solution)/shard_map/ppermute | solution.py:72
  32.4 4.1 %collective-permute-done.7.r1 = bf16[1536,128]{1,0:T(8,128)(2,1)S(1)} collective-permute-done((bf16[1536,128]{1,0:T(8,128)(2,1)S(1)}, bf16[1536,128]{1,0:T(8,128)(2,1)S(1)}, u32[]{:S(2)}, u32[]{:S(2)}) %collective-permute-start.7) | collective-permute-done | bytes 393248 | tf_op jit(solution)/shard_map/ppermute | solution.py:72
  37.0 4.8 %collective-permute-done.9.r2 = bf16[1536,128]{1,0:T(8,128)(2,1)S(1)} collective-permute-done((bf16[1536,128]{1,0:T(8,128)(2,1)S(1)}, bf16[1536,128]{1,0:T(8,128)(2,1)S(1)}, u32[]{:S(2)}, u32[]{:S(2)}) %collective-permute-start.9) | collective-permute-done | bytes 393248 | tf_op jit(solution)/shard_map/ppermute | solution.py:72
  42.8 1.5 %collective-permute-start.12 = (bf16[1296,128]{1,0:T(8,128)(2,1)S(1)}, bf16[1296,128]{1,0:T(8,128)(2,1)S(1)}, u32[]{:S(2)}, u32[]{:S(2)}) collective-permute-start(bf16[1296,128]{1,0:T(8,128)(2,1)S(1)} %get-tuple-element.87.refs_0_), channel_id=1, source_target_pairs={{0,3},{1,8},{2,11},{3,4},{4,7},{5,12},{6,15},{7,0},{8,17},{9,10},{... | collective-permute-start | bytes 995336 | tf_op jit(solution)/shard_map/ppermute | solution.py:72
  44.3 2.3 %collective-permute-start.10 = (bf16[1296,128]{1,0:T(8,128)(2,1)S(1)}, bf16[1296,128]{1,0:T(8,128)(2,1)S(1)}, u32[]{:S(2)}, u32[]{:S(2)}) collective-permute-start(bf16[1296,128]{1,0:T(8,128)(2,1)S(1)} %get-tuple-element.87.refs_0_), channel_id=1, source_target_pairs={{0,7},{1,24},{2,27},{3,0},{4,3},{5,28},{6,31},{7,4},{8,1},{9,14},{... | collective-permute-start | bytes 995336 | tf_op jit(solution)/shard_map/ppermute | solution.py:72
  46.6 1.4 %collective-permute-start.11 = (bf16[1296,128]{1,0:T(8,128)(2,1)S(1)}, bf16[1296,128]{1,0:T(8,128)(2,1)S(1)}, u32[]{:S(2)}, u32[]{:S(2)}) collective-permute-start(bf16[1296,128]{1,0:T(8,128)(2,1)S(1)} %get-tuple-element.87.refs_0_), channel_id=1, source_target_pairs={{0,4},{1,17},{2,18},{3,7},{4,0},{5,21},{6,22},{7,3},{8,24},{9,13},... | collective-permute-start | bytes 995336 | tf_op jit(solution)/shard_map/ppermute | solution.py:72
  48.0 2.6 %collective-permute-done.12.refs_1_ = bf16[1296,128]{1,0:T(8,128)(2,1)S(1)} collective-permute-done((bf16[1296,128]{1,0:T(8,128)(2,1)S(1)}, bf16[1296,128]{1,0:T(8,128)(2,1)S(1)}, u32[]{:S(2)}, u32[]{:S(2)}) %collective-permute-start.12) | collective-permute-done | bytes 331808 | tf_op jit(solution)/shard_map/ppermute | solution.py:72
  51.1 1.6 %shard_map.118 = (f32[9,128,128]{2,1,0:T(8,128)S(1)}, f32[272,128]{1,0:T(8,128)S(1)}) custom-call(s32[1,640]{1,0:T(1,128)S(1)} %get-tuple-element.83.tab, bf16[128,128,128]{2,1,0:T(8,128)(2,1)S(1)} %bitcast.6, bf16[1296,128]{1,0:T(8,128)(2,1)S(1)} %get-tuple-element.87.refs_0_, bf16[1296,128]{1,0:T(8,128)(2,1)S(1)} %collective-permute-done.12.refs_1_, ...), custom_call_target="tpu_custom_call" | custom-call | flops 201326592 | bytes 3145728 | tf_op jit(solution)/shard_map/pallas_call | solution.py:373
  52.7 1.6 %collective-permute-done.10.refs_0_ = bf16[1296,128]{1,0:T(8,128)(2,1)S(1)} collective-permute-done((bf16[1296,128]{1,0:T(8,128)(2,1)S(1)}, bf16[1296,128]{1,0:T(8,128)(2,1)S(1)}, u32[]{:S(2)}, u32[]{:S(2)}) %collective-permute-start.10) | collective-permute-done | bytes 331808 | tf_op jit(solution)/shard_map/ppermute | solution.py:72
  55.1 1.6 %shard_map.119 = (f32[9,128,128]{2,1,0:T(8,128)S(1)}, f32[272,128]{1,0:T(8,128)S(1)}) custom-call(s32[1,640]{1,0:T(1,128)S(1)} %get-tuple-element.83.tab, bf16[128,128,128]{2,1,0:T(8,128)(2,1)S(1)} %bitcast.7, bf16[1296,128]{1,0:T(8,128)(2,1)S(1)} %collective-permute-done.10.refs_0_, ...), custom_call_target="tpu_custom_call", output_to_operand_aliasing={{0}: (5, {})} | custom-call | flops 201326592 | bytes 3145728 | tf_op jit(solution)/shard_map/pallas_call | solution.py:373
  58.4 2.0 %collective-permute-start.18 = (bf16[528,128]{1,0:T(8,128)(2,1)S(1)}, bf16[528,128]{1,0:T(8,128)(2,1)S(1)}, u32[]{:S(2)}, u32[]{:S(2)}) collective-permute-start(bf16[528,128]{1,0:T(8,128)(2,1)S(1)} %get-tuple-element.97), channel_id=1, source_target_pairs={{0,96},{32,0},{64,32},{96,64},{1,97},{33,1},{65,33},{97,65},{2,98}... | collective-permute-start | bytes 405512 | tf_op jit(solution)/shard_map/ppermute | solution.py:390
  62.4 1.4 %collective-permute-done.17.r1 = bf16[528,128]{1,0:T(8,128)(2,1)S(1)} collective-permute-done((bf16[528,128]{1,0:T(8,128)(2,1)S(1)}, bf16[528,128]{1,0:T(8,128)(2,1)S(1)}, u32[]{:S(2)}, u32[]{:S(2)}) %collective-permute-start.17) | collective-permute-done | bytes 135200 | tf_op jit(solution)/shard_map/ppermute | solution.py:390
  63.8 3.6 %collective-permute-done.19.r3 = bf16[528,128]{1,0:T(8,128)(2,1)S(1)} collective-permute-done((bf16[528,128]{1,0:T(8,128)(2,1)S(1)}, bf16[528,128]{1,0:T(8,128)(2,1)S(1)}, u32[]{:S(2)}, u32[]{:S(2)}) %collective-permute-start.19) | collective-permute-done | bytes 135200 | tf_op jit(solution)/shard_map/ppermute | solution.py:390
  (42 shorter events, 13.0 us)
Async XLA Ops:
  0.7 8.8 %collective-permute-start = (bf16[256,128]{1,0:T(8,128)(2,1)}, bf16[256,128]{1,0:T(8,128)(2,1)S(1)}, u32[]{:S(2)}, u32[]{:S(2)}) collective-permute-start(bf16[256,128]{1,0:T(8,128)(2,1)} %x0.3), channel_id=1, source_target_pairs={{0,32},{32,64},{64,96},{96,0},{1,33},{33,65},{65,97},{97,1},{2,34}... | collective-permute-start | bytes 196616 | tf_op jit(solution)/shard_map/ppermute | solution.py:72
  2.8 6.7 %collective-permute-start.1 = (bf16[256,128]{1,0:T(8,128)(2,1)}, bf16[256,128]{1,0:T(8,128)(2,1)S(1)}, u32[]{:S(2)}, u32[]{:S(2)}) collective-permute-start(bf16[256,128]{1,0:T(8,128)(2,1)} %x0.3), channel_id=1, source_target_pairs={{0,96},{32,0},{64,32},{96,64},{1,97},{33,1},{65,33},{97,65},{2,98}... | collective-permute-start | bytes 196616 | tf_op jit(solution)/shard_map/ppermute | solution.py:72
  4.1 5.4 %collective-permute-start.2 = (bf16[256,128]{1,0:T(8,128)(2,1)}, bf16[256,128]{1,0:T(8,128)(2,1)S(1)}, u32[]{:S(2)}, u32[]{:S(2)}) collective-permute-start(bf16[256,128]{1,0:T(8,128)(2,1)} %x0.3), channel_id=1, source_target_pairs={{0,64},{32,96},{64,0},{96,32},{1,65},{33,97},{65,1},{97,33},{2,66}... | collective-permute-start | bytes 196616 | tf_op jit(solution)/shard_map/ppermute | solution.py:72
  11.5 3.6 %collective-permute-start.3 = (bf16[4096,128]{1,0:T(8,128)(2,1)S(1)}, bf16[4096,128]{1,0:T(8,128)(2,1)S(1)}, u32[]{:S(2)}, u32[]{:S(2)}) collective-permute-start(bf16[4096,128]{1,0:T(8,128)(2,1)S(1)} %get-tuple-element.63), channel_id=1, source_target_pairs={{0,1},{1,0},{2,3},{3,2},{4,5},{5,4},{6,7},{7,6},{8,9},{9,8},{10,11... | collective-permute-start | bytes 3145736 | tf_op jit(solution)/shard_map/ppermute | solution.py:345
  14.8 11.7 %copy-start.1 = (bf16[256,256]{1,0:T(8,128)(2,1)S(1)}, bf16[256,256]{1,0:T(8,128)(2,1)}, u32[]{:S(2)}) copy-start(bf16[256,256]{1,0:T(8,128)(2,1)} %cot.3) | copy-start | bytes 393220
  14.8 27.0 %copy-start.3 = (bf16[128,256]{1,0:T(8,128)(2,1)S(1)}, bf16[128,256]{1,0:T(8,128)(2,1)}, u32[]{:S(2)}) copy-start(bf16[128,256]{1,0:T(8,128)(2,1)} %weight.1) | copy-start | bytes 196612
  14.8 27.0 %copy-start.4 = (f32[256]{0:T(256)S(1)}, f32[256]{0:T(256)}, u32[]{:S(2)}) copy-start(f32[256]{0:T(256)} %param.10) | copy-start | bytes 3076
  15.2 35.9 %copy-start = (bf16[1,1,128,128,128]{4,3,2,1,0:T(8,128)(2,1)S(1)}, bf16[1,1,128,128,128]{4,3,2,1,0:T(8,128)(2,1)}, u32[]{:S(2)}) copy-start(bf16[1,1,128,128,128]{4,3,2,1,0:T(8,128)(2,1)} %param.11) | copy-start | bytes 12582916
  15.3 7.5 %collective-permute-start.4 = (bf16[1024,128]{1,0:T(8,128)(2,1)S(1)}, bf16[1024,128]{1,0:T(8,128)(2,1)S(1)}, u32[]{:S(2)}, u32[]{:S(2)}) collective-permute-start(bf16[1024,128]{1,0:T(8,128)(2,1)S(1)} %get-tuple-element.68), channel_id=1, source_target_pairs={{0,3},{1,8},{2,11},{3,4},{4,7},{5,12},{6,15},{7,0},{8,17},{9,10},{... | collective-permute-start | bytes 786440 | tf_op jit(solution)/shard_map/ppermute | solution.py:72
  17.4 6.1 %collective-permute-start.5 = (bf16[1024,128]{1,0:T(8,128)(2,1)S(1)}, bf16[1024,128]{1,0:T(8,128)(2,1)S(1)}, u32[]{:S(2)}, u32[]{:S(2)}) collective-permute-start(bf16[1024,128]{1,0:T(8,128)(2,1)S(1)} %get-tuple-element.69), channel_id=1, source_target_pairs={{0,7},{1,24},{2,27},{3,0},{4,3},{5,28},{6,31},{7,4},{8,1},{9,14},{... | collective-permute-start | bytes 786440 | tf_op jit(solution)/shard_map/ppermute | solution.py:72
  18.6 8.0 %collective-permute-start.6 = (bf16[1024,128]{1,0:T(8,128)(2,1)S(1)}, bf16[1024,128]{1,0:T(8,128)(2,1)S(1)}, u32[]{:S(2)}, u32[]{:S(2)}) collective-permute-start(bf16[1024,128]{1,0:T(8,128)(2,1)S(1)} %get-tuple-element.70), channel_id=1, source_target_pairs={{0,4},{1,17},{2,18},{3,7},{4,0},{5,21},{6,22},{7,3},{8,24},{9,13},... | collective-permute-start | bytes 786440 | tf_op jit(solution)/shard_map/ppermute | solution.py:72
  26.7 9.9 %collective-permute-start.7 = (bf16[1536,128]{1,0:T(8,128)(2,1)S(1)}, bf16[1536,128]{1,0:T(8,128)(2,1)S(1)}, u32[]{:S(2)}, u32[]{:S(2)}) collective-permute-start(bf16[1536,128]{1,0:T(8,128)(2,1)S(1)} %get-tuple-element.78), channel_id=1, source_target_pairs={{0,9},{1,2},{2,5},{3,10},{4,13},{5,6},{6,1},{7,14},{8,11},{9,16},{... | collective-permute-start | bytes 1179656 | tf_op jit(solution)/shard_map/ppermute | solution.py:72
  29.6 7.4 %collective-permute-start.8 = (bf16[1536,128]{1,0:T(8,128)(2,1)S(1)}, bf16[1536,128]{1,0:T(8,128)(2,1)S(1)}, u32[]{:S(2)}, u32[]{:S(2)}) collective-permute-start(bf16[1536,128]{1,0:T(8,128)(2,1)S(1)} %get-tuple-element.78), channel_id=1, source_target_pairs={{0,25},{1,6},{2,1},{3,26},{4,29},{5,2},{6,5},{7,30},{8,15},{9,0},{... | collective-permute-start | bytes 1179656 | tf_op jit(solution)/shard_map/ppermute | solution.py:72
  31.2 10.7 %collective-permute-start.9 = (bf16[1536,128]{1,0:T(8,128)(2,1)S(1)}, bf16[1536,128]{1,0:T(8,128)(2,1)S(1)}, u32[]{:S(2)}, u32[]{:S(2)}) collective-permute-start(bf16[1536,128]{1,0:T(8,128)(2,1)S(1)} %get-tuple-element.78), channel_id=1, source_target_pairs={{0,16},{1,5},{2,6},{3,19},{4,20},{5,1},{6,2},{7,23},{8,12},{9,25},... | collective-permute-start | bytes 1179656 | tf_op jit(solution)/shard_map/ppermute | solution.py:72
  42.8 7.8 %collective-permute-start.12 = (bf16[1296,128]{1,0:T(8,128)(2,1)S(1)}, bf16[1296,128]{1,0:T(8,128)(2,1)S(1)}, u32[]{:S(2)}, u32[]{:S(2)}) collective-permute-start(bf16[1296,128]{1,0:T(8,128)(2,1)S(1)} %get-tuple-element.87.refs_0_), channel_id=1, source_target_pairs={{0,3},{1,8},{2,11},{3,4},{4,7},{5,12},{6,15},{7,0},{8,17},{9,10},{... | collective-permute-start | bytes 995336 | tf_op jit(solution)/shard_map/ppermute | solution.py:72
  44.3 6.8 %collective-permute-start.13 = (bf16[1296,128]{1,0:T(8,128)(2,1)S(1)}, bf16[1296,128]{1,0:T(8,128)(2,1)S(1)}, u32[]{:S(2)}, u32[]{:S(2)}) collective-permute-start(bf16[1296,128]{1,0:T(8,128)(2,1)S(1)} %get-tuple-element.87.refs_0_), channel_id=1, source_target_pairs={{0,1},{1,0},{2,3},{3,2},{4,5},{5,4},{6,7},{7,6},{8,9},{9,8},{10,11... | collective-permute-start | bytes 995336 | tf_op jit(solution)/shard_map/ppermute | solution.py:366
  44.3 9.9 %collective-permute-start.10 = (bf16[1296,128]{1,0:T(8,128)(2,1)S(1)}, bf16[1296,128]{1,0:T(8,128)(2,1)S(1)}, u32[]{:S(2)}, u32[]{:S(2)}) collective-permute-start(bf16[1296,128]{1,0:T(8,128)(2,1)S(1)} %get-tuple-element.87.refs_0_), channel_id=1, source_target_pairs={{0,7},{1,24},{2,27},{3,0},{4,3},{5,28},{6,31},{7,4},{8,1},{9,14},{... | collective-permute-start | bytes 995336 | tf_op jit(solution)/shard_map/ppermute | solution.py:72
  46.6 7.9 %collective-permute-start.11 = (bf16[1296,128]{1,0:T(8,128)(2,1)S(1)}, bf16[1296,128]{1,0:T(8,128)(2,1)S(1)}, u32[]{:S(2)}, u32[]{:S(2)}) collective-permute-start(bf16[1296,128]{1,0:T(8,128)(2,1)S(1)} %get-tuple-element.87.refs_0_), channel_id=1, source_target_pairs={{0,4},{1,17},{2,18},{3,7},{4,0},{5,21},{6,22},{7,3},{8,24},{9,13},... | collective-permute-start | bytes 995336 | tf_op jit(solution)/shard_map/ppermute | solution.py:72
  50.7 4.4 %collective-permute-start.16 = (bf16[1296,128]{1,0:T(8,128)(2,1)S(1)}, bf16[1296,128]{1,0:T(8,128)(2,1)S(1)}, u32[]{:S(2)}, u32[]{:S(2)}) collective-permute-start(bf16[1296,128]{1,0:T(8,128)(2,1)S(1)} %collective-permute-done.12.refs_1_), channel_id=1, source_target_pairs={{0,1},{1,0},{2,3},{3,2},{4,5},{5,4},{6,7},{7,6},{8,9},{9,8},{10,11... | collective-permute-start | bytes 995336 | tf_op jit(solution)/shard_map/ppermute | solution.py:366
  54.6 2.1 %collective-permute-start.14 = (bf16[1296,128]{1,0:T(8,128)(2,1)S(1)}, bf16[1296,128]{1,0:T(8,128)(2,1)S(1)}, u32[]{:S(2)}, u32[]{:S(2)}) collective-permute-start(bf16[1296,128]{1,0:T(8,128)(2,1)S(1)} %collective-permute-done.10.refs_0_), channel_id=1, source_target_pairs={{0,1},{1,0},{2,3},{3,2},{4,5},{5,4},{6,7},{7,6},{8,9},{9,8},{10,11... | collective-permute-start | bytes 995336 | tf_op jit(solution)/shard_map/ppermute | solution.py:385
  54.9 1.7 %collective-permute-start.15 = (bf16[1296,128]{1,0:T(8,128)(2,1)S(1)}, bf16[1296,128]{1,0:T(8,128)(2,1)S(1)}, u32[]{:S(2)}, u32[]{:S(2)}) collective-permute-start(bf16[1296,128]{1,0:T(8,128)(2,1)S(1)} %collective-permute-done.11.refs_1_), channel_id=1, source_target_pairs={{0,1},{1,0},{2,3},{3,2},{4,5},{5,4},{6,7},{7,6},{8,9},{9,8},{10,11... | collective-permute-start | bytes 995336 | tf_op jit(solution)/shard_map/ppermute | solution.py:385
  57.7 6.1 %collective-permute-start.17 = (bf16[528,128]{1,0:T(8,128)(2,1)S(1)}, bf16[528,128]{1,0:T(8,128)(2,1)S(1)}, u32[]{:S(2)}, u32[]{:S(2)}) collective-permute-start(bf16[528,128]{1,0:T(8,128)(2,1)S(1)} %get-tuple-element.96), channel_id=1, source_target_pairs={{0,32},{32,64},{64,96},{96,0},{1,33},{33,65},{65,97},{97,1},{2,34}... | collective-permute-start | bytes 405512 | tf_op jit(solution)/shard_map/ppermute | solution.py:390
  58.4 5.4 %collective-permute-start.18 = (bf16[528,128]{1,0:T(8,128)(2,1)S(1)}, bf16[528,128]{1,0:T(8,128)(2,1)S(1)}, u32[]{:S(2)}, u32[]{:S(2)}) collective-permute-start(bf16[528,128]{1,0:T(8,128)(2,1)S(1)} %get-tuple-element.97), channel_id=1, source_target_pairs={{0,96},{32,0},{64,32},{96,64},{1,97},{33,1},{65,33},{97,65},{2,98}... | collective-permute-start | bytes 405512 | tf_op jit(solution)/shard_map/ppermute | solution.py:390
  60.4 6.9 %collective-permute-start.19 = (bf16[528,128]{1,0:T(8,128)(2,1)S(1)}, bf16[528,128]{1,0:T(8,128)(2,1)S(1)}, u32[]{:S(2)}, u32[]{:S(2)}) collective-permute-start(bf16[528,128]{1,0:T(8,128)(2,1)S(1)} %get-tuple-element.98), channel_id=1, source_target_pairs={{0,64},{32,96},{64,0},{96,32},{1,65},{33,97},{65,1},{97,33},{2,66}... | collective-permute-start | bytes 405512 | tf_op jit(solution)/shard_map/ppermute | solution.py:390
  (3 other events, 24.9 us)

commit v6 on v5

--- a/solution.py
+++ b/solution.py
@@ -74,6 +74,7 @@
 
 
 ORDER = (1, 3, 2)
+FAR_FIRST = (2, 1, 3)
 
 
 def sort_tiles(rows, cols, count, forward_tab, backward_tab):
@@ -92,7 +93,7 @@
     slot = lax.broadcasted_iota(jnp.int32, (1, 128), 1)
 
     def table(key, keys, take, to, pad, width):
-        key = jnp.where(slot < count[0, 0], key, keys)
+        key = jnp.where(slot < count[...], key, keys)
         is_key = [jnp.where(key == k, 1.0, 0.0) for k in range(keys)]
         is_key = jnp.concatenate(is_key + [jnp.zeros((8 - keys, 128), F32)]).astype(BF16)
         low = lax.broadcasted_iota(jnp.int32, (128, 128), 0)
@@ -164,15 +165,8 @@
 
 
 def forward_tiles(key, tab, x0, x1, x2, x3, adj, _, acc, *refs):
-    *out, xs, sem = refs
-    copies = [
-        pltpu.make_async_copy(x0.at[pl.ds(k * B, B)], xs.at[k], sem.at[k]) for k in range(2)
-    ]
-    for copy in copies:
-        copy.start()
-    load_blocks([x1, x2, x3], 256, xs.at[pl.ds(2, 6)])
-    for copy in copies:
-        copy.wait()
+    *out, xs = refs
+    load_blocks([x0, x1, x2, x3], 256, xs)
     each_tile(tab, key, 2, adj, lambda t, i: jnp.dot(t, xs[i], preferred_element_type=F32), acc)
     if key == 0:
 
@@ -322,7 +316,7 @@
     forward_tab, backward_tab = call(
         sort_tiles,
         (sds(1, TAB, jnp.int32), sds(1, BACKWARD_TAB, jnp.int32)),
-        [VMEM, VMEM, SMEM],
+        [VMEM] * 3,
     )(tile_rows[0], tile_cols[0], tile_count)
     half = jax.ShapeDtypeStruct((33, B, B), F32)
     tiles, acc0, acc1 = call(
@@ -333,11 +327,11 @@
         limit=43,
     )(adj)
     xs = (features, x3, x2, x1)
-    scratch = [pltpu.VMEM((8, B, B), BF16), pltpu.SemaphoreType.DMA((2,))]
+    scratch = [pltpu.VMEM((8, B, B), BF16)]
     _, other = call(
         functools.partial(forward_tiles, 0),
         (half, sds(4096)),
-        [SMEM, ANY] + [VMEM] * 5,
+        [SMEM] + [VMEM] * 6,
         scratch,
         tiles=64,
         aliases={6: 0},
@@ -346,16 +340,16 @@
     acc = call(
         functools.partial(forward_tiles, 1),
         half,
-        [SMEM, ANY] + [VMEM] * 5,
+        [SMEM] + [VMEM] * 6,
         scratch,
         aliases={6: 0},
     )(forward_tab, *xs, tiles, acc1)
     ms = call(core_sum, (sds(1024, dtype=F32),) + (sds(1024),) * 3, [VMEM] * 2)(acc, got)
-    r1, r3, r2 = permute([ms[d] for d in ORDER], "col", [col_shift(True, d) for d in ORDER])
+    r2, r1, r3 = permute([ms[d] for d in FAR_FIRST], "col", [col_shift(True, d) for d in FAR_FIRST])
     total, msg = call(first_sum, (sds(1024, dtype=F32), sds(1536)), [VMEM] * 5)(
         ms[0], r1, r2, r3, cotangent
     )
-    r1, r3, r2 = permute([msg] * 3, "col", [col_shift(False, d) for d in ORDER])
+    r2, r1, r3 = permute([msg] * 3, "col", [col_shift(False, d) for d in FAR_FIRST])
     act, msg = call(local, (sds(256, 256), sds(1024 + TAIL)), [VMEM] * 7)(
         total, r1, r2, r3, weight, bias_vector.reshape(1, 256), cotangent
     )

time: 68.8 us -> 68.1 us (0.990)
  waiting for transfers between devices: 25.3 us -> 21.9 us
  starting transfers between devices: 27.1 us -> 29.8 us
  Pallas kernels: 14.2 us -> 14.9 us
    ppermute x12, waiting for transfers between devices: 20 us -> 17.3 us  [permute(): moved = [lax.ppermute(a, axis, p) for a, p in zip(arrays, pairs)]]
    ppermute x12, starting transfers between devices: 21.1 us -> 23 us  [permute(): moved = [lax.ppermute(a, axis, p) for a, p in zip(arrays, pairs)]]
    ppermute x4, starting transfers between devices: 0.91 us -> 1.71 us  [on_device(): theirs[k] = lax.ppermute(mine[k], 'col', core_swap())]
  transfers between devices with their start and end apart: 20 -> 20, of which waited for: 12 -> 13; matrix products, arithmetic and copies ran while one was open for 0% -> 0% of each run, Pallas kernels for 13% -> 14%
where the time goes in v6:
time: 68.1 us
  starting transfers between devices  29.8 us (44%)
  waiting for transfers between devices  21.9 us (32%)
  Pallas kernels  14.9 us (22%)
  between operations  1.49 us (2%)
    ppermute x12, starting transfers between devices, permute(): moved = [lax.ppermute(a, axis, p) for a, p in zip(arrays, pairs)]  23 us
    ppermute x12, waiting for transfers between devices, permute(): moved = [lax.ppermute(a, axis, p) for a, p in zip(arrays, pairs)]  17.3 us
    pallas_call x4, Pallas kernels, backward(): call(functools.partial(backward_tiles, key, places), outs, [SMEM] + [VMEM...  5.75 us
    ppermute x3, waiting for transfers between devices, on_device(): rs = [lax.ppermute(a, 'row', row_shift(d)) for a, d in zip(ms, ORDER)]  4.4 us
    ppermute x3, starting transfers between devices, on_device(): rs = [lax.ppermute(a, 'row', row_shift(d)) for a, d in zip(ms, ORDER)]  3.49 us
    pallas_call x1, Pallas kernels, on_device(): call(hold, (jax.ShapeDtypeStruct((128, B, B), BF16), half, half), [ANY],...  2.22 us
    pallas_call x1, Pallas kernels, on_device(): call(functools.partial(forward_tiles, 1), half, [SMEM] + [VMEM] * 6, scra...  2.11 us
    pallas_call x1, Pallas kernels, on_device(): call(functools.partial(forward_tiles, 0), (half, sds(4096)), [SMEM] + [VM...  1.93 us
  transfers between devices with their start and end apart: 20, of which 13 were waited for; matrix products, arithmetic and copies ran while one was open for 0% of the time, Pallas kernels for 14%

profile of v6, /device:TPU:1, one launch (start us, length us, event | category | flops | bytes accessed | tf_op | source)
XLA Modules:
  0.0 68.1 jit_solution(6309347616337915339)
XLA Ops:
  0.7 2.1 %collective-permute-start = (bf16[256,128]{1,0:T(8,128)(2,1)}, bf16[256,128]{1,0:T(8,128)(2,1)S(1)}, u32[]{:S(2)}, u32[]{:S(2)}) collective-permute-start(bf16[256,128]{1,0:T(8,128)(2,1)} %x0.3), channel_id=1, source_target_pairs={{0,32},{32,64},{64,96},{96,0},{1,33},{33,65},{65,97},{97,1},{2,34}... | collective-permute-start | bytes 196616 | tf_op jit(solution)/shard_map/ppermute | solution.py:72
  2.8 1.3 %collective-permute-start.1 = (bf16[256,128]{1,0:T(8,128)(2,1)}, bf16[256,128]{1,0:T(8,128)(2,1)S(1)}, u32[]{:S(2)}, u32[]{:S(2)}) collective-permute-start(bf16[256,128]{1,0:T(8,128)(2,1)} %x0.3), channel_id=1, source_target_pairs={{0,96},{32,0},{64,32},{96,64},{1,97},{33,1},{65,33},{97,65},{2,98}... | collective-permute-start | bytes 196616 | tf_op jit(solution)/shard_map/ppermute | solution.py:72
  4.1 1.6 %collective-permute-start.2 = (bf16[256,128]{1,0:T(8,128)(2,1)}, bf16[256,128]{1,0:T(8,128)(2,1)S(1)}, u32[]{:S(2)}, u32[]{:S(2)}) collective-permute-start(bf16[256,128]{1,0:T(8,128)(2,1)} %x0.3), channel_id=1, source_target_pairs={{0,64},{32,96},{64,0},{96,32},{1,65},{33,97},{65,1},{97,33},{2,66}... | collective-permute-start | bytes 196616 | tf_op jit(solution)/shard_map/ppermute | solution.py:72
  6.4 2.2 %shard_map.112 = (bf16[128,128,128]{2,1,0:T(8,128)(2,1)S(1)}, f32[33,128,128]{2,1,0:T(8,128)S(1)}, f32[33,128,128]{2,1,0:T(8,128)S(1)}) custom-call(bf16[128,128,128]{2,1,0:T(8,128)(2,1)} %bitcast.5), custom_call_target="tpu_custom_call" | custom-call | tf_op jit(solution)/shard_map/pallas_call | solution.py:322
  9.5 1.9 %shard_map.114 = (f32[33,128,128]{2,1,0:T(8,128)S(1)}, bf16[4096,128]{1,0:T(8,128)(2,1)S(1)}) custom-call(s32[1,384]{1,0:T(1,128)S(1)} %get-tuple-element.53.tab, bf16[256,128]{1,0:T(8,128)(2,1)S(1)} %copy-done.2, bf16[256,128]{1,0:T(8,128)(2,1)S(1)} %collective-permute-done.1.x1, ...), custom_call_target="tpu_custom_call", output_to_operand_aliasing={{0}: (6, {})} | custom-call | flops 268435456 | bytes 4194304 | tf_op jit(solution)/shard_map/pallas_call | solution.py:331
  11.5 1.6 %collective-permute-start.3 = (bf16[4096,128]{1,0:T(8,128)(2,1)S(1)}, bf16[4096,128]{1,0:T(8,128)(2,1)S(1)}, u32[]{:S(2)}, u32[]{:S(2)}) collective-permute-start(bf16[4096,128]{1,0:T(8,128)(2,1)S(1)} %get-tuple-element.63), channel_id=1, source_target_pairs={{0,1},{1,0},{2,3},{3,2},{4,5},{5,4},{6,7},{7,6},{8,9},{9,8},{10,11... | collective-permute-start | bytes 3145736 | tf_op jit(solution)/shard_map/ppermute | solution.py:339
  13.1 2.1 %shard_map.113.acc = f32[33,128,128]{2,1,0:T(8,128)S(1)} custom-call(s32[1,384]{1,0:T(1,128)S(1)} %get-tuple-element.53.tab, bf16[256,128]{1,0:T(8,128)(2,1)S(1)} %copy-done.2, bf16[256,128]{1,0:T(8,128)(2,1)S(1)} %collective-permute-done.1.x1, bf16[256,128]{1,0:T(8,128)(2,1)S(1)} %collective-permute-done.2.x2, ...), custom_call_target="tpu_custom_call", output_to_operand_aliasing={{}: (6, {})} | custom-call | tf_op jit(solution)/shard_map/pallas_call | solution.py:340
  15.5 3.4 %collective-permute-start.4 = (bf16[1024,128]{1,0:T(8,128)(2,1)S(1)}, bf16[1024,128]{1,0:T(8,128)(2,1)S(1)}, u32[]{:S(2)}, u32[]{:S(2)}) collective-permute-start(bf16[1024,128]{1,0:T(8,128)(2,1)S(1)} %get-tuple-element.68), channel_id=1, source_target_pairs={{0,4},{1,17},{2,18},{3,7},{4,0},{5,21},{6,22},{7,3},{8,24},{9,13},... | collective-permute-start | bytes 786440 | tf_op jit(solution)/shard_map/ppermute | solution.py:72
  19.3 2.6 %collective-permute-start.6 = (bf16[1024,128]{1,0:T(8,128)(2,1)S(1)}, bf16[1024,128]{1,0:T(8,128)(2,1)S(1)}, u32[]{:S(2)}, u32[]{:S(2)}) collective-permute-start(bf16[1024,128]{1,0:T(8,128)(2,1)S(1)} %get-tuple-element.70), channel_id=1, source_target_pairs={{0,7},{1,24},{2,27},{3,0},{4,3},{5,28},{6,31},{7,4},{8,1},{9,14},{... | collective-permute-start | bytes 786440 | tf_op jit(solution)/shard_map/ppermute | solution.py:72
  23.0 3.2 %collective-permute-done.5.r1 = bf16[1024,128]{1,0:T(8,128)(2,1)S(1)} collective-permute-done((bf16[1024,128]{1,0:T(8,128)(2,1)S(1)}, bf16[1024,128]{1,0:T(8,128)(2,1)S(1)}, u32[]{:S(2)}, u32[]{:S(2)}) %collective-permute-start.5) | collective-permute-done | bytes 262176 | tf_op jit(solution)/shard_map/ppermute | solution.py:72
  26.5 3.7 %collective-permute-start.7 = (bf16[1536,128]{1,0:T(8,128)(2,1)S(1)}, bf16[1536,128]{1,0:T(8,128)(2,1)S(1)}, u32[]{:S(2)}, u32[]{:S(2)}) collective-permute-start(bf16[1536,128]{1,0:T(8,128)(2,1)S(1)} %get-tuple-element.78), channel_id=1, source_target_pairs={{0,16},{1,5},{2,6},{3,19},{4,20},{5,1},{6,2},{7,23},{8,12},{9,25},... | collective-permute-start | bytes 1179656 | tf_op jit(solution)/shard_map/ppermute | solution.py:72
  31.2 2.0 %collective-permute-start.9 = (bf16[1536,128]{1,0:T(8,128)(2,1)S(1)}, bf16[1536,128]{1,0:T(8,128)(2,1)S(1)}, u32[]{:S(2)}, u32[]{:S(2)}) collective-permute-start(bf16[1536,128]{1,0:T(8,128)(2,1)S(1)} %get-tuple-element.78), channel_id=1, source_target_pairs={{0,25},{1,6},{2,1},{3,26},{4,29},{5,2},{6,5},{7,30},{8,15},{9,0},{... | collective-permute-start | bytes 1179656 | tf_op jit(solution)/shard_map/ppermute | solution.py:72
  33.2 2.5 %collective-permute-done.7.r2 = bf16[1536,128]{1,0:T(8,128)(2,1)S(1)} collective-permute-done((bf16[1536,128]{1,0:T(8,128)(2,1)S(1)}, bf16[1536,128]{1,0:T(8,128)(2,1)S(1)}, u32[]{:S(2)}, u32[]{:S(2)}) %collective-permute-start.7) | collective-permute-done | bytes 393248 | tf_op jit(solution)/shard_map/ppermute | solution.py:72
  35.7 4.2 %collective-permute-done.8.r1 = bf16[1536,128]{1,0:T(8,128)(2,1)S(1)} collective-permute-done((bf16[1536,128]{1,0:T(8,128)(2,1)S(1)}, bf16[1536,128]{1,0:T(8,128)(2,1)S(1)}, u32[]{:S(2)}, u32[]{:S(2)}) %collective-permute-start.8) | collective-permute-done | bytes 393248 | tf_op jit(solution)/shard_map/ppermute | solution.py:72
  41.9 1.2 %collective-permute-start.12 = (bf16[1296,128]{1,0:T(8,128)(2,1)S(1)}, bf16[1296,128]{1,0:T(8,128)(2,1)S(1)}, u32[]{:S(2)}, u32[]{:S(2)}) collective-permute-start(bf16[1296,128]{1,0:T(8,128)(2,1)S(1)} %get-tuple-element.87.refs_0_), channel_id=1, source_target_pairs={{0,3},{1,8},{2,11},{3,4},{4,7},{5,12},{6,15},{7,0},{8,17},{9,10},{... | collective-permute-start | bytes 995336 | tf_op jit(solution)/shard_map/ppermute | solution.py:72
  43.5 2.7 %collective-permute-start.10 = (bf16[1296,128]{1,0:T(8,128)(2,1)S(1)}, bf16[1296,128]{1,0:T(8,128)(2,1)S(1)}, u32[]{:S(2)}, u32[]{:S(2)}) collective-permute-start(bf16[1296,128]{1,0:T(8,128)(2,1)S(1)} %get-tuple-element.87.refs_0_), channel_id=1, source_target_pairs={{0,7},{1,24},{2,27},{3,0},{4,3},{5,28},{6,31},{7,4},{8,1},{9,14},{... | collective-permute-start | bytes 995336 | tf_op jit(solution)/shard_map/ppermute | solution.py:72
  47.2 2.6 %collective-permute-done.12.refs_1_ = bf16[1296,128]{1,0:T(8,128)(2,1)S(1)} collective-permute-done((bf16[1296,128]{1,0:T(8,128)(2,1)S(1)}, bf16[1296,128]{1,0:T(8,128)(2,1)S(1)}, u32[]{:S(2)}, u32[]{:S(2)}) %collective-permute-start.12) | collective-permute-done | bytes 331808 | tf_op jit(solution)/shard_map/ppermute | solution.py:72
  49.9 1.6 %shard_map.118 = (f32[9,128,128]{2,1,0:T(8,128)S(1)}, f32[272,128]{1,0:T(8,128)S(1)}) custom-call(s32[1,640]{1,0:T(1,128)S(1)} %get-tuple-element.83.tab, bf16[128,128,128]{2,1,0:T(8,128)(2,1)S(1)} %bitcast.6, bf16[1296,128]{1,0:T(8,128)(2,1)S(1)} %get-tuple-element.87.refs_0_, bf16[1296,128]{1,0:T(8,128)(2,1)S(1)} %collective-permute-done.12.refs_1_, ...), custom_call_target="tpu_custom_call" | custom-call | flops 201326592 | bytes 3145728 | tf_op jit(solution)/shard_map/pallas_call | solution.py:367
  51.5 2.3 %collective-permute-done.10.refs_0_ = bf16[1296,128]{1,0:T(8,128)(2,1)S(1)} collective-permute-done((bf16[1296,128]{1,0:T(8,128)(2,1)S(1)}, bf16[1296,128]{1,0:T(8,128)(2,1)S(1)}, u32[]{:S(2)}, u32[]{:S(2)}) %collective-permute-start.10) | collective-permute-done | bytes 331808 | tf_op jit(solution)/shard_map/ppermute | solution.py:72
  55.2 1.9 %shard_map.119 = (f32[9,128,128]{2,1,0:T(8,128)S(1)}, f32[272,128]{1,0:T(8,128)S(1)}) custom-call(s32[1,640]{1,0:T(1,128)S(1)} %get-tuple-element.83.tab, bf16[128,128,128]{2,1,0:T(8,128)(2,1)S(1)} %bitcast.7, bf16[1296,128]{1,0:T(8,128)(2,1)S(1)} %collective-permute-done.10.refs_0_, ...), custom_call_target="tpu_custom_call", output_to_operand_aliasing={{0}: (5, {})} | custom-call | flops 201326592 | bytes 3145728 | tf_op jit(solution)/shard_map/pallas_call | solution.py:367
  57.1 1.3 %shard_map.121 = (bf16[528,128]{1,0:T(8,128)(2,1)S(1)}, bf16[528,128]{1,0:T(8,128)(2,1)S(1)}, bf16[528,128]{1,0:T(8,128)(2,1)S(1)}) custom-call(s32[1,640]{1,0:T(1,128)S(1)} %get-tuple-element.83.tab, bf16[128,128,128]{2,1,0:T(8,128)(2,1)S(1)} %bitcast.8, bf16[1296,128]{1,0:T(8,128)(2,1)S(1)} %collective-permute-done.14.refs_0_, ...), custom_call_target="tpu_custom_call" | custom-call | flops 67108864 | bytes 1048576 | tf_op jit(solution)/shard_map/pallas_call | solution.py:367
  58.5 2.7 %collective-permute-start.18 = (bf16[528,128]{1,0:T(8,128)(2,1)S(1)}, bf16[528,128]{1,0:T(8,128)(2,1)S(1)}, u32[]{:S(2)}, u32[]{:S(2)}) collective-permute-start(bf16[528,128]{1,0:T(8,128)(2,1)S(1)} %get-tuple-element.97), channel_id=1, source_target_pairs={{0,96},{32,0},{64,32},{96,64},{1,97},{33,1},{65,33},{97,65},{2,98}... | collective-permute-start | bytes 405512 | tf_op jit(solution)/shard_map/ppermute | solution.py:384
  62.9 1.8 %collective-permute-done.17.r1 = bf16[528,128]{1,0:T(8,128)(2,1)S(1)} collective-permute-done((bf16[528,128]{1,0:T(8,128)(2,1)S(1)}, bf16[528,128]{1,0:T(8,128)(2,1)S(1)}, u32[]{:S(2)}, u32[]{:S(2)}) %collective-permute-start.17) | collective-permute-done | bytes 135200 | tf_op jit(solution)/shard_map/ppermute | solution.py:384
  64.7 1.8 %collective-permute-done.18.r2 = bf16[528,128]{1,0:T(8,128)(2,1)S(1)} collective-permute-done((bf16[528,128]{1,0:T(8,128)(2,1)S(1)}, bf16[528,128]{1,0:T(8,128)(2,1)S(1)}, u32[]{:S(2)}, u32[]{:S(2)}) %collective-permute-start.18) | collective-permute-done | bytes 135200 | tf_op jit(solution)/shard_map/ppermute | solution.py:384
  (42 shorter events, 12.1 us)
Async XLA Ops:
  0.7 8.8 %collective-permute-start = (bf16[256,128]{1,0:T(8,128)(2,1)}, bf16[256,128]{1,0:T(8,128)(2,1)S(1)}, u32[]{:S(2)}, u32[]{:S(2)}) collective-permute-start(bf16[256,128]{1,0:T(8,128)(2,1)} %x0.3), channel_id=1, source_target_pairs={{0,32},{32,64},{64,96},{96,0},{1,33},{33,65},{65,97},{97,1},{2,34}... | collective-permute-start | bytes 196616 | tf_op jit(solution)/shard_map/ppermute | solution.py:72
  2.8 6.7 %collective-permute-start.1 = (bf16[256,128]{1,0:T(8,128)(2,1)}, bf16[256,128]{1,0:T(8,128)(2,1)S(1)}, u32[]{:S(2)}, u32[]{:S(2)}) collective-permute-start(bf16[256,128]{1,0:T(8,128)(2,1)} %x0.3), channel_id=1, source_target_pairs={{0,96},{32,0},{64,32},{96,64},{1,97},{33,1},{65,33},{97,65},{2,98}... | collective-permute-start | bytes 196616 | tf_op jit(solution)/shard_map/ppermute | solution.py:72
  4.1 5.4 %collective-permute-start.2 = (bf16[256,128]{1,0:T(8,128)(2,1)}, bf16[256,128]{1,0:T(8,128)(2,1)S(1)}, u32[]{:S(2)}, u32[]{:S(2)}) collective-permute-start(bf16[256,128]{1,0:T(8,128)(2,1)} %x0.3), channel_id=1, source_target_pairs={{0,64},{32,96},{64,0},{96,32},{1,65},{33,97},{65,1},{97,33},{2,66}... | collective-permute-start | bytes 196616 | tf_op jit(solution)/shard_map/ppermute | solution.py:72
  11.5 3.9 %collective-permute-start.3 = (bf16[4096,128]{1,0:T(8,128)(2,1)S(1)}, bf16[4096,128]{1,0:T(8,128)(2,1)S(1)}, u32[]{:S(2)}, u32[]{:S(2)}) collective-permute-start(bf16[4096,128]{1,0:T(8,128)(2,1)S(1)} %get-tuple-element.63), channel_id=1, source_target_pairs={{0,1},{1,0},{2,3},{3,2},{4,5},{5,4},{6,7},{7,6},{8,9},{9,8},{10,11... | collective-permute-start | bytes 3145736 | tf_op jit(solution)/shard_map/ppermute | solution.py:339
  15.2 11.2 %copy-start.1 = (bf16[256,256]{1,0:T(8,128)(2,1)S(1)}, bf16[256,256]{1,0:T(8,128)(2,1)}, u32[]{:S(2)}) copy-start(bf16[256,256]{1,0:T(8,128)(2,1)} %cot.3) | copy-start | bytes 393220
  15.2 25.7 %copy-start.3 = (bf16[128,256]{1,0:T(8,128)(2,1)S(1)}, bf16[128,256]{1,0:T(8,128)(2,1)}, u32[]{:S(2)}) copy-start(bf16[128,256]{1,0:T(8,128)(2,1)} %weight.1) | copy-start | bytes 196612
  15.2 25.7 %copy-start.4 = (f32[256]{0:T(256)S(1)}, f32[256]{0:T(256)}, u32[]{:S(2)}) copy-start(f32[256]{0:T(256)} %param.10) | copy-start | bytes 3076
  15.4 34.5 %copy-start = (bf16[1,1,128,128,128]{4,3,2,1,0:T(8,128)(2,1)S(1)}, bf16[1,1,128,128,128]{4,3,2,1,0:T(8,128)(2,1)}, u32[]{:S(2)}) copy-start(bf16[1,1,128,128,128]{4,3,2,1,0:T(8,128)(2,1)} %param.11) | copy-start | bytes 12582916
  15.5 7.4 %collective-permute-start.4 = (bf16[1024,128]{1,0:T(8,128)(2,1)S(1)}, bf16[1024,128]{1,0:T(8,128)(2,1)S(1)}, u32[]{:S(2)}, u32[]{:S(2)}) collective-permute-start(bf16[1024,128]{1,0:T(8,128)(2,1)S(1)} %get-tuple-element.68), channel_id=1, source_target_pairs={{0,4},{1,17},{2,18},{3,7},{4,0},{5,21},{6,22},{7,3},{8,24},{9,13},... | collective-permute-start | bytes 786440 | tf_op jit(solution)/shard_map/ppermute | solution.py:72
  18.9 7.3 %collective-permute-start.5 = (bf16[1024,128]{1,0:T(8,128)(2,1)S(1)}, bf16[1024,128]{1,0:T(8,128)(2,1)S(1)}, u32[]{:S(2)}, u32[]{:S(2)}) collective-permute-start(bf16[1024,128]{1,0:T(8,128)(2,1)S(1)} %get-tuple-element.69), channel_id=1, source_target_pairs={{0,3},{1,8},{2,11},{3,4},{4,7},{5,12},{6,15},{7,0},{8,17},{9,10},{... | collective-permute-start | bytes 786440 | tf_op jit(solution)/shard_map/ppermute | solution.py:72
  19.3 7.2 %collective-permute-start.6 = (bf16[1024,128]{1,0:T(8,128)(2,1)S(1)}, bf16[1024,128]{1,0:T(8,128)(2,1)S(1)}, u32[]{:S(2)}, u32[]{:S(2)}) collective-permute-start(bf16[1024,128]{1,0:T(8,128)(2,1)S(1)} %get-tuple-element.70), channel_id=1, source_target_pairs={{0,7},{1,24},{2,27},{3,0},{4,3},{5,28},{6,31},{7,4},{8,1},{9,14},{... | collective-permute-start | bytes 786440 | tf_op jit(solution)/shard_map/ppermute | solution.py:72
  26.5 9.2 %collective-permute-start.7 = (bf16[1536,128]{1,0:T(8,128)(2,1)S(1)}, bf16[1536,128]{1,0:T(8,128)(2,1)S(1)}, u32[]{:S(2)}, u32[]{:S(2)}) collective-permute-start(bf16[1536,128]{1,0:T(8,128)(2,1)S(1)} %get-tuple-element.78), channel_id=1, source_target_pairs={{0,16},{1,5},{2,6},{3,19},{4,20},{5,1},{6,2},{7,23},{8,12},{9,25},... | collective-permute-start | bytes 1179656 | tf_op jit(solution)/shard_map/ppermute | solution.py:72
  30.2 9.7 %collective-permute-start.8 = (bf16[1536,128]{1,0:T(8,128)(2,1)S(1)}, bf16[1536,128]{1,0:T(8,128)(2,1)S(1)}, u32[]{:S(2)}, u32[]{:S(2)}) collective-permute-start(bf16[1536,128]{1,0:T(8,128)(2,1)S(1)} %get-tuple-element.78), channel_id=1, source_target_pairs={{0,9},{1,2},{2,5},{3,10},{4,13},{5,6},{6,1},{7,14},{8,11},{9,16},{... | collective-permute-start | bytes 1179656 | tf_op jit(solution)/shard_map/ppermute | solution.py:72
  31.2 9.7 %collective-permute-start.9 = (bf16[1536,128]{1,0:T(8,128)(2,1)S(1)}, bf16[1536,128]{1,0:T(8,128)(2,1)S(1)}, u32[]{:S(2)}, u32[]{:S(2)}) collective-permute-start(bf16[1536,128]{1,0:T(8,128)(2,1)S(1)} %get-tuple-element.78), channel_id=1, source_target_pairs={{0,25},{1,6},{2,1},{3,26},{4,29},{5,2},{6,5},{7,30},{8,15},{9,0},{... | collective-permute-start | bytes 1179656 | tf_op jit(solution)/shard_map/ppermute | solution.py:72
  41.9 7.8 %collective-permute-start.12 = (bf16[1296,128]{1,0:T(8,128)(2,1)S(1)}, bf16[1296,128]{1,0:T(8,128)(2,1)S(1)}, u32[]{:S(2)}, u32[]{:S(2)}) collective-permute-start(bf16[1296,128]{1,0:T(8,128)(2,1)S(1)} %get-tuple-element.87.refs_0_), channel_id=1, source_target_pairs={{0,3},{1,8},{2,11},{3,4},{4,7},{5,12},{6,15},{7,0},{8,17},{9,10},{... | collective-permute-start | bytes 995336 | tf_op jit(solution)/shard_map/ppermute | solution.py:72
  43.1 6.8 %collective-permute-start.13 = (bf16[1296,128]{1,0:T(8,128)(2,1)S(1)}, bf16[1296,128]{1,0:T(8,128)(2,1)S(1)}, u32[]{:S(2)}, u32[]{:S(2)}) collective-permute-start(bf16[1296,128]{1,0:T(8,128)(2,1)S(1)} %get-tuple-element.87.refs_0_), channel_id=1, source_target_pairs={{0,1},{1,0},{2,3},{3,2},{4,5},{5,4},{6,7},{7,6},{8,9},{9,8},{10,11... | collective-permute-start | bytes 995336 | tf_op jit(solution)/shard_map/ppermute | solution.py:360
  43.5 10.3 %collective-permute-start.10 = (bf16[1296,128]{1,0:T(8,128)(2,1)S(1)}, bf16[1296,128]{1,0:T(8,128)(2,1)S(1)}, u32[]{:S(2)}, u32[]{:S(2)}) collective-permute-start(bf16[1296,128]{1,0:T(8,128)(2,1)S(1)} %get-tuple-element.87.refs_0_), channel_id=1, source_target_pairs={{0,7},{1,24},{2,27},{3,0},{4,3},{5,28},{6,31},{7,4},{8,1},{9,14},{... | collective-permute-start | bytes 995336 | tf_op jit(solution)/shard_map/ppermute | solution.py:72
  46.2 7.9 %collective-permute-start.11 = (bf16[1296,128]{1,0:T(8,128)(2,1)S(1)}, bf16[1296,128]{1,0:T(8,128)(2,1)S(1)}, u32[]{:S(2)}, u32[]{:S(2)}) collective-permute-start(bf16[1296,128]{1,0:T(8,128)(2,1)S(1)} %get-tuple-element.87.refs_0_), channel_id=1, source_target_pairs={{0,4},{1,17},{2,18},{3,7},{4,0},{5,21},{6,22},{7,3},{8,24},{9,13},... | collective-permute-start | bytes 995336 | tf_op jit(solution)/shard_map/ppermute | solution.py:72
  49.7 5.5 %collective-permute-start.16 = (bf16[1296,128]{1,0:T(8,128)(2,1)S(1)}, bf16[1296,128]{1,0:T(8,128)(2,1)S(1)}, u32[]{:S(2)}, u32[]{:S(2)}) collective-permute-start(bf16[1296,128]{1,0:T(8,128)(2,1)S(1)} %collective-permute-done.12.refs_1_), channel_id=1, source_target_pairs={{0,1},{1,0},{2,3},{3,2},{4,5},{5,4},{6,7},{7,6},{8,9},{9,8},{10,11... | collective-permute-start | bytes 995336 | tf_op jit(solution)/shard_map/ppermute | solution.py:360
  54.1 3.0 %collective-permute-start.14 = (bf16[1296,128]{1,0:T(8,128)(2,1)S(1)}, bf16[1296,128]{1,0:T(8,128)(2,1)S(1)}, u32[]{:S(2)}, u32[]{:S(2)}) collective-permute-start(bf16[1296,128]{1,0:T(8,128)(2,1)S(1)} %collective-permute-done.10.refs_0_), channel_id=1, source_target_pairs={{0,1},{1,0},{2,3},{3,2},{4,5},{5,4},{6,7},{7,6},{8,9},{9,8},{10,11... | collective-permute-start | bytes 995336 | tf_op jit(solution)/shard_map/ppermute | solution.py:379
  55.2 1.9 %collective-permute-start.15 = (bf16[1296,128]{1,0:T(8,128)(2,1)S(1)}, bf16[1296,128]{1,0:T(8,128)(2,1)S(1)}, u32[]{:S(2)}, u32[]{:S(2)}) collective-permute-start(bf16[1296,128]{1,0:T(8,128)(2,1)S(1)} %collective-permute-done.11.refs_1_), channel_id=1, source_target_pairs={{0,1},{1,0},{2,3},{3,2},{4,5},{5,4},{6,7},{7,6},{8,9},{9,8},{10,11... | collective-permute-start | bytes 995336 | tf_op jit(solution)/shard_map/ppermute | solution.py:379
  58.4 6.3 %collective-permute-start.17 = (bf16[528,128]{1,0:T(8,128)(2,1)S(1)}, bf16[528,128]{1,0:T(8,128)(2,1)S(1)}, u32[]{:S(2)}, u32[]{:S(2)}) collective-permute-start(bf16[528,128]{1,0:T(8,128)(2,1)S(1)} %get-tuple-element.96), channel_id=1, source_target_pairs={{0,32},{32,64},{64,96},{96,0},{1,33},{33,65},{65,97},{97,1},{2,34}... | collective-permute-start | bytes 405512 | tf_op jit(solution)/shard_map/ppermute | solution.py:384
  58.5 8.0 %collective-permute-start.18 = (bf16[528,128]{1,0:T(8,128)(2,1)S(1)}, bf16[528,128]{1,0:T(8,128)(2,1)S(1)}, u32[]{:S(2)}, u32[]{:S(2)}) collective-permute-start(bf16[528,128]{1,0:T(8,128)(2,1)S(1)} %get-tuple-element.97), channel_id=1, source_target_pairs={{0,96},{32,0},{64,32},{96,64},{1,97},{33,1},{65,33},{97,65},{2,98}... | collective-permute-start | bytes 405512 | tf_op jit(solution)/shard_map/ppermute | solution.py:384
  61.2 6.1 %collective-permute-start.19 = (bf16[528,128]{1,0:T(8,128)(2,1)S(1)}, bf16[528,128]{1,0:T(8,128)(2,1)S(1)}, u32[]{:S(2)}, u32[]{:S(2)}) collective-permute-start(bf16[528,128]{1,0:T(8,128)(2,1)S(1)} %get-tuple-element.98), channel_id=1, source_target_pairs={{0,64},{32,96},{64,0},{96,32},{1,65},{33,97},{65,1},{97,33},{2,66}... | collective-permute-start | bytes 405512 | tf_op jit(solution)/shard_map/ppermute | solution.py:384
  (3 other events, 24.9 us)

commit v7 on v6

--- a/solution.py
+++ b/solution.py
@@ -215,7 +215,8 @@
 def local(s0, r1, r2, r3, weight, bias, cot, act, msg):
     w = weight[...]
     over_nodes = (((0,), (0,)), ((), ()))
-    wg, bg = jnp.zeros((B, 256), F32), jnp.zeros((1, 256), F32)
+    w_twice = jnp.concatenate([w, w])
+    wg, bg = jnp.zeros((2 * B, 256), F32), jnp.zeros((1, 256), F32)
     for k, r in enumerate((None, r3, r2, r1)):
         if k == 0:
             c = cot[...]
@@ -226,9 +227,8 @@
             y += r[pl.ds((k + d) % 4 * 256, 256)].astype(F32)
         y_high = y.astype(BF16)
         y_low = (y - y_high.astype(F32)).astype(BF16)
-        summed = jnp.dot(y_high, w, preferred_element_type=F32) + jnp.dot(
-            y_low, w, preferred_element_type=F32
-        )
+        y_both = jnp.concatenate([y_high, y_low], axis=1)
+        summed = jnp.dot(y_both, w_twice, preferred_element_type=F32)
         pre = summed + bias[...]
         sig = jax.nn.sigmoid(pre)
         if k == 0:
@@ -239,9 +239,9 @@
         g = g.astype(BF16)
         msg[pl.ds(k * 256, B)] = g[:, 0:B]
         msg[pl.ds(k * 256 + B, B)] = g[:, B : 2 * B]
-        wg += lax.dot_general(y_high, grad, over_nodes, preferred_element_type=F32)
-        wg += lax.dot_general(y_low, grad, over_nodes, preferred_element_type=F32)
+        wg += lax.dot_general(y_both, grad, over_nodes, preferred_element_type=F32)
         bg += jnp.sum(grad.astype(F32), axis=0, keepdims=True)
+    wg = wg[0:B] + wg[B : 2 * B]
     put_tail(
         msg,
         1024,

time: 68.1 us -> 68.6 us (level)
  waiting for transfers between devices: 21.9 us -> 24.7 us
  starting transfers between devices: 29.8 us -> 27.6 us
    ppermute x12, starting transfers between devices: 23 us -> 21.4 us  [permute(): moved = [lax.ppermute(a, axis, p) for a, p in zip(arrays, pairs)]]
    ppermute x12, waiting for transfers between devices: 17.3 us -> 18.8 us  [permute(): moved = [lax.ppermute(a, axis, p) for a, p in zip(arrays, pairs)]]
  transfers between devices with their start and end apart: 20 -> 20, of which waited for: 13 -> 13; matrix products, arithmetic and copies ran while one was open for 0% -> 0% of each run, Pallas kernels for 14% -> 13%
where the time goes in v7:
time: 68.6 us; the launch traced here: 68.3 us
  starting transfers between devices  27.6 us (40%)
  waiting for transfers between devices  24.7 us (36%)
  Pallas kernels  14.6 us (21%)
  between operations  1.47 us (2%)
    ppermute x12, starting transfers between devices, permute(): moved = [lax.ppermute(a, axis, p) for a, p in zip(arrays, pairs)]  21.4 us
    ppermute x12, waiting for transfers between devices, permute(): moved = [lax.ppermute(a, axis, p) for a, p in zip(arrays, pairs)]  18.8 us
    pallas_call x4, Pallas kernels, backward(): call(functools.partial(backward_tiles, key, places), outs, [SMEM] + [VMEM...  5.46 us
    ppermute x3, waiting for transfers between devices, on_device(): rs = [lax.ppermute(a, 'row', row_shift(d)) for a, d in zip(ms, ORDER)]  4.94 us
    ppermute x3, starting transfers between devices, on_device(): rs = [lax.ppermute(a, 'row', row_shift(d)) for a, d in zip(ms, ORDER)]  2.84 us
    pallas_call x1, Pallas kernels, on_device(): call(hold, (jax.ShapeDtypeStruct((128, B, B), BF16), half, half), [ANY],...  2.22 us
    pallas_call x1, Pallas kernels, on_device(): call(functools.partial(forward_tiles, 0), (half, sds(4096)), [SMEM] + [VM...  1.93 us
    ppermute x4, starting transfers between devices, on_device(): theirs[k] = lax.ppermute(mine[k], 'col', core_swap())  1.71 us
  transfers between devices with their start and end apart: 20, of which 13 were waited for; matrix products, arithmetic and copies ran while one was open for 0% of the time, Pallas kernels for 13%

profile of v7, /device:TPU:1, one launch (start us, length us, event | category | flops | bytes accessed | tf_op | source)
XLA Modules:
  0.0 68.3 jit_solution(9608484282666706824)
XLA Ops:
  0.7 2.1 %collective-permute-start = (bf16[256,128]{1,0:T(8,128)(2,1)}, bf16[256,128]{1,0:T(8,128)(2,1)S(1)}, u32[]{:S(2)}, u32[]{:S(2)}) collective-permute-start(bf16[256,128]{1,0:T(8,128)(2,1)} %x0.3), channel_id=1, source_target_pairs={{0,32},{32,64},{64,96},{96,0},{1,33},{33,65},{65,97},{97,1},{2,34}... | collective-permute-start | bytes 196616 | tf_op jit(solution)/shard_map/ppermute | solution.py:72
  2.8 1.3 %collective-permute-start.1 = (bf16[256,128]{1,0:T(8,128)(2,1)}, bf16[256,128]{1,0:T(8,128)(2,1)S(1)}, u32[]{:S(2)}, u32[]{:S(2)}) collective-permute-start(bf16[256,128]{1,0:T(8,128)(2,1)} %x0.3), channel_id=1, source_target_pairs={{0,96},{32,0},{64,32},{96,64},{1,97},{33,1},{65,33},{97,65},{2,98}... | collective-permute-start | bytes 196616 | tf_op jit(solution)/shard_map/ppermute | solution.py:72
  4.1 1.6 %collective-permute-start.2 = (bf16[256,128]{1,0:T(8,128)(2,1)}, bf16[256,128]{1,0:T(8,128)(2,1)S(1)}, u32[]{:S(2)}, u32[]{:S(2)}) collective-permute-start(bf16[256,128]{1,0:T(8,128)(2,1)} %x0.3), channel_id=1, source_target_pairs={{0,64},{32,96},{64,0},{96,32},{1,65},{33,97},{65,1},{97,33},{2,66}... | collective-permute-start | bytes 196616 | tf_op jit(solution)/shard_map/ppermute | solution.py:72
  6.4 2.2 %shard_map.112 = (bf16[128,128,128]{2,1,0:T(8,128)(2,1)S(1)}, f32[33,128,128]{2,1,0:T(8,128)S(1)}, f32[33,128,128]{2,1,0:T(8,128)S(1)}) custom-call(bf16[128,128,128]{2,1,0:T(8,128)(2,1)} %bitcast.5), custom_call_target="tpu_custom_call" | custom-call | tf_op jit(solution)/shard_map/pallas_call | solution.py:322
  9.5 1.9 %shard_map.114 = (f32[33,128,128]{2,1,0:T(8,128)S(1)}, bf16[4096,128]{1,0:T(8,128)(2,1)S(1)}) custom-call(s32[1,384]{1,0:T(1,128)S(1)} %get-tuple-element.53.tab, bf16[256,128]{1,0:T(8,128)(2,1)S(1)} %copy-done.2, bf16[256,128]{1,0:T(8,128)(2,1)S(1)} %collective-permute-done.1.x1, ...), custom_call_target="tpu_custom_call", output_to_operand_aliasing={{0}: (6, {})} | custom-call | flops 268435456 | bytes 4194304 | tf_op jit(solution)/shard_map/pallas_call | solution.py:331
  11.5 1.6 %collective-permute-start.3 = (bf16[4096,128]{1,0:T(8,128)(2,1)S(1)}, bf16[4096,128]{1,0:T(8,128)(2,1)S(1)}, u32[]{:S(2)}, u32[]{:S(2)}) collective-permute-start(bf16[4096,128]{1,0:T(8,128)(2,1)S(1)} %get-tuple-element.63), channel_id=1, source_target_pairs={{0,1},{1,0},{2,3},{3,2},{4,5},{5,4},{6,7},{7,6},{8,9},{9,8},{10,11... | collective-permute-start | bytes 3145736 | tf_op jit(solution)/shard_map/ppermute | solution.py:339
  13.1 1.5 %shard_map.113.acc = f32[33,128,128]{2,1,0:T(8,128)S(1)} custom-call(s32[1,384]{1,0:T(1,128)S(1)} %get-tuple-element.53.tab, bf16[256,128]{1,0:T(8,128)(2,1)S(1)} %copy-done.2, bf16[256,128]{1,0:T(8,128)(2,1)S(1)} %collective-permute-done.1.x1, bf16[256,128]{1,0:T(8,128)(2,1)S(1)} %collective-permute-done.2.x2, ...), custom_call_target="tpu_custom_call", output_to_operand_aliasing={{}: (6, {})} | custom-call | tf_op jit(solution)/shard_map/pallas_call | solution.py:340
  15.5 3.1 %collective-permute-start.4 = (bf16[1024,128]{1,0:T(8,128)(2,1)S(1)}, bf16[1024,128]{1,0:T(8,128)(2,1)S(1)}, u32[]{:S(2)}, u32[]{:S(2)}) collective-permute-start(bf16[1024,128]{1,0:T(8,128)(2,1)S(1)} %get-tuple-element.68), channel_id=1, source_target_pairs={{0,4},{1,17},{2,18},{3,7},{4,0},{5,21},{6,22},{7,3},{8,24},{9,13},... | collective-permute-start | bytes 786440 | tf_op jit(solution)/shard_map/ppermute | solution.py:72
  19.9 1.7 %collective-permute-start.6 = (bf16[1024,128]{1,0:T(8,128)(2,1)S(1)}, bf16[1024,128]{1,0:T(8,128)(2,1)S(1)}, u32[]{:S(2)}, u32[]{:S(2)}) collective-permute-start(bf16[1024,128]{1,0:T(8,128)(2,1)S(1)} %get-tuple-element.70), channel_id=1, source_target_pairs={{0,7},{1,24},{2,27},{3,0},{4,3},{5,28},{6,31},{7,4},{8,1},{9,14},{... | collective-permute-start | bytes 786440 | tf_op jit(solution)/shard_map/ppermute | solution.py:72
  22.7 3.2 %collective-permute-done.5.r1 = bf16[1024,128]{1,0:T(8,128)(2,1)S(1)} collective-permute-done((bf16[1024,128]{1,0:T(8,128)(2,1)S(1)}, bf16[1024,128]{1,0:T(8,128)(2,1)S(1)}, u32[]{:S(2)}, u32[]{:S(2)}) %collective-permute-start.5) | collective-permute-done | bytes 262176 | tf_op jit(solution)/shard_map/ppermute | solution.py:72
  26.9 3.1 %collective-permute-start.7 = (bf16[1536,128]{1,0:T(8,128)(2,1)S(1)}, bf16[1536,128]{1,0:T(8,128)(2,1)S(1)}, u32[]{:S(2)}, u32[]{:S(2)}) collective-permute-start(bf16[1536,128]{1,0:T(8,128)(2,1)S(1)} %get-tuple-element.78), channel_id=1, source_target_pairs={{0,16},{1,5},{2,6},{3,19},{4,20},{5,1},{6,2},{7,23},{8,12},{9,25},... | collective-permute-start | bytes 1179656 | tf_op jit(solution)/shard_map/ppermute | solution.py:72
  31.2 1.7 %collective-permute-start.9 = (bf16[1536,128]{1,0:T(8,128)(2,1)S(1)}, bf16[1536,128]{1,0:T(8,128)(2,1)S(1)}, u32[]{:S(2)}, u32[]{:S(2)}) collective-permute-start(bf16[1536,128]{1,0:T(8,128)(2,1)S(1)} %get-tuple-element.78), channel_id=1, source_target_pairs={{0,25},{1,6},{2,1},{3,26},{4,29},{5,2},{6,5},{7,30},{8,15},{9,0},{... | collective-permute-start | bytes 1179656 | tf_op jit(solution)/shard_map/ppermute | solution.py:72
  32.9 2.5 %collective-permute-done.7.r2 = bf16[1536,128]{1,0:T(8,128)(2,1)S(1)} collective-permute-done((bf16[1536,128]{1,0:T(8,128)(2,1)S(1)}, bf16[1536,128]{1,0:T(8,128)(2,1)S(1)}, u32[]{:S(2)}, u32[]{:S(2)}) %collective-permute-start.7) | collective-permute-done | bytes 393248 | tf_op jit(solution)/shard_map/ppermute | solution.py:72
  35.4 4.2 %collective-permute-done.8.r1 = bf16[1536,128]{1,0:T(8,128)(2,1)S(1)} collective-permute-done((bf16[1536,128]{1,0:T(8,128)(2,1)S(1)}, bf16[1536,128]{1,0:T(8,128)(2,1)S(1)}, u32[]{:S(2)}, u32[]{:S(2)}) %collective-permute-start.8) | collective-permute-done | bytes 393248 | tf_op jit(solution)/shard_map/ppermute | solution.py:72
  40.9 1.6 %shard_map.117 = (bf16[256,256]{1,0:T(8,128)(2,1)}, bf16[1296,128]{1,0:T(8,128)(2,1)S(1)}) custom-call(f32[1024,128]{1,0:T(8,128)S(1)} %get-tuple-element.74.s0, bf16[1536,128]{1,0:T(8,128)(2,1)S(1)} %collective-permute-done.8.r1, bf16[1536,128]{1,0:T(8,128)(2,1)S(1)} %collective-permute-done.7.r2, bf16[1536,128]{1,0:T(8,128)(2,1)S(1)} %collective-permute-done.9.r3, ...), custom_call_target="tpu_custom_call" | custom-call | tf_op jit(solution)/shard_map/pallas_call | solution.py:353
  43.9 2.9 %collective-permute-start.10 = (bf16[1296,128]{1,0:T(8,128)(2,1)S(1)}, bf16[1296,128]{1,0:T(8,128)(2,1)S(1)}, u32[]{:S(2)}, u32[]{:S(2)}) collective-permute-start(bf16[1296,128]{1,0:T(8,128)(2,1)S(1)} %get-tuple-element.87.refs_0_), channel_id=1, source_target_pairs={{0,7},{1,24},{2,27},{3,0},{4,3},{5,28},{6,31},{7,4},{8,1},{9,14},{... | collective-permute-start | bytes 995336 | tf_op jit(solution)/shard_map/ppermute | solution.py:72
  47.1 3.2 %collective-permute-done.12.refs_1_ = bf16[1296,128]{1,0:T(8,128)(2,1)S(1)} collective-permute-done((bf16[1296,128]{1,0:T(8,128)(2,1)S(1)}, bf16[1296,128]{1,0:T(8,128)(2,1)S(1)}, u32[]{:S(2)}, u32[]{:S(2)}) %collective-permute-start.12) | collective-permute-done | bytes 331808 | tf_op jit(solution)/shard_map/ppermute | solution.py:72
  50.5 1.6 %shard_map.118 = (f32[9,128,128]{2,1,0:T(8,128)S(1)}, f32[272,128]{1,0:T(8,128)S(1)}) custom-call(s32[1,640]{1,0:T(1,128)S(1)} %get-tuple-element.83.tab, bf16[128,128,128]{2,1,0:T(8,128)(2,1)S(1)} %bitcast.6, bf16[1296,128]{1,0:T(8,128)(2,1)S(1)} %get-tuple-element.87.refs_0_, bf16[1296,128]{1,0:T(8,128)(2,1)S(1)} %collective-permute-done.12.refs_1_, ...), custom_call_target="tpu_custom_call" | custom-call | flops 201326592 | bytes 3145728 | tf_op jit(solution)/shard_map/pallas_call | solution.py:367
  52.1 2.3 %collective-permute-done.10.refs_0_ = bf16[1296,128]{1,0:T(8,128)(2,1)S(1)} collective-permute-done((bf16[1296,128]{1,0:T(8,128)(2,1)S(1)}, bf16[1296,128]{1,0:T(8,128)(2,1)S(1)}, u32[]{:S(2)}, u32[]{:S(2)}) %collective-permute-start.10) | collective-permute-done | bytes 331808 | tf_op jit(solution)/shard_map/ppermute | solution.py:72
  55.8 1.6 %shard_map.119 = (f32[9,128,128]{2,1,0:T(8,128)S(1)}, f32[272,128]{1,0:T(8,128)S(1)}) custom-call(s32[1,640]{1,0:T(1,128)S(1)} %get-tuple-element.83.tab, bf16[128,128,128]{2,1,0:T(8,128)(2,1)S(1)} %bitcast.7, bf16[1296,128]{1,0:T(8,128)(2,1)S(1)} %collective-permute-done.10.refs_0_, ...), custom_call_target="tpu_custom_call", output_to_operand_aliasing={{0}: (5, {})} | custom-call | flops 201326592 | bytes 3145728 | tf_op jit(solution)/shard_map/pallas_call | solution.py:367
  57.5 1.3 %shard_map.121 = (bf16[528,128]{1,0:T(8,128)(2,1)S(1)}, bf16[528,128]{1,0:T(8,128)(2,1)S(1)}, bf16[528,128]{1,0:T(8,128)(2,1)S(1)}) custom-call(s32[1,640]{1,0:T(1,128)S(1)} %get-tuple-element.83.tab, bf16[128,128,128]{2,1,0:T(8,128)(2,1)S(1)} %bitcast.8, bf16[1296,128]{1,0:T(8,128)(2,1)S(1)} %collective-permute-done.14.refs_0_, ...), custom_call_target="tpu_custom_call" | custom-call | flops 67108864 | bytes 1048576 | tf_op jit(solution)/shard_map/pallas_call | solution.py:367
  59.8 1.8 %collective-permute-start.18 = (bf16[528,128]{1,0:T(8,128)(2,1)S(1)}, bf16[528,128]{1,0:T(8,128)(2,1)S(1)}, u32[]{:S(2)}, u32[]{:S(2)}) collective-permute-start(bf16[528,128]{1,0:T(8,128)(2,1)S(1)} %get-tuple-element.97), channel_id=1, source_target_pairs={{0,96},{32,0},{64,32},{96,64},{1,97},{33,1},{65,33},{97,65},{2,98}... | collective-permute-start | bytes 405512 | tf_op jit(solution)/shard_map/ppermute | solution.py:384
  62.6 2.6 %collective-permute-done.17.r1 = bf16[528,128]{1,0:T(8,128)(2,1)S(1)} collective-permute-done((bf16[528,128]{1,0:T(8,128)(2,1)S(1)}, bf16[528,128]{1,0:T(8,128)(2,1)S(1)}, u32[]{:S(2)}, u32[]{:S(2)}) %collective-permute-start.17) | collective-permute-done | bytes 135200 | tf_op jit(solution)/shard_map/ppermute | solution.py:384
  65.2 2.3 %collective-permute-done.19.r3 = bf16[528,128]{1,0:T(8,128)(2,1)S(1)} collective-permute-done((bf16[528,128]{1,0:T(8,128)(2,1)S(1)}, bf16[528,128]{1,0:T(8,128)(2,1)S(1)}, u32[]{:S(2)}, u32[]{:S(2)}) %collective-permute-start.19) | collective-permute-done | bytes 135200 | tf_op jit(solution)/shard_map/ppermute | solution.py:384
  (42 shorter events, 13.8 us)
Async XLA Ops:
  0.7 8.8 %collective-permute-start = (bf16[256,128]{1,0:T(8,128)(2,1)}, bf16[256,128]{1,0:T(8,128)(2,1)S(1)}, u32[]{:S(2)}, u32[]{:S(2)}) collective-permute-start(bf16[256,128]{1,0:T(8,128)(2,1)} %x0.3), channel_id=1, source_target_pairs={{0,32},{32,64},{64,96},{96,0},{1,33},{33,65},{65,97},{97,1},{2,34}... | collective-permute-start | bytes 196616 | tf_op jit(solution)/shard_map/ppermute | solution.py:72
  2.8 6.7 %collective-permute-start.1 = (bf16[256,128]{1,0:T(8,128)(2,1)}, bf16[256,128]{1,0:T(8,128)(2,1)S(1)}, u32[]{:S(2)}, u32[]{:S(2)}) collective-permute-start(bf16[256,128]{1,0:T(8,128)(2,1)} %x0.3), channel_id=1, source_target_pairs={{0,96},{32,0},{64,32},{96,64},{1,97},{33,1},{65,33},{97,65},{2,98}... | collective-permute-start | bytes 196616 | tf_op jit(solution)/shard_map/ppermute | solution.py:72
  4.1 5.4 %collective-permute-start.2 = (bf16[256,128]{1,0:T(8,128)(2,1)}, bf16[256,128]{1,0:T(8,128)(2,1)S(1)}, u32[]{:S(2)}, u32[]{:S(2)}) collective-permute-start(bf16[256,128]{1,0:T(8,128)(2,1)} %x0.3), channel_id=1, source_target_pairs={{0,64},{32,96},{64,0},{96,32},{1,65},{33,97},{65,1},{97,33},{2,66}... | collective-permute-start | bytes 196616 | tf_op jit(solution)/shard_map/ppermute | solution.py:72
  11.5 3.9 %collective-permute-start.3 = (bf16[4096,128]{1,0:T(8,128)(2,1)S(1)}, bf16[4096,128]{1,0:T(8,128)(2,1)S(1)}, u32[]{:S(2)}, u32[]{:S(2)}) collective-permute-start(bf16[4096,128]{1,0:T(8,128)(2,1)S(1)} %get-tuple-element.63), channel_id=1, source_target_pairs={{0,1},{1,0},{2,3},{3,2},{4,5},{5,4},{6,7},{7,6},{8,9},{9,8},{10,11... | collective-permute-start | bytes 3145736 | tf_op jit(solution)/shard_map/ppermute | solution.py:339
  14.6 12.2 %copy-start.1 = (bf16[256,256]{1,0:T(8,128)(2,1)S(1)}, bf16[256,256]{1,0:T(8,128)(2,1)}, u32[]{:S(2)}) copy-start(bf16[256,256]{1,0:T(8,128)(2,1)} %cot.3) | copy-start | bytes 393220
  14.6 26.3 %copy-start.3 = (bf16[128,256]{1,0:T(8,128)(2,1)S(1)}, bf16[128,256]{1,0:T(8,128)(2,1)}, u32[]{:S(2)}) copy-start(bf16[128,256]{1,0:T(8,128)(2,1)} %weight.1) | copy-start | bytes 196612
  14.6 26.3 %copy-start.4 = (f32[256]{0:T(256)S(1)}, f32[256]{0:T(256)}, u32[]{:S(2)}) copy-start(f32[256]{0:T(256)} %param.10) | copy-start | bytes 3076
  15.4 35.1 %copy-start = (bf16[1,1,128,128,128]{4,3,2,1,0:T(8,128)(2,1)S(1)}, bf16[1,1,128,128,128]{4,3,2,1,0:T(8,128)(2,1)}, u32[]{:S(2)}) copy-start(bf16[1,1,128,128,128]{4,3,2,1,0:T(8,128)(2,1)} %param.11) | copy-start | bytes 12582916
  15.5 7.1 %collective-permute-start.4 = (bf16[1024,128]{1,0:T(8,128)(2,1)S(1)}, bf16[1024,128]{1,0:T(8,128)(2,1)S(1)}, u32[]{:S(2)}, u32[]{:S(2)}) collective-permute-start(bf16[1024,128]{1,0:T(8,128)(2,1)S(1)} %get-tuple-element.68), channel_id=1, source_target_pairs={{0,4},{1,17},{2,18},{3,7},{4,0},{5,21},{6,22},{7,3},{8,24},{9,13},... | collective-permute-start | bytes 786440 | tf_op jit(solution)/shard_map/ppermute | solution.py:72
  18.6 7.3 %collective-permute-start.5 = (bf16[1024,128]{1,0:T(8,128)(2,1)S(1)}, bf16[1024,128]{1,0:T(8,128)(2,1)S(1)}, u32[]{:S(2)}, u32[]{:S(2)}) collective-permute-start(bf16[1024,128]{1,0:T(8,128)(2,1)S(1)} %get-tuple-element.69), channel_id=1, source_target_pairs={{0,3},{1,8},{2,11},{3,4},{4,7},{5,12},{6,15},{7,0},{8,17},{9,10},{... | collective-permute-start | bytes 786440 | tf_op jit(solution)/shard_map/ppermute | solution.py:72
  19.9 6.9 %collective-permute-start.6 = (bf16[1024,128]{1,0:T(8,128)(2,1)S(1)}, bf16[1024,128]{1,0:T(8,128)(2,1)S(1)}, u32[]{:S(2)}, u32[]{:S(2)}) collective-permute-start(bf16[1024,128]{1,0:T(8,128)(2,1)S(1)} %get-tuple-element.70), channel_id=1, source_target_pairs={{0,7},{1,24},{2,27},{3,0},{4,3},{5,28},{6,31},{7,4},{8,1},{9,14},{... | collective-permute-start | bytes 786440 | tf_op jit(solution)/shard_map/ppermute | solution.py:72
  26.9 8.5 %collective-permute-start.7 = (bf16[1536,128]{1,0:T(8,128)(2,1)S(1)}, bf16[1536,128]{1,0:T(8,128)(2,1)S(1)}, u32[]{:S(2)}, u32[]{:S(2)}) collective-permute-start(bf16[1536,128]{1,0:T(8,128)(2,1)S(1)} %get-tuple-element.78), channel_id=1, source_target_pairs={{0,16},{1,5},{2,6},{3,19},{4,20},{5,1},{6,2},{7,23},{8,12},{9,25},... | collective-permute-start | bytes 1179656 | tf_op jit(solution)/shard_map/ppermute | solution.py:72
  29.9 9.7 %collective-permute-start.8 = (bf16[1536,128]{1,0:T(8,128)(2,1)S(1)}, bf16[1536,128]{1,0:T(8,128)(2,1)S(1)}, u32[]{:S(2)}, u32[]{:S(2)}) collective-permute-start(bf16[1536,128]{1,0:T(8,128)(2,1)S(1)} %get-tuple-element.78), channel_id=1, source_target_pairs={{0,9},{1,2},{2,5},{3,10},{4,13},{5,6},{6,1},{7,14},{8,11},{9,16},{... | collective-permute-start | bytes 1179656 | tf_op jit(solution)/shard_map/ppermute | solution.py:72
  31.2 9.7 %collective-permute-start.9 = (bf16[1536,128]{1,0:T(8,128)(2,1)S(1)}, bf16[1536,128]{1,0:T(8,128)(2,1)S(1)}, u32[]{:S(2)}, u32[]{:S(2)}) collective-permute-start(bf16[1536,128]{1,0:T(8,128)(2,1)S(1)} %get-tuple-element.78), channel_id=1, source_target_pairs={{0,25},{1,6},{2,1},{3,26},{4,29},{5,2},{6,5},{7,30},{8,15},{9,0},{... | collective-permute-start | bytes 1179656 | tf_op jit(solution)/shard_map/ppermute | solution.py:72
  42.5 7.8 %collective-permute-start.12 = (bf16[1296,128]{1,0:T(8,128)(2,1)S(1)}, bf16[1296,128]{1,0:T(8,128)(2,1)S(1)}, u32[]{:S(2)}, u32[]{:S(2)}) collective-permute-start(bf16[1296,128]{1,0:T(8,128)(2,1)S(1)} %get-tuple-element.87.refs_0_), channel_id=1, source_target_pairs={{0,3},{1,8},{2,11},{3,4},{4,7},{5,12},{6,15},{7,0},{8,17},{9,10},{... | collective-permute-start | bytes 995336 | tf_op jit(solution)/shard_map/ppermute | solution.py:72
  43.5 7.0 %collective-permute-start.13 = (bf16[1296,128]{1,0:T(8,128)(2,1)S(1)}, bf16[1296,128]{1,0:T(8,128)(2,1)S(1)}, u32[]{:S(2)}, u32[]{:S(2)}) collective-permute-start(bf16[1296,128]{1,0:T(8,128)(2,1)S(1)} %get-tuple-element.87.refs_0_), channel_id=1, source_target_pairs={{0,1},{1,0},{2,3},{3,2},{4,5},{5,4},{6,7},{7,6},{8,9},{9,8},{10,11... | collective-permute-start | bytes 995336 | tf_op jit(solution)/shard_map/ppermute | solution.py:360
  43.9 10.5 %collective-permute-start.10 = (bf16[1296,128]{1,0:T(8,128)(2,1)S(1)}, bf16[1296,128]{1,0:T(8,128)(2,1)S(1)}, u32[]{:S(2)}, u32[]{:S(2)}) collective-permute-start(bf16[1296,128]{1,0:T(8,128)(2,1)S(1)} %get-tuple-element.87.refs_0_), channel_id=1, source_target_pairs={{0,7},{1,24},{2,27},{3,0},{4,3},{5,28},{6,31},{7,4},{8,1},{9,14},{... | collective-permute-start | bytes 995336 | tf_op jit(solution)/shard_map/ppermute | solution.py:72
  46.8 7.8 %collective-permute-start.11 = (bf16[1296,128]{1,0:T(8,128)(2,1)S(1)}, bf16[1296,128]{1,0:T(8,128)(2,1)S(1)}, u32[]{:S(2)}, u32[]{:S(2)}) collective-permute-start(bf16[1296,128]{1,0:T(8,128)(2,1)S(1)} %get-tuple-element.87.refs_0_), channel_id=1, source_target_pairs={{0,4},{1,17},{2,18},{3,7},{4,0},{5,21},{6,22},{7,3},{8,24},{9,13},... | collective-permute-start | bytes 995336 | tf_op jit(solution)/shard_map/ppermute | solution.py:72
  50.3 5.5 %collective-permute-start.16 = (bf16[1296,128]{1,0:T(8,128)(2,1)S(1)}, bf16[1296,128]{1,0:T(8,128)(2,1)S(1)}, u32[]{:S(2)}, u32[]{:S(2)}) collective-permute-start(bf16[1296,128]{1,0:T(8,128)(2,1)S(1)} %collective-permute-done.12.refs_1_), channel_id=1, source_target_pairs={{0,1},{1,0},{2,3},{3,2},{4,5},{5,4},{6,7},{7,6},{8,9},{9,8},{10,11... | collective-permute-start | bytes 995336 | tf_op jit(solution)/shard_map/ppermute | solution.py:360
  54.6 2.8 %collective-permute-start.14 = (bf16[1296,128]{1,0:T(8,128)(2,1)S(1)}, bf16[1296,128]{1,0:T(8,128)(2,1)S(1)}, u32[]{:S(2)}, u32[]{:S(2)}) collective-permute-start(bf16[1296,128]{1,0:T(8,128)(2,1)S(1)} %collective-permute-done.10.refs_0_), channel_id=1, source_target_pairs={{0,1},{1,0},{2,3},{3,2},{4,5},{5,4},{6,7},{7,6},{8,9},{9,8},{10,11... | collective-permute-start | bytes 995336 | tf_op jit(solution)/shard_map/ppermute | solution.py:379
  55.8 1.7 %collective-permute-start.15 = (bf16[1296,128]{1,0:T(8,128)(2,1)S(1)}, bf16[1296,128]{1,0:T(8,128)(2,1)S(1)}, u32[]{:S(2)}, u32[]{:S(2)}) collective-permute-start(bf16[1296,128]{1,0:T(8,128)(2,1)S(1)} %collective-permute-done.11.refs_1_), channel_id=1, source_target_pairs={{0,1},{1,0},{2,3},{3,2},{4,5},{5,4},{6,7},{7,6},{8,9},{9,8},{10,11... | collective-permute-start | bytes 995336 | tf_op jit(solution)/shard_map/ppermute | solution.py:379
  58.8 6.4 %collective-permute-start.17 = (bf16[528,128]{1,0:T(8,128)(2,1)S(1)}, bf16[528,128]{1,0:T(8,128)(2,1)S(1)}, u32[]{:S(2)}, u32[]{:S(2)}) collective-permute-start(bf16[528,128]{1,0:T(8,128)(2,1)S(1)} %get-tuple-element.96), channel_id=1, source_target_pairs={{0,32},{32,64},{64,96},{96,0},{1,33},{33,65},{65,97},{97,1},{2,34}... | collective-permute-start | bytes 405512 | tf_op jit(solution)/shard_map/ppermute | solution.py:384
  59.8 5.4 %collective-permute-start.18 = (bf16[528,128]{1,0:T(8,128)(2,1)S(1)}, bf16[528,128]{1,0:T(8,128)(2,1)S(1)}, u32[]{:S(2)}, u32[]{:S(2)}) collective-permute-start(bf16[528,128]{1,0:T(8,128)(2,1)S(1)} %get-tuple-element.97), channel_id=1, source_target_pairs={{0,96},{32,0},{64,32},{96,64},{1,97},{33,1},{65,33},{97,65},{2,98}... | collective-permute-start | bytes 405512 | tf_op jit(solution)/shard_map/ppermute | solution.py:384
  61.6 6.0 %collective-permute-start.19 = (bf16[528,128]{1,0:T(8,128)(2,1)S(1)}, bf16[528,128]{1,0:T(8,128)(2,1)S(1)}, u32[]{:S(2)}, u32[]{:S(2)}) collective-permute-start(bf16[528,128]{1,0:T(8,128)(2,1)S(1)} %get-tuple-element.98), channel_id=1, source_target_pairs={{0,64},{32,96},{64,0},{96,32},{1,65},{33,97},{65,1},{97,33},{2,66}... | collective-permute-start | bytes 405512 | tf_op jit(solution)/shard_map/ppermute | solution.py:384
  (3 other events, 24.9 us)

commit v8 on v6

--- a/solution.py
+++ b/solution.py
@@ -349,7 +349,7 @@
     total, msg = call(first_sum, (sds(1024, dtype=F32), sds(1536)), [VMEM] * 5)(
         ms[0], r1, r2, r3, cotangent
     )
-    r2, r1, r3 = permute([msg] * 3, "col", [col_shift(False, d) for d in FAR_FIRST])
+    r1, r3, r2 = permute([msg] * 3, "col", [col_shift(False, d) for d in ORDER])
     act, msg = call(local, (sds(256, 256), sds(1024 + TAIL)), [VMEM] * 7)(
         total, r1, r2, r3, weight, bias_vector.reshape(1, 256), cotangent
     )

time: 68.1 us -> 68.7 us (level); the launches traced: 68.1 us -> 67.7 us
  waiting for transfers between devices: 21.9 us -> 26.6 us
  Pallas kernels: 14.9 us -> 11.8 us
  starting transfers between devices: 29.8 us -> 27.7 us
    ppermute x12, waiting for transfers between devices: 17.3 us -> 20.9 us  [permute(): moved = [lax.ppermute(a, axis, p) for a, p in zip(arrays, pairs)]]
    pallas_call x4, Pallas kernels: 5.75 us -> 4.25 us  [backward(): call(functools.partial(backward_tiles, key, places), outs, [SMEM] + [VMEM...]
    ppermute x12, starting transfers between devices: 23 us -> 21.8 us  [permute(): moved = [lax.ppermute(a, axis, p) for a, p in zip(arrays, pairs)]]
    ppermute x1, waiting for transfers between devices: 0.14 us -> 1.06 us  [on_device(): got = lax.ppermute(other, 'col', core_swap())]
    pallas_call x1, Pallas kernels: 2.11 us -> 1.18 us  [on_device(): call(functools.partial(forward_tiles, 1), half, [SMEM] + [VMEM] * 6, scra...]
    ppermute x4, starting transfers between devices: 1.71 us -> 0.91 us  [on_device(): theirs[k] = lax.ppermute(mine[k], 'col', core_swap())]
  transfers between devices with their start and end apart: 20 -> 20, of which waited for: 13 -> 12; matrix products, arithmetic and copies ran while one was open for 0% -> 0% of each run, Pallas kernels for 14% -> 11%
where the time goes in v8:
time: 68.7 us; the launch traced here: 67.7 us
  starting transfers between devices  27.7 us (40%)
  waiting for transfers between devices  26.6 us (39%)
  Pallas kernels  11.8 us (17%)
  between operations  1.48 us (2%)
    ppermute x12, starting transfers between devices, permute(): moved = [lax.ppermute(a, axis, p) for a, p in zip(arrays, pairs)]  21.8 us
    ppermute x12, waiting for transfers between devices, permute(): moved = [lax.ppermute(a, axis, p) for a, p in zip(arrays, pairs)]  20.9 us
    ppermute x3, waiting for transfers between devices, on_device(): rs = [lax.ppermute(a, 'row', row_shift(d)) for a, d in zip(ms, ORDER)]  4.34 us
    pallas_call x4, Pallas kernels, backward(): call(functools.partial(backward_tiles, key, places), outs, [SMEM] + [VMEM...  4.25 us
    ppermute x3, starting transfers between devices, on_device(): rs = [lax.ppermute(a, 'row', row_shift(d)) for a, d in zip(ms, ORDER)]  3.11 us
    pallas_call x1, Pallas kernels, on_device(): call(hold, (jax.ShapeDtypeStruct((128, B, B), BF16), half, half), [ANY],...  2.22 us
    ppermute x1, starting transfers between devices, on_device(): got = lax.ppermute(other, 'col', core_swap())  1.91 us
  transfers between devices with their start and end apart: 20, of which 12 were waited for; matrix products, arithmetic and copies ran while one was open for 0% of the time, Pallas kernels for 11%

profile of v8, /device:TPU:1, one launch (start us, length us, event | category | flops | bytes accessed | tf_op | source)
XLA Modules:
  0.0 67.7 jit_solution(5204330665673308527)
XLA Ops:
  0.7 2.1 %collective-permute-start = (bf16[256,128]{1,0:T(8,128)(2,1)}, bf16[256,128]{1,0:T(8,128)(2,1)S(1)}, u32[]{:S(2)}, u32[]{:S(2)}) collective-permute-start(bf16[256,128]{1,0:T(8,128)(2,1)} %x0.3), channel_id=1, source_target_pairs={{0,32},{32,64},{64,96},{96,0},{1,33},{33,65},{65,97},{97,1},{2,34}... | collective-permute-start | bytes 196616 | tf_op jit(solution)/shard_map/ppermute | solution.py:72
  2.8 1.3 %collective-permute-start.1 = (bf16[256,128]{1,0:T(8,128)(2,1)}, bf16[256,128]{1,0:T(8,128)(2,1)S(1)}, u32[]{:S(2)}, u32[]{:S(2)}) collective-permute-start(bf16[256,128]{1,0:T(8,128)(2,1)} %x0.3), channel_id=1, source_target_pairs={{0,96},{32,0},{64,32},{96,64},{1,97},{33,1},{65,33},{97,65},{2,98}... | collective-permute-start | bytes 196616 | tf_op jit(solution)/shard_map/ppermute | solution.py:72
  4.1 1.6 %collective-permute-start.2 = (bf16[256,128]{1,0:T(8,128)(2,1)}, bf16[256,128]{1,0:T(8,128)(2,1)S(1)}, u32[]{:S(2)}, u32[]{:S(2)}) collective-permute-start(bf16[256,128]{1,0:T(8,128)(2,1)} %x0.3), channel_id=1, source_target_pairs={{0,64},{32,96},{64,0},{96,32},{1,65},{33,97},{65,1},{97,33},{2,66}... | collective-permute-start | bytes 196616 | tf_op jit(solution)/shard_map/ppermute | solution.py:72
  6.4 2.2 %shard_map.112 = (bf16[128,128,128]{2,1,0:T(8,128)(2,1)S(1)}, f32[33,128,128]{2,1,0:T(8,128)S(1)}, f32[33,128,128]{2,1,0:T(8,128)S(1)}) custom-call(bf16[128,128,128]{2,1,0:T(8,128)(2,1)} %bitcast.5), custom_call_target="tpu_custom_call" | custom-call | tf_op jit(solution)/shard_map/pallas_call | solution.py:322
  9.5 1.3 %shard_map.114 = (f32[33,128,128]{2,1,0:T(8,128)S(1)}, bf16[4096,128]{1,0:T(8,128)(2,1)S(1)}) custom-call(s32[1,384]{1,0:T(1,128)S(1)} %get-tuple-element.53.tab, bf16[256,128]{1,0:T(8,128)(2,1)S(1)} %copy-done.2, bf16[256,128]{1,0:T(8,128)(2,1)S(1)} %collective-permute-done.1.x1, ...), custom_call_target="tpu_custom_call", output_to_operand_aliasing={{0}: (6, {})} | custom-call | flops 268435456 | bytes 4194304 | tf_op jit(solution)/shard_map/pallas_call | solution.py:331
  10.9 1.9 %collective-permute-start.3 = (bf16[4096,128]{1,0:T(8,128)(2,1)S(1)}, bf16[4096,128]{1,0:T(8,128)(2,1)S(1)}, u32[]{:S(2)}, u32[]{:S(2)}) collective-permute-start(bf16[4096,128]{1,0:T(8,128)(2,1)S(1)} %get-tuple-element.63), channel_id=1, source_target_pairs={{0,1},{1,0},{2,3},{3,2},{4,5},{5,4},{6,7},{7,6},{8,9},{9,8},{10,11... | collective-permute-start | bytes 3145736 | tf_op jit(solution)/shard_map/ppermute | solution.py:339
  12.8 1.2 %shard_map.113.acc = f32[33,128,128]{2,1,0:T(8,128)S(1)} custom-call(s32[1,384]{1,0:T(1,128)S(1)} %get-tuple-element.53.tab, bf16[256,128]{1,0:T(8,128)(2,1)S(1)} %copy-done.2, bf16[256,128]{1,0:T(8,128)(2,1)S(1)} %collective-permute-done.1.x1, bf16[256,128]{1,0:T(8,128)(2,1)S(1)} %collective-permute-done.2.x2, ...), custom_call_target="tpu_custom_call", output_to_operand_aliasing={{}: (6, {})} | custom-call | tf_op jit(solution)/shard_map/pallas_call | solution.py:340
  15.2 3.4 %collective-permute-start.4 = (bf16[1024,128]{1,0:T(8,128)(2,1)S(1)}, bf16[1024,128]{1,0:T(8,128)(2,1)S(1)}, u32[]{:S(2)}, u32[]{:S(2)}) collective-permute-start(bf16[1024,128]{1,0:T(8,128)(2,1)S(1)} %get-tuple-element.68), channel_id=1, source_target_pairs={{0,4},{1,17},{2,18},{3,7},{4,0},{5,21},{6,22},{7,3},{8,24},{9,13},... | collective-permute-start | bytes 786440 | tf_op jit(solution)/shard_map/ppermute | solution.py:72
  19.3 2.3 %collective-permute-start.6 = (bf16[1024,128]{1,0:T(8,128)(2,1)S(1)}, bf16[1024,128]{1,0:T(8,128)(2,1)S(1)}, u32[]{:S(2)}, u32[]{:S(2)}) collective-permute-start(bf16[1024,128]{1,0:T(8,128)(2,1)S(1)} %get-tuple-element.70), channel_id=1, source_target_pairs={{0,7},{1,24},{2,27},{3,0},{4,3},{5,28},{6,31},{7,4},{8,1},{9,14},{... | collective-permute-start | bytes 786440 | tf_op jit(solution)/shard_map/ppermute | solution.py:72
  21.6 1.1 %collective-permute-done.4.r2 = bf16[1024,128]{1,0:T(8,128)(2,1)S(1)} collective-permute-done((bf16[1024,128]{1,0:T(8,128)(2,1)S(1)}, bf16[1024,128]{1,0:T(8,128)(2,1)S(1)}, u32[]{:S(2)}, u32[]{:S(2)}) %collective-permute-start.4) | collective-permute-done | bytes 262176 | tf_op jit(solution)/shard_map/ppermute | solution.py:72
  22.7 3.2 %collective-permute-done.5.r1 = bf16[1024,128]{1,0:T(8,128)(2,1)S(1)} collective-permute-done((bf16[1024,128]{1,0:T(8,128)(2,1)S(1)}, bf16[1024,128]{1,0:T(8,128)(2,1)S(1)}, u32[]{:S(2)}, u32[]{:S(2)}) %collective-permute-start.5) | collective-permute-done | bytes 262176 | tf_op jit(solution)/shard_map/ppermute | solution.py:72
  26.5 2.3 %collective-permute-start.7 = (bf16[1536,128]{1,0:T(8,128)(2,1)S(1)}, bf16[1536,128]{1,0:T(8,128)(2,1)S(1)}, u32[]{:S(2)}, u32[]{:S(2)}) collective-permute-start(bf16[1536,128]{1,0:T(8,128)(2,1)S(1)} %get-tuple-element.78), channel_id=1, source_target_pairs={{0,9},{1,2},{2,5},{3,10},{4,13},{5,6},{6,1},{7,14},{8,11},{9,16},{... | collective-permute-start | bytes 1179656 | tf_op jit(solution)/shard_map/ppermute | solution.py:72
  28.8 1.9 %collective-permute-start.8 = (bf16[1536,128]{1,0:T(8,128)(2,1)S(1)}, bf16[1536,128]{1,0:T(8,128)(2,1)S(1)}, u32[]{:S(2)}, u32[]{:S(2)}) collective-permute-start(bf16[1536,128]{1,0:T(8,128)(2,1)S(1)} %get-tuple-element.78), channel_id=1, source_target_pairs={{0,25},{1,6},{2,1},{3,26},{4,29},{5,2},{6,5},{7,30},{8,15},{9,0},{... | collective-permute-start | bytes 1179656 | tf_op jit(solution)/shard_map/ppermute | solution.py:72
  30.7 1.6 %collective-permute-start.9 = (bf16[1536,128]{1,0:T(8,128)(2,1)S(1)}, bf16[1536,128]{1,0:T(8,128)(2,1)S(1)}, u32[]{:S(2)}, u32[]{:S(2)}) collective-permute-start(bf16[1536,128]{1,0:T(8,128)(2,1)S(1)} %get-tuple-element.78), channel_id=1, source_target_pairs={{0,16},{1,5},{2,6},{3,19},{4,20},{5,1},{6,2},{7,23},{8,12},{9,25},... | collective-permute-start | bytes 1179656 | tf_op jit(solution)/shard_map/ppermute | solution.py:72
  32.3 3.9 %collective-permute-done.7.r1 = bf16[1536,128]{1,0:T(8,128)(2,1)S(1)} collective-permute-done((bf16[1536,128]{1,0:T(8,128)(2,1)S(1)}, bf16[1536,128]{1,0:T(8,128)(2,1)S(1)}, u32[]{:S(2)}, u32[]{:S(2)}) %collective-permute-start.7) | collective-permute-done | bytes 393248 | tf_op jit(solution)/shard_map/ppermute | solution.py:72
  36.2 5.3 %collective-permute-done.9.r2 = bf16[1536,128]{1,0:T(8,128)(2,1)S(1)} collective-permute-done((bf16[1536,128]{1,0:T(8,128)(2,1)S(1)}, bf16[1536,128]{1,0:T(8,128)(2,1)S(1)}, u32[]{:S(2)}, u32[]{:S(2)}) %collective-permute-start.9) | collective-permute-done | bytes 393248 | tf_op jit(solution)/shard_map/ppermute | solution.py:72
  42.5 1.8 %collective-permute-start.12 = (bf16[1296,128]{1,0:T(8,128)(2,1)S(1)}, bf16[1296,128]{1,0:T(8,128)(2,1)S(1)}, u32[]{:S(2)}, u32[]{:S(2)}) collective-permute-start(bf16[1296,128]{1,0:T(8,128)(2,1)S(1)} %get-tuple-element.87.refs_0_), channel_id=1, source_target_pairs={{0,3},{1,8},{2,11},{3,4},{4,7},{5,12},{6,15},{7,0},{8,17},{9,10},{... | collective-permute-start | bytes 995336 | tf_op jit(solution)/shard_map/ppermute | solution.py:72
  44.3 1.8 %collective-permute-start.10 = (bf16[1296,128]{1,0:T(8,128)(2,1)S(1)}, bf16[1296,128]{1,0:T(8,128)(2,1)S(1)}, u32[]{:S(2)}, u32[]{:S(2)}) collective-permute-start(bf16[1296,128]{1,0:T(8,128)(2,1)S(1)} %get-tuple-element.87.refs_0_), channel_id=1, source_target_pairs={{0,7},{1,24},{2,27},{3,0},{4,3},{5,28},{6,31},{7,4},{8,1},{9,14},{... | collective-permute-start | bytes 995336 | tf_op jit(solution)/shard_map/ppermute | solution.py:72
  47.1 3.9 %collective-permute-done.12.refs_1_ = bf16[1296,128]{1,0:T(8,128)(2,1)S(1)} collective-permute-done((bf16[1296,128]{1,0:T(8,128)(2,1)S(1)}, bf16[1296,128]{1,0:T(8,128)(2,1)S(1)}, u32[]{:S(2)}, u32[]{:S(2)}) %collective-permute-start.12) | collective-permute-done | bytes 331808 | tf_op jit(solution)/shard_map/ppermute | solution.py:72
  52.4 3.0 %collective-permute-done.11.refs_1_ = bf16[1296,128]{1,0:T(8,128)(2,1)S(1)} collective-permute-done((bf16[1296,128]{1,0:T(8,128)(2,1)S(1)}, bf16[1296,128]{1,0:T(8,128)(2,1)S(1)}, u32[]{:S(2)}, u32[]{:S(2)}) %collective-permute-start.11) | collective-permute-done | bytes 331808 | tf_op jit(solution)/shard_map/ppermute | solution.py:72
  55.9 1.3 %shard_map.119 = (f32[9,128,128]{2,1,0:T(8,128)S(1)}, f32[272,128]{1,0:T(8,128)S(1)}) custom-call(s32[1,640]{1,0:T(1,128)S(1)} %get-tuple-element.83.tab, bf16[128,128,128]{2,1,0:T(8,128)(2,1)S(1)} %bitcast.7, bf16[1296,128]{1,0:T(8,128)(2,1)S(1)} %collective-permute-done.10.refs_0_, ...), custom_call_target="tpu_custom_call", output_to_operand_aliasing={{0}: (5, {})} | custom-call | flops 201326592 | bytes 3145728 | tf_op jit(solution)/shard_map/pallas_call | solution.py:367
  58.9 2.4 %collective-permute-start.18 = (bf16[528,128]{1,0:T(8,128)(2,1)S(1)}, bf16[528,128]{1,0:T(8,128)(2,1)S(1)}, u32[]{:S(2)}, u32[]{:S(2)}) collective-permute-start(bf16[528,128]{1,0:T(8,128)(2,1)S(1)} %get-tuple-element.97), channel_id=1, source_target_pairs={{0,96},{32,0},{64,32},{96,64},{1,97},{33,1},{65,33},{97,65},{2,98}... | collective-permute-start | bytes 405512 | tf_op jit(solution)/shard_map/ppermute | solution.py:384
  62.6 2.0 %collective-permute-done.17.r1 = bf16[528,128]{1,0:T(8,128)(2,1)S(1)} collective-permute-done((bf16[528,128]{1,0:T(8,128)(2,1)S(1)}, bf16[528,128]{1,0:T(8,128)(2,1)S(1)}, u32[]{:S(2)}, u32[]{:S(2)}) %collective-permute-start.17) | collective-permute-done | bytes 135200 | tf_op jit(solution)/shard_map/ppermute | solution.py:384
  64.9 2.1 %collective-permute-done.19.r3 = bf16[528,128]{1,0:T(8,128)(2,1)S(1)} collective-permute-done((bf16[528,128]{1,0:T(8,128)(2,1)S(1)}, bf16[528,128]{1,0:T(8,128)(2,1)S(1)}, u32[]{:S(2)}, u32[]{:S(2)}) %collective-permute-start.19) | collective-permute-done | bytes 135200 | tf_op jit(solution)/shard_map/ppermute | solution.py:384
  (42 shorter events, 11.3 us)
Async XLA Ops:
  0.7 8.8 %collective-permute-start = (bf16[256,128]{1,0:T(8,128)(2,1)}, bf16[256,128]{1,0:T(8,128)(2,1)S(1)}, u32[]{:S(2)}, u32[]{:S(2)}) collective-permute-start(bf16[256,128]{1,0:T(8,128)(2,1)} %x0.3), channel_id=1, source_target_pairs={{0,32},{32,64},{64,96},{96,0},{1,33},{33,65},{65,97},{97,1},{2,34}... | collective-permute-start | bytes 196616 | tf_op jit(solution)/shard_map/ppermute | solution.py:72
  2.8 6.7 %collective-permute-start.1 = (bf16[256,128]{1,0:T(8,128)(2,1)}, bf16[256,128]{1,0:T(8,128)(2,1)S(1)}, u32[]{:S(2)}, u32[]{:S(2)}) collective-permute-start(bf16[256,128]{1,0:T(8,128)(2,1)} %x0.3), channel_id=1, source_target_pairs={{0,96},{32,0},{64,32},{96,64},{1,97},{33,1},{65,33},{97,65},{2,98}... | collective-permute-start | bytes 196616 | tf_op jit(solution)/shard_map/ppermute | solution.py:72
  4.1 5.4 %collective-permute-start.2 = (bf16[256,128]{1,0:T(8,128)(2,1)}, bf16[256,128]{1,0:T(8,128)(2,1)S(1)}, u32[]{:S(2)}, u32[]{:S(2)}) collective-permute-start(bf16[256,128]{1,0:T(8,128)(2,1)} %x0.3), channel_id=1, source_target_pairs={{0,64},{32,96},{64,0},{96,32},{1,65},{33,97},{65,1},{97,33},{2,66}... | collective-permute-start | bytes 196616 | tf_op jit(solution)/shard_map/ppermute | solution.py:72
  10.9 4.2 %collective-permute-start.3 = (bf16[4096,128]{1,0:T(8,128)(2,1)S(1)}, bf16[4096,128]{1,0:T(8,128)(2,1)S(1)}, u32[]{:S(2)}, u32[]{:S(2)}) collective-permute-start(bf16[4096,128]{1,0:T(8,128)(2,1)S(1)} %get-tuple-element.63), channel_id=1, source_target_pairs={{0,1},{1,0},{2,3},{3,2},{4,5},{5,4},{6,7},{7,6},{8,9},{9,8},{10,11... | collective-permute-start | bytes 3145736 | tf_op jit(solution)/shard_map/ppermute | solution.py:339
  14.0 12.4 %copy-start.1 = (bf16[256,256]{1,0:T(8,128)(2,1)S(1)}, bf16[256,256]{1,0:T(8,128)(2,1)}, u32[]{:S(2)}) copy-start(bf16[256,256]{1,0:T(8,128)(2,1)} %cot.3) | copy-start | bytes 393220
  14.0 27.5 %copy-start.3 = (bf16[128,256]{1,0:T(8,128)(2,1)S(1)}, bf16[128,256]{1,0:T(8,128)(2,1)}, u32[]{:S(2)}) copy-start(bf16[128,256]{1,0:T(8,128)(2,1)} %weight.1) | copy-start | bytes 196612
  14.0 27.5 %copy-start.4 = (f32[256]{0:T(256)S(1)}, f32[256]{0:T(256)}, u32[]{:S(2)}) copy-start(f32[256]{0:T(256)} %param.10) | copy-start | bytes 3076
  15.1 36.3 %copy-start = (bf16[1,1,128,128,128]{4,3,2,1,0:T(8,128)(2,1)S(1)}, bf16[1,1,128,128,128]{4,3,2,1,0:T(8,128)(2,1)}, u32[]{:S(2)}) copy-start(bf16[1,1,128,128,128]{4,3,2,1,0:T(8,128)(2,1)} %param.11) | copy-start | bytes 12582916
  15.2 7.4 %collective-permute-start.4 = (bf16[1024,128]{1,0:T(8,128)(2,1)S(1)}, bf16[1024,128]{1,0:T(8,128)(2,1)S(1)}, u32[]{:S(2)}, u32[]{:S(2)}) collective-permute-start(bf16[1024,128]{1,0:T(8,128)(2,1)S(1)} %get-tuple-element.68), channel_id=1, source_target_pairs={{0,4},{1,17},{2,18},{3,7},{4,0},{5,21},{6,22},{7,3},{8,24},{9,13},... | collective-permute-start | bytes 786440 | tf_op jit(solution)/shard_map/ppermute | solution.py:72
  18.6 7.3 %collective-permute-start.5 = (bf16[1024,128]{1,0:T(8,128)(2,1)S(1)}, bf16[1024,128]{1,0:T(8,128)(2,1)S(1)}, u32[]{:S(2)}, u32[]{:S(2)}) collective-permute-start(bf16[1024,128]{1,0:T(8,128)(2,1)S(1)} %get-tuple-element.69), channel_id=1, source_target_pairs={{0,3},{1,8},{2,11},{3,4},{4,7},{5,12},{6,15},{7,0},{8,17},{9,10},{... | collective-permute-start | bytes 786440 | tf_op jit(solution)/shard_map/ppermute | solution.py:72
  19.3 7.2 %collective-permute-start.6 = (bf16[1024,128]{1,0:T(8,128)(2,1)S(1)}, bf16[1024,128]{1,0:T(8,128)(2,1)S(1)}, u32[]{:S(2)}, u32[]{:S(2)}) collective-permute-start(bf16[1024,128]{1,0:T(8,128)(2,1)S(1)} %get-tuple-element.70), channel_id=1, source_target_pairs={{0,7},{1,24},{2,27},{3,0},{4,3},{5,28},{6,31},{7,4},{8,1},{9,14},{... | collective-permute-start | bytes 786440 | tf_op jit(solution)/shard_map/ppermute | solution.py:72
  26.5 9.6 %collective-permute-start.7 = (bf16[1536,128]{1,0:T(8,128)(2,1)S(1)}, bf16[1536,128]{1,0:T(8,128)(2,1)S(1)}, u32[]{:S(2)}, u32[]{:S(2)}) collective-permute-start(bf16[1536,128]{1,0:T(8,128)(2,1)S(1)} %get-tuple-element.78), channel_id=1, source_target_pairs={{0,9},{1,2},{2,5},{3,10},{4,13},{5,6},{6,1},{7,14},{8,11},{9,16},{... | collective-permute-start | bytes 1179656 | tf_op jit(solution)/shard_map/ppermute | solution.py:72
  28.8 7.4 %collective-permute-start.8 = (bf16[1536,128]{1,0:T(8,128)(2,1)S(1)}, bf16[1536,128]{1,0:T(8,128)(2,1)S(1)}, u32[]{:S(2)}, u32[]{:S(2)}) collective-permute-start(bf16[1536,128]{1,0:T(8,128)(2,1)S(1)} %get-tuple-element.78), channel_id=1, source_target_pairs={{0,25},{1,6},{2,1},{3,26},{4,29},{5,2},{6,5},{7,30},{8,15},{9,0},{... | collective-permute-start | bytes 1179656 | tf_op jit(solution)/shard_map/ppermute | solution.py:72
  30.7 10.8 %collective-permute-start.9 = (bf16[1536,128]{1,0:T(8,128)(2,1)S(1)}, bf16[1536,128]{1,0:T(8,128)(2,1)S(1)}, u32[]{:S(2)}, u32[]{:S(2)}) collective-permute-start(bf16[1536,128]{1,0:T(8,128)(2,1)S(1)} %get-tuple-element.78), channel_id=1, source_target_pairs={{0,16},{1,5},{2,6},{3,19},{4,20},{5,1},{6,2},{7,23},{8,12},{9,25},... | collective-permute-start | bytes 1179656 | tf_op jit(solution)/shard_map/ppermute | solution.py:72
  42.5 8.5 %collective-permute-start.12 = (bf16[1296,128]{1,0:T(8,128)(2,1)S(1)}, bf16[1296,128]{1,0:T(8,128)(2,1)S(1)}, u32[]{:S(2)}, u32[]{:S(2)}) collective-permute-start(bf16[1296,128]{1,0:T(8,128)(2,1)S(1)} %get-tuple-element.87.refs_0_), channel_id=1, source_target_pairs={{0,3},{1,8},{2,11},{3,4},{4,7},{5,12},{6,15},{7,0},{8,17},{9,10},{... | collective-permute-start | bytes 995336 | tf_op jit(solution)/shard_map/ppermute | solution.py:72
  44.3 7.1 %collective-permute-start.13 = (bf16[1296,128]{1,0:T(8,128)(2,1)S(1)}, bf16[1296,128]{1,0:T(8,128)(2,1)S(1)}, u32[]{:S(2)}, u32[]{:S(2)}) collective-permute-start(bf16[1296,128]{1,0:T(8,128)(2,1)S(1)} %get-tuple-element.87.refs_0_), channel_id=1, source_target_pairs={{0,1},{1,0},{2,3},{3,2},{4,5},{5,4},{6,7},{7,6},{8,9},{9,8},{10,11... | collective-permute-start | bytes 995336 | tf_op jit(solution)/shard_map/ppermute | solution.py:360
  44.3 8.1 %collective-permute-start.10 = (bf16[1296,128]{1,0:T(8,128)(2,1)S(1)}, bf16[1296,128]{1,0:T(8,128)(2,1)S(1)}, u32[]{:S(2)}, u32[]{:S(2)}) collective-permute-start(bf16[1296,128]{1,0:T(8,128)(2,1)S(1)} %get-tuple-element.87.refs_0_), channel_id=1, source_target_pairs={{0,7},{1,24},{2,27},{3,0},{4,3},{5,28},{6,31},{7,4},{8,1},{9,14},{... | collective-permute-start | bytes 995336 | tf_op jit(solution)/shard_map/ppermute | solution.py:72
  46.1 9.3 %collective-permute-start.11 = (bf16[1296,128]{1,0:T(8,128)(2,1)S(1)}, bf16[1296,128]{1,0:T(8,128)(2,1)S(1)}, u32[]{:S(2)}, u32[]{:S(2)}) collective-permute-start(bf16[1296,128]{1,0:T(8,128)(2,1)S(1)} %get-tuple-element.87.refs_0_), channel_id=1, source_target_pairs={{0,4},{1,17},{2,18},{3,7},{4,0},{5,21},{6,22},{7,3},{8,24},{9,13},... | collective-permute-start | bytes 995336 | tf_op jit(solution)/shard_map/ppermute | solution.py:72
  50.9 5.0 %collective-permute-start.16 = (bf16[1296,128]{1,0:T(8,128)(2,1)S(1)}, bf16[1296,128]{1,0:T(8,128)(2,1)S(1)}, u32[]{:S(2)}, u32[]{:S(2)}) collective-permute-start(bf16[1296,128]{1,0:T(8,128)(2,1)S(1)} %collective-permute-done.12.refs_1_), channel_id=1, source_target_pairs={{0,1},{1,0},{2,3},{3,2},{4,5},{5,4},{6,7},{7,6},{8,9},{9,8},{10,11... | collective-permute-start | bytes 995336 | tf_op jit(solution)/shard_map/ppermute | solution.py:360
  55.4 1.8 %collective-permute-start.14 = (bf16[1296,128]{1,0:T(8,128)(2,1)S(1)}, bf16[1296,128]{1,0:T(8,128)(2,1)S(1)}, u32[]{:S(2)}, u32[]{:S(2)}) collective-permute-start(bf16[1296,128]{1,0:T(8,128)(2,1)S(1)} %collective-permute-done.10.refs_0_), channel_id=1, source_target_pairs={{0,1},{1,0},{2,3},{3,2},{4,5},{5,4},{6,7},{7,6},{8,9},{9,8},{10,11... | collective-permute-start | bytes 995336 | tf_op jit(solution)/shard_map/ppermute | solution.py:379
  55.8 1.7 %collective-permute-start.15 = (bf16[1296,128]{1,0:T(8,128)(2,1)S(1)}, bf16[1296,128]{1,0:T(8,128)(2,1)S(1)}, u32[]{:S(2)}, u32[]{:S(2)}) collective-permute-start(bf16[1296,128]{1,0:T(8,128)(2,1)S(1)} %collective-permute-done.11.refs_1_), channel_id=1, source_target_pairs={{0,1},{1,0},{2,3},{3,2},{4,5},{5,4},{6,7},{7,6},{8,9},{9,8},{10,11... | collective-permute-start | bytes 995336 | tf_op jit(solution)/shard_map/ppermute | solution.py:379
  58.5 6.1 %collective-permute-start.17 = (bf16[528,128]{1,0:T(8,128)(2,1)S(1)}, bf16[528,128]{1,0:T(8,128)(2,1)S(1)}, u32[]{:S(2)}, u32[]{:S(2)}) collective-permute-start(bf16[528,128]{1,0:T(8,128)(2,1)S(1)} %get-tuple-element.96), channel_id=1, source_target_pairs={{0,32},{32,64},{64,96},{96,0},{1,33},{33,65},{65,97},{97,1},{2,34}... | collective-permute-start | bytes 405512 | tf_op jit(solution)/shard_map/ppermute | solution.py:384
  58.9 6.0 %collective-permute-start.18 = (bf16[528,128]{1,0:T(8,128)(2,1)S(1)}, bf16[528,128]{1,0:T(8,128)(2,1)S(1)}, u32[]{:S(2)}, u32[]{:S(2)}) collective-permute-start(bf16[528,128]{1,0:T(8,128)(2,1)S(1)} %get-tuple-element.97), channel_id=1, source_target_pairs={{0,96},{32,0},{64,32},{96,64},{1,97},{33,1},{65,33},{97,65},{2,98}... | collective-permute-start | bytes 405512 | tf_op jit(solution)/shard_map/ppermute | solution.py:384
  61.3 5.7 %collective-permute-start.19 = (bf16[528,128]{1,0:T(8,128)(2,1)S(1)}, bf16[528,128]{1,0:T(8,128)(2,1)S(1)}, u32[]{:S(2)}, u32[]{:S(2)}) collective-permute-start(bf16[528,128]{1,0:T(8,128)(2,1)S(1)} %get-tuple-element.98), channel_id=1, source_target_pairs={{0,64},{32,96},{64,0},{96,32},{1,65},{33,97},{65,1},{97,33},{2,66}... | collective-permute-start | bytes 405512 | tf_op jit(solution)/shard_map/ppermute | solution.py:384
  (3 other events, 24.9 us)
